TPU v7x, 256 devices: a whole 4x4x8 slice. The times are simulated.
256 devices in a mesh: mode: 64 (over x_hi, y, z), atom: 4 (over x_lo, core).
Axes of the slice: x: 4 (x_hi: 2, x_lo: 2; x = x_hi * 2 + x_lo), y: 4, z: 8, core: 2. Of those that a mesh axis runs over, the one named last changes fastest.
Arguments:
- vectors: bfloat16 [15360, 8192], P('atom', 'mode'), may hold values from -0.046875 to 0.046875
- couplings: float32 [4, 3, 3, 3, 5120], P(None, None, None, None, 'atom'), may hold values from -6 to 6, as said below
- neighbours: int32 [4, 5120], P(None, 'atom'), may hold values from 0 to 5119, as said below
- frequency: float32 [8192], replicated, may hold values from 1 to 2, as said below
Outputs:
- diffusivity: float32 [8192], P('mode')
Inputs may be any that keep to these rules, and one draw needn't show every extreme that they name: neighbours[k, i] differs from i by 2 to 64 positions in atom order, counted around the end, upward for k < 2 and downward otherwise; the lists are mutual: neighbours[k + 2, neighbours[k, i]] = i for k < 2; some atoms in every slab have a neighbour exactly 64 positions above and some exactly 64 below. Antisymmetric bonds: couplings[k + 2, a, q, p, j] = -couplings[k, a, p, q, neighbours[k + 2, j]] for k < 2. `frequency`: strictly ascending.
All inputs are finite; a program needn't handle non-finite values.
Results may differ from a plain program's by a relative error of at most 0.00075.
Values may be sent and summed in bfloat16 or wider, within the bound.
No kernel may reach another device: no remote copies, remote signals or barrier semaphores. Data moves between devices by JAX's collectives and lax.ppermute only.
A program may use at most 128 MiB of HBM per device.

v0:
```python
import math

import jax
import jax.numpy as jnp
from jax import lax
from jax.sharding import PartitionSpec as P

HALO = 64
PARTNERS = 4
WIDTH_MODES = 320


def extended(cells, sides, width):
    for axis, dim in sides:
        count = lax.axis_size(axis)
        head = lax.slice_in_dim(cells, 0, width, axis=dim)
        tail = lax.slice_in_dim(cells, cells.shape[dim] - width, cells.shape[dim], axis=dim)
        cells = jnp.concatenate(
            [
                lax.ppermute(tail, axis, [(i, (i + 1) % count) for i in range(count)]),
                cells,
                lax.ppermute(head, axis, [((i + 1) % count, i) for i in range(count)]),
            ],
            axis=dim,
        )
    return cells


def passed_along(block, axis, distance):
    devices = range(lax.axis_size(axis))
    route = [(i - distance, i) for i in devices if i - distance in devices]
    return lax.ppermute(block, axis, route)


def cut_along(x, dim, devices):
    before, after = (x.shape[:dim], x.shape[dim + 1 :])
    return jnp.moveaxis(x.reshape(*before, devices, -1, *after), dim, 0)


def summed_on_arrival(x, axis, dim):
    parts = cut_along(x, dim, lax.axis_size(axis))
    arrived = lax.all_to_all(parts, axis, split_axis=0, concat_axis=0, tiled=True)
    return arrived.astype(jnp.float32).sum(axis=0)


def in_order(parts, dim):
    lengths = list(parts.shape[1:])
    lengths[dim] *= parts.shape[0]
    return jnp.moveaxis(parts, 0, dim).reshape(lengths)


def sent_to_all(x, axis):
    copies = jnp.broadcast_to(x, (lax.axis_size(axis), *x.shape))
    return lax.all_to_all(copies, axis, split_axis=0, concat_axis=0, tiled=True)


def gathered_copies(x, axis, dim):
    return in_order(sent_to_all(x, axis), dim)


def velocity(padded, local_index, couplings):
    count = local_index.shape[1]
    block_width = padded.shape[2]
    coupled = jnp.transpose(couplings, (4, 0, 1, 2, 3))
    summed = jnp.zeros((count, 3, 3, block_width), jnp.float32)
    for slot in range(local_index.shape[0]):
        picked = jnp.take(padded, local_index[slot], axis=0).astype(jnp.float32)
        summed = summed + jnp.einsum("iapq,iqm->ipam", coupled[:, slot], picked)
    return summed.astype(jnp.bfloat16).reshape(count * 3, 3 * block_width)


def lorentz(offset, half_width):
    return half_width / math.pi / (offset * offset + half_width * half_width)


def weighted(cross_part, row_freq, col_freq, half_width):
    reshaped = cross_part.reshape(cross_part.shape[0], 3, -1)
    squares = jnp.sum(reshaped * reshaped, axis=1)
    return jnp.sum(squares * lorentz(row_freq[:, None] - col_freq[None, :], half_width), axis=1)


def local(vectors, couplings, neighbours, frequency):
    rows_dev, block_width = vectors.shape
    atoms_dev = rows_dev // 3
    atom_groups = lax.axis_size("atom")
    total_atoms = atoms_dev * atom_groups
    first_atom = lax.axis_index("atom") * atoms_dev
    local_index = jnp.mod(neighbours - first_atom + HALO, total_atoms)
    padded = extended(vectors.reshape(atoms_dev, 3, block_width), (("atom", 0),), HALO)
    own_app = velocity(padded, local_index, couplings)
    modes_all = block_width * lax.axis_size("mode")
    half_width = WIDTH_MODES / modes_all
    block_index = lax.axis_index("mode")
    own_freq = lax.dynamic_slice_in_dim(frequency, block_index * block_width, block_width)
    products = [jnp.dot(vectors.T, own_app, preferred_element_type=jnp.float32)]
    crosses = []
    partner_freqs = []
    carried = vectors
    for distance in range(1, PARTNERS + 1):
        source, stride = (vectors, distance)
        carried = passed_along(source, "mode", -stride)
        joint = jnp.dot(own_app.T, carried, preferred_element_type=jnp.float32)
        cube = joint.reshape(3, block_width, block_width)
        products.append(-jnp.transpose(cube, (1, 0, 2)).reshape(block_width, 3 * block_width))
        crosses.append(jnp.transpose(cube, (2, 0, 1)).reshape(block_width, 3 * block_width))
        partner_freqs.append(
            lax.dynamic_slice_in_dim(frequency, (block_index + distance) * block_width, block_width)
        )
    stacked = jnp.stack(products + crosses)
    summed = summed_on_arrival(stacked.astype(jnp.bfloat16), "atom", 1)
    share_rows = block_width // atom_groups
    row_first = lax.axis_index("atom") * share_rows
    row_freq = lax.dynamic_slice_in_dim(own_freq, row_first, share_rows)
    own_total = weighted(summed[0], row_freq, own_freq, half_width)
    partner_terms = []
    for distance in range(1, PARTNERS + 1):
        own_total = own_total + weighted(
            summed[distance], row_freq, partner_freqs[distance - 1], half_width
        )
        partner_rows = lax.dynamic_slice_in_dim(partner_freqs[distance - 1], row_first, share_rows)
        partner_terms.append(
            weighted(summed[PARTNERS + distance], partner_rows, own_freq, half_width)
        )
    for distance in range(1, PARTNERS + 1):
        own_total = own_total + passed_along(partner_terms[distance - 1], "mode", distance)
    result = math.pi / (3.0 * row_freq * row_freq) * own_total
    result = gathered_copies(result, "atom", 0)
    return result


def solution(mesh):
    return jax.shard_map(
        local,
        mesh=mesh,
        in_specs=(P("atom", "mode"), P(None, None, None, None, "atom"), P(None, "atom"), P()),
        out_specs=P("mode"),
        check_vma=False,
    )
```

profile of v0, /device:TPU:1, one launch (start us, length us, event | category | flops | bytes accessed | tf_op | source)
XLA Modules:
  0.0 237.1 jit_solution(16504179947864603709)
XLA Ops:
  0.0 1.4 collective-permute-start.2
  1.4 1.3 collective-permute-start.3
  2.7 1.3 collective-permute-start.4
  4.0 1.3 collective-permute-start.5
  5.3 0.8 fusion.43
  6.2 2.7 %collective-permute-start = (bf16[64,3,128]{2,1,0:T(4,128)(2,1)S(1)}, bf16[64,3,128]{2,1,0:T(4,128)(2,1)S(1)}, u32[]{:S(2)}, u32[]{:S(2)}) collective-permute-start(bf16[64,3,128]{2,1,0:T(4,128)(2,1)S(1)} %slice.64), channel_id=1, source_target_pairs={{0,1},{1,2},{2,3},{3,0},{4,5},{5,6},{6,7},{7,4},{8,9},{9,10},{10,1... | collective-permute-start | bytes 147464 | tf_op jit(solution)/shard_map/ppermute | solution.py:20
  8.9 0.8 add_select_fusion
  9.6 0.1 slice_reduce_fusion
  9.8 2.7 %reshape.124 = bf16[1280,3,128]{2,1,0:T(4,128)(2,1)S(1)} reshape(bf16[3840,128]{1,0:T(8,128)(2,1)} %param.6) | data formatting | bytes 1966080 | tf_op jit(solution)/shard_map/reshape | solution.py:89
  12.6 19.5 %copy.47 = bf16[4,3,3,3,1280]{3,2,1,4,0:T(4,128)(2,1)} copy(f32[4,3,3,3,1280]{4,0,3,2,1:T(4,128)S(1)} %copy-done.6) | data formatting | bytes 829440 | tf_op args[1]
  32.1 0.7 collective-permute-start.1
  32.8 0.6 constant_dynamic-update-slice_fusion.1
  33.4 2.8 %collective-permute-done.1 = bf16[64,3,128]{2,1,0:T(4,128)(2,1)S(1)} collective-permute-done((bf16[64,3,128]{2,1,0:T(4,128)(2,1)S(1)}, bf16[64,3,128]{2,1,0:T(4,128)(2,1)S(1)}, u32[]{:S(2)}, u32[]{:S(2)}) %collective-permute-start.1) | collective-permute-done | bytes 49184 | tf_op jit(solution)/shard_map/ppermute | solution.py:22
  36.3 4.6 %gather_fusion.1 = bf16[1280,3,128]{2,1,0:T(4,128)(2,1)} fusion(bf16[1408,3,128]{2,1,0:T(4,128)(2,1)S(1)} %constant_dynamic-update-slice_fusion, s32[2048]{0:T(1024)S(1)} %pad_clamp_fusion.2), kind=kCustom, calls=%fused_computation.1.clone | custom fusion | bytes 1971200 | tf_op jit(solution)/shard_map/jit(_take)/gather | solution.py:67
  40.9 4.6 %gather_fusion = bf16[1280,3,128]{2,1,0:T(4,128)(2,1)} fusion(bf16[1408,3,128]{2,1,0:T(4,128)(2,1)S(1)} %constant_dynamic-update-slice_fusion, s32[2048]{0:T(1024)S(1)} %pad_clamp_fusion.3), kind=kCustom, calls=%fused_computation.clone | custom fusion | bytes 1971200 | tf_op jit(solution)/shard_map/jit(_take)/gather | solution.py:67
  45.5 5.4 %gather_fusion.2 = bf16[1280,3,128]{2,1,0:T(4,128)(2,1)} fusion(bf16[1408,3,128]{2,1,0:T(4,128)(2,1)} %copy-done, s32[2048]{0:T(1024)S(1)} %pad_clamp_fusion.1), kind=kCustom, calls=%fused_computation.2.clone | custom fusion | bytes 1971200 | tf_op jit(solution)/shard_map/jit(_take)/gather | solution.py:67
  50.9 5.3 %gather_fusion.3 = bf16[1280,3,128]{2,1,0:T(4,128)(2,1)} fusion(bf16[1408,3,128]{2,1,0:T(4,128)(2,1)} %copy-done, s32[2048]{0:T(1024)S(1)} %pad_clamp_fusion), kind=kCustom, calls=%fused_computation.3.clone | custom fusion | bytes 1971200 | tf_op jit(solution)/shard_map/jit(_take)/gather | solution.py:67
  56.2 8.6 %fusion.2 = f32[1280,128,3,3]{1,3,2,0:T(4,128)} fusion(bf16[1280,4,3,3,3]{4,3,2,0,1:T(4,128)(2,1)} %bitcast.97, bf16[1280,3,128]{2,1,0:T(4,128)(2,1)} %gather_fusion.1, pred[1280]{0:T(1024)(128)(4,1)S(1)} %get-tuple-element.54), kind=kOutput, calls=%fused_computation.9 | convolution fusion | flops 9338880 | bytes 11142400 | tf_op jit(solution)/shard_map/iapq,iqm->ipam/dot_general | solution.py:68
  64.9 7.1 %fusion.3 = f32[1280,128,3,3]{1,3,2,0:T(4,128)} fusion(bf16[1280,4,3,3,3]{4,3,2,0,1:T(4,128)(2,1)S(1)} %bitcast.101, bf16[1280,3,128]{2,1,0:T(4,128)(2,1)S(1)} %copy-done.3, pred[1280]{0:T(1024)(128)(4,1)S(1)} %get-tuple-element.55), kind=kOutput, calls=%fused_computation.11 | convolution fusion | flops 9338880 | bytes 11143168 | tf_op jit(solution)/shard_map/iapq,iqm->ipam/dot_general | solution.py:68
  71.9 7.0 %fusion.1 = f32[1280,128,3,3]{1,3,2,0:T(4,128)} fusion(bf16[1280,4,3,3,3]{4,3,2,0,1:T(4,128)(2,1)S(1)} %bitcast.102, bf16[1280,3,128]{2,1,0:T(4,128)(2,1)S(1)} %copy-done.2, pred[1280]{0:T(1024)(128)(4,1)S(1)} %get-tuple-element.53), kind=kOutput, calls=%fused_computation.7 | convolution fusion | flops 9338880 | bytes 11143168 | tf_op jit(solution)/shard_map/iapq,iqm->ipam/dot_general | solution.py:68
  78.9 13.8 %fusion.4 = bf16[1280,3,3,128]{3,1,2,0:T(4,128)(2,1)} fusion(bf16[1280,4,3,3,3]{4,3,2,0,1:T(4,128)(2,1)} %bitcast.98, f32[1280,128,3,3]{1,3,2,0:T(4,128)} %fusion.1, f32[1280,128,3,3]{1,3,2,0:T(4,128)} %fusion.3, f32[1280,128,3,3]{1,3,2,0:T(4,128)} %fusion.2, bf16[1280,3,128]{2,1,0:T(4,128)(2,1)} %gather_fusion.3, pred[1280]{0:T(1024)(128)(4,1)S(1)} %get-tuple-element.52), kind=kOutput, calls=%fused_computation.13 | convolution fusion | flops 15237120 | bytes 31786240 | tf_op jit(solution)/shard_map/iapq,iqm->ipam/dot_general | solution.py:68
  92.7 5.6 %copy.48 = bf16[1280,3,3,128]{3,2,1,0:T(4,128)(2,1)S(1)} copy(bf16[1280,3,3,128]{3,1,2,0:T(4,128)(2,1)} %fusion.4) | data formatting | bytes 5898240 | tf_op jit(solution)/shard_map/convert_element_type | solution.py:69
  98.3 0.5 copy.71
  98.8 1.4 copy-done.1
  100.1 3.3 %copy.49 = bf16[384,3840]{1,0:T(8,128)(2,1)} copy(bf16[384,3840]{0,1:T(8,128)(2,1)S(1)} %bitcast.105) | data formatting | bytes 5898240 | tf_op jit(solution)/shard_map/dot_general | solution.py:102
  103.4 3.3 %fusion.20 = bf16[384,128]{0,1:T(8,128)(2,1)S(1)} fusion(bf16[3840,128]{1,0:T(8,128)(2,1)} %param.6, bf16[480,8,3,128]{3,2,1,0:T(4,128)(2,1)} %bitcast.104), kind=kOutput, calls=%fused_computation.31 | convolution fusion | flops 377536512 | bytes 4030464 | tf_op jit(solution)/shard_map/dot_general | solution.py:95
  106.7 0.6 constant_dynamic-update-slice_fusion.11
  107.4 2.1 convert_bitcast_fusion.3
  109.5 0.1 copy.50
  109.6 0.1 neg.70
  109.7 0.0 collective-permute-done.3
  109.7 2.8 %convert_bitcast_fusion.2 = (bf16[128,3,128]{0,2,1:T(8,128)(2,1)}, bf16[128,3,128]{2,0,1:T(8,128)(2,1)S(1)}) fusion(bf16[3,128,3840]{2,1,0:T(8,128)(2,1)S(1)} %bitcast.107, bf16[3840,128]{1,0:T(8,128)(2,1)} %collective-permute-done.3), kind=kOutput, calls=%fused_computation.54 | convolution fusion | flops 377634816 | bytes 4128768 | tf_op jit(solution)/shard_map/dot_general | solution.py:102
  112.5 0.1 copy.51
  112.5 0.1 neg.73
  112.6 2.8 %convert_bitcast_fusion.1 = (bf16[128,3,128]{0,2,1:T(8,128)(2,1)}, bf16[128,3,128]{2,0,1:T(8,128)(2,1)S(1)}) fusion(bf16[3,128,3840]{2,1,0:T(8,128)(2,1)S(1)} %bitcast.108, bf16[3840,128]{1,0:T(8,128)(2,1)} %collective-permute-done.4), kind=kOutput, calls=%fused_computation.53 | convolution fusion | flops 377634816 | bytes 4128768 | tf_op jit(solution)/shard_map/dot_general | solution.py:102
  115.4 0.1 copy.52
  115.5 0.1 neg.76
  115.6 2.8 %convert_bitcast_fusion = (bf16[128,3,128]{0,2,1:T(8,128)(2,1)}, bf16[128,3,128]{2,0,1:T(8,128)(2,1)S(1)}) fusion(bf16[3,128,3840]{2,1,0:T(8,128)(2,1)S(1)} %bitcast.109, bf16[3840,128]{1,0:T(8,128)(2,1)} %collective-permute-done.5), kind=kOutput, calls=%fused_computation.52 | convolution fusion | flops 377634816 | bytes 4128768 | tf_op jit(solution)/shard_map/dot_general | solution.py:102
  118.4 0.1 copy.53
  118.5 0.1 neg.79
  118.6 0.1 copy.54
  118.7 0.1 stack.19
  118.8 0.1 copy.55
  119.0 0.1 stack.20
  119.1 1.0 copy.56
  120.1 0.1 stack.21
  120.2 0.1 copy.57
  120.4 0.1 stack.22
  120.7 1.0 copy.58
  121.7 3.7 %all-to-all-start = ((bf16[4,9,32,384]{3,2,1,0:T(8,128)(2,1)}), bf16[4,9,32,384]{3,2,1,0:T(8,128)(2,1)S(1)}, u32[]{:S(2)}, u32[]{:S(2)}) async-start(bf16[4,9,32,384]{3,2,1,0:T(8,128)(2,1)} %copy.58), calls=%async_computation | async-start | bytes 1769472 | tf_op jit(solution)/shard_map/all_to_all | solution.py:42
  125.4 0.9 fusion.45
  126.3 1.0 fusion.44
  127.3 10.7 %all-to-all-done = bf16[4,9,32,384]{3,2,1,0:T(8,128)(2,1)S(1)} async-done(((bf16[4,9,32,384]{3,2,1,0:T(8,128)(2,1)}), bf16[4,9,32,384]{3,2,1,0:T(8,128)(2,1)S(1)}, u32[]{:S(2)}, u32[]{:S(2)}) %all-to-all-start) | async-done | bytes 884768 | tf_op jit(solution)/shard_map/all_to_all | solution.py:42
  138.0 0.1 convert_reduce_fusion
  138.8 0.3 multiply_reduce_fusion.7
  139.2 67.0 %collective-permute-start.6 = (f32[32]{0:T(128)S(1)}, f32[32]{0:T(128)S(1)}, u32[]{:S(2)}, u32[]{:S(2)}) collective-permute-start(f32[32]{0:T(128)S(1)} %get-tuple-element.15), channel_id=1, source_target_pairs={{0,4},{4,8},{8,12},{12,16},{16,20},{20,24},{24,28},{28,32},{32,36}... | collective-permute-start | bytes 392 | tf_op jit(solution)/shard_map/ppermute | solution.py:32
  206.2 1.3 collective-permute-start.7
  207.5 17.8 %collective-permute-start.8 = (f32[32]{0:T(128)S(1)}, f32[32]{0:T(128)S(1)}, u32[]{:S(2)}, u32[]{:S(2)}) collective-permute-start(f32[32]{0:T(128)S(1)} %get-tuple-element.17), channel_id=1, source_target_pairs={{0,12},{4,16},{8,20},{12,24},{16,28},{20,32},{24,36},{28,40},{32,4... | collective-permute-start | bytes 392 | tf_op jit(solution)/shard_map/ppermute | solution.py:32
  225.3 1.9 collective-permute-start.9
  227.2 0.7 collective-permute-done.9
  227.9 7.4 %all_to_all.11 = f32[4,1,32]{2,1,0:T(1,128)S(1)} all-to-all(f32[4,1,32]{2,1,0:T(1,128)S(1)} %broadcast_in_dim.11), channel_id=1, replica_groups=mesh['mode'=64,'atom'=4] {'atom'}, dimensions={0} | all-to-all | bytes 1024 | tf_op jit(solution)/shard_map/all_to_all | solution.py:54
  235.3 0.5 broadcast.67
  235.8 0.7 reduce.11
  236.5 0.6 reshape.126
  (74 shorter events, 1.0 us)
Async XLA Ops:
  0.0 12.6 %copy-start.6 = (f32[4,3,3,3,1280]{4,0,3,2,1:T(4,128)S(1)}, f32[4,3,3,3,1280]{4,0,3,2,1:T(4,128)}, u32[]{:S(2)}) copy-start(f32[4,3,3,3,1280]{4,0,3,2,1:T(4,128)} %param.7) | copy-start | bytes 1658884
  0.0 107.4 %collective-permute-start.2 = (bf16[3840,128]{1,0:T(8,128)(2,1)}, bf16[3840,128]{1,0:T(8,128)(2,1)}, u32[]{:S(2)}, u32[]{:S(2)}) collective-permute-start(bf16[3840,128]{1,0:T(8,128)(2,1)} %param.6), channel_id=1, source_target_pairs={{4,0},{8,4},{12,8},{16,12},{20,16},{24,20},{28,24},{32,28},{36,32}... | collective-permute-start | bytes 2949128 | tf_op jit(solution)/shard_map/ppermute | solution.py:32
  1.4 108.3 %collective-permute-start.3 = (bf16[3840,128]{1,0:T(8,128)(2,1)}, bf16[3840,128]{1,0:T(8,128)(2,1)}, u32[]{:S(2)}, u32[]{:S(2)}) collective-permute-start(bf16[3840,128]{1,0:T(8,128)(2,1)} %param.6), channel_id=1, source_target_pairs={{8,0},{12,4},{16,8},{20,12},{24,16},{28,20},{32,24},{36,28},{40,32... | collective-permute-start | bytes 2949128 | tf_op jit(solution)/shard_map/ppermute | solution.py:32
  2.7 109.9 %collective-permute-start.4 = (bf16[3840,128]{1,0:T(8,128)(2,1)}, bf16[3840,128]{1,0:T(8,128)(2,1)}, u32[]{:S(2)}, u32[]{:S(2)}) collective-permute-start(bf16[3840,128]{1,0:T(8,128)(2,1)} %param.6), channel_id=1, source_target_pairs={{12,0},{16,4},{20,8},{24,12},{28,16},{32,20},{36,24},{40,28},{44,3... | collective-permute-start | bytes 2949128 | tf_op jit(solution)/shard_map/ppermute | solution.py:32
  4.0 111.6 %collective-permute-start.5 = (bf16[3840,128]{1,0:T(8,128)(2,1)}, bf16[3840,128]{1,0:T(8,128)(2,1)}, u32[]{:S(2)}, u32[]{:S(2)}) collective-permute-start(bf16[3840,128]{1,0:T(8,128)(2,1)} %param.6), channel_id=1, source_target_pairs={{16,0},{20,4},{24,8},{28,12},{32,16},{36,20},{40,24},{44,28},{48,3... | collective-permute-start | bytes 2949128 | tf_op jit(solution)/shard_map/ppermute | solution.py:32
  6.2 25.9 %collective-permute-start = (bf16[64,3,128]{2,1,0:T(4,128)(2,1)S(1)}, bf16[64,3,128]{2,1,0:T(4,128)(2,1)S(1)}, u32[]{:S(2)}, u32[]{:S(2)}) collective-permute-start(bf16[64,3,128]{2,1,0:T(4,128)(2,1)S(1)} %slice.64), channel_id=1, source_target_pairs={{0,1},{1,2},{2,3},{3,0},{4,5},{5,6},{6,7},{7,4},{8,9},{9,10},{10,1... | collective-permute-start | bytes 147464 | tf_op jit(solution)/shard_map/ppermute | solution.py:20
  32.1 4.1 %collective-permute-start.1 = (bf16[64,3,128]{2,1,0:T(4,128)(2,1)S(1)}, bf16[64,3,128]{2,1,0:T(4,128)(2,1)S(1)}, u32[]{:S(2)}, u32[]{:S(2)}) collective-permute-start(bf16[64,3,128]{2,1,0:T(4,128)(2,1)S(1)} %slice.66), channel_id=1, source_target_pairs={{1,0},{2,1},{3,2},{0,3},{5,4},{6,5},{7,6},{4,7},{9,8},{10,9},{11,1... | collective-permute-start | bytes 147464 | tf_op jit(solution)/shard_map/ppermute | solution.py:22
  36.2 4.6 %copy-start = (bf16[1408,3,128]{2,1,0:T(4,128)(2,1)}, bf16[1408,3,128]{2,1,0:T(4,128)(2,1)S(1)}, u32[]{:S(2)}) copy-start(bf16[1408,3,128]{2,1,0:T(4,128)(2,1)S(1)} %constant_dynamic-update-slice_fusion) | copy-start | bytes 3244036
  45.5 19.4 %slice-start = ((s8[15728640]{0:T(1024)(128)(4,1)}), s8[3145728]{0:T(1024)(128)(4,1)S(1)}, s32[]{:S(2)}) async-start(s8[15728640]{0:T(1024)(128)(4,1)} %bitcast.99), calls=%async_computation.2 | async-start | bytes 6291456
  56.2 8.6 %slice-start.1 = ((s8[15728640]{0:T(1024)(128)(4,1)}), s8[4194304]{0:T(1024)(128)(4,1)S(1)}, s32[]{:S(2)}) async-start(s8[15728640]{0:T(1024)(128)(4,1)} %bitcast.99), calls=%async_computation.3 | async-start | bytes 8388608
  56.2 8.6 %slice-start.2 = ((s8[15728640]{0:T(1024)(128)(4,1)}), s8[4194304]{0:T(1024)(128)(4,1)S(1)}, s32[]{:S(2)}) async-start(s8[15728640]{0:T(1024)(128)(4,1)} %bitcast.99), calls=%async_computation.4 | async-start | bytes 8388608
  56.2 8.6 %slice-start.3 = ((s8[15728640]{0:T(1024)(128)(4,1)}), s8[4194304]{0:T(1024)(128)(4,1)S(1)}, s32[]{:S(2)}) async-start(s8[15728640]{0:T(1024)(128)(4,1)} %bitcast.99), calls=%async_computation.5 | async-start | bytes 8388608
  56.2 8.7 %copy-start.3 = (bf16[1280,3,128]{2,1,0:T(4,128)(2,1)S(1)}, bf16[1280,3,128]{2,1,0:T(4,128)(2,1)}, u32[]{:S(2)}) copy-start(bf16[1280,3,128]{2,1,0:T(4,128)(2,1)} %gather_fusion) | copy-start | bytes 2949124
  64.8 7.1 %copy-start.2 = (bf16[1280,3,128]{2,1,0:T(4,128)(2,1)S(1)}, bf16[1280,3,128]{2,1,0:T(4,128)(2,1)}, u32[]{:S(2)}) copy-start(bf16[1280,3,128]{2,1,0:T(4,128)(2,1)} %gather_fusion.2) | copy-start | bytes 2949124
  98.3 1.9 copy-start.1
  103.4 3.9 %copy-start.4 = (bf16[384,3840]{1,0:T(8,128)(2,1)S(1)}, bf16[384,3840]{1,0:T(8,128)(2,1)}, u32[]{:S(2)}) copy-start(bf16[384,3840]{1,0:T(8,128)(2,1)} %copy.49) | copy-start | bytes 8847364
  115.6 3.2 %copy-start.7 = (bf16[128,3,128]{0,2,1:T(8,128)(2,1)S(1)}, bf16[128,3,128]{0,2,1:T(8,128)(2,1)}, u32[]{:S(2)}) copy-start(bf16[128,3,128]{0,2,1:T(8,128)(2,1)} %get-tuple-element.34) | copy-start | bytes 294916
  118.4 1.8 copy-start.8
  118.4 2.0 copy-start.5
  121.7 16.3 %all-to-all-start = ((bf16[4,9,32,384]{3,2,1,0:T(8,128)(2,1)}), bf16[4,9,32,384]{3,2,1,0:T(8,128)(2,1)S(1)}, u32[]{:S(2)}, u32[]{:S(2)}) async-start(bf16[4,9,32,384]{3,2,1,0:T(8,128)(2,1)} %copy.58), calls=%async_computation | async-start | bytes 1769472 | tf_op jit(solution)/shard_map/all_to_all | solution.py:42
  139.2 88.0 %collective-permute-start.6 = (f32[32]{0:T(128)S(1)}, f32[32]{0:T(128)S(1)}, u32[]{:S(2)}, u32[]{:S(2)}) collective-permute-start(f32[32]{0:T(128)S(1)} %get-tuple-element.15), channel_id=1, source_target_pairs={{0,4},{4,8},{8,12},{12,16},{16,20},{20,24},{24,28},{28,32},{32,36}... | collective-permute-start | bytes 392 | tf_op jit(solution)/shard_map/ppermute | solution.py:32
  206.2 21.0 %collective-permute-start.7 = (f32[32]{0:T(128)S(1)}, f32[32]{0:T(128)S(1)}, u32[]{:S(2)}, u32[]{:S(2)}) collective-permute-start(f32[32]{0:T(128)S(1)} %get-tuple-element.16), channel_id=1, source_target_pairs={{0,8},{4,12},{8,16},{12,20},{16,24},{20,28},{24,32},{28,36},{32,40... | collective-permute-start | bytes 392 | tf_op jit(solution)/shard_map/ppermute | solution.py:32
  207.5 19.7 %collective-permute-start.8 = (f32[32]{0:T(128)S(1)}, f32[32]{0:T(128)S(1)}, u32[]{:S(2)}, u32[]{:S(2)}) collective-permute-start(f32[32]{0:T(128)S(1)} %get-tuple-element.17), channel_id=1, source_target_pairs={{0,12},{4,16},{8,20},{12,24},{16,28},{20,32},{24,36},{28,40},{32,4... | collective-permute-start | bytes 392 | tf_op jit(solution)/shard_map/ppermute | solution.py:32
  225.3 2.6 %collective-permute-start.9 = (f32[32]{0:T(128)S(1)}, f32[32]{0:T(128)S(1)}, u32[]{:S(2)}, u32[]{:S(2)}) collective-permute-start(f32[32]{0:T(128)S(1)} %get-tuple-element.18), channel_id=1, source_target_pairs={{0,16},{4,20},{8,24},{12,28},{16,32},{20,36},{24,40},{28,44},{32,4... | collective-permute-start | bytes 392 | tf_op jit(solution)/shard_map/ppermute | solution.py:32
where the time goes:
time: 239 us; the launch traced here: 237 us
  starting transfers between devices  100 us (42%)
  local copies, waits for them, and re-layouts  62 us (26%)
  matrix products  50.2 us (21%)
  waiting for transfers between devices  14.2 us (6%)
  blocking collectives  7.4 us (3%)
    ppermute x8, starting transfers between devices, passed_along(): return lax.ppermute(block, axis, route)  93.3 us
    dot_general x4, matrix products, velocity(): summed = summed + jnp.einsum('iapq,iqm->ipam', coupled[:, slot], picked)  36.4 us
    unnamed x38, local copies, waits for them, and re-layouts  22.8 us
    gather x4, local copies, waits for them, and re-layouts, velocity(): picked = jnp.take(padded, local_index[slot], axis=0).astype(jnp.float32)  19.9 us
    all_to_all x1, waiting for transfers between devices, summed_on_arrival(): lax.all_to_all(parts, axis, split_axis=0, concat_axis=0, tiled=True)  10.7 us
    dot_general x4, matrix products, local(): joint = jnp.dot(own_app.T, carried, preferred_element_type=jnp.float32)  10.5 us
    all_to_all x1, blocking collectives, sent_to_all(): return lax.all_to_all(copies, axis, split_axis=0, concat_axis=0, tiled=True)  7.4 us
    convert_element_type x1, local copies, waits for them, and re-layouts, velocity(): return summed.astype(jnp.bfloat16).reshape(count * 3, 3 * block_width)  5.57 us
  transfers between devices with their start and end apart: 11, of which 3 were waited for; matrix products, arithmetic and copies ran while one was open for 44% of the time, Pallas kernels for 0%

commit v1 on v0

v1 whole, which is shorter than its diff:
```python
import functools
import math

import jax
import jax.numpy as jnp
from jax import lax
from jax.experimental import pallas as pl
from jax.experimental.pallas import tpu as pltpu
from jax.sharding import PartitionSpec as P

HALO = 64
PARTNERS = 4
WIDTH_MODES = 320
BLOCK = 128
WIN = BLOCK + 2 * HALO
ROWS = 3 * BLOCK
SPLIT = 7
SLOTS = 5
F32, BF16 = jnp.float32, jnp.bfloat16


def shifted(x, axis, distance):
    count = lax.axis_size(axis)
    return lax.ppermute(x, axis, [(i, (i + distance) % count) for i in range(count)])


def operator_kernel(packed_ref, out_ref, plane_ref):
    lane = lax.broadcasted_iota(jnp.int32, (BLOCK, ROWS), 1)
    atom = lax.broadcasted_iota(jnp.int32, (BLOCK, ROWS), 0)
    spread = jnp.zeros((40, ROWS), F32)
    for p in range(3):
        place = jnp.where(lane == 3 * atom + p, 1.0, 0.0).astype(BF16)
        spread += jnp.dot(packed_ref[p].astype(BF16), place, preferred_element_type=F32)
    target = [spread[36 + k : 37 + k] for k in range(4)]
    same = [target[0] == target[1], target[2] == target[3]]

    def mask(k, first, rows):
        row = lax.broadcasted_iota(jnp.int32, (rows, ROWS), 0).astype(F32) + float(first)
        return row == target[k]

    strips = [(0, HALO, (2, 3)), (HALO, HALO, (0, 1, 2, 3)), (2 * HALO, HALO, (0, 1, 2, 3)), (3 * HALO, HALO, (0, 1))]
    for first, rows, slots in strips:
        masks = {k: mask(k, first, rows) for k in slots}
        for a in range(3):
            for q in range(3):
                value = jnp.zeros((rows, ROWS), F32)
                for k in reversed(slots):
                    at = (k * 3 + a) * 3 + q
                    own = spread[at : at + 1]
                    if k % 2 == 0:
                        twin = spread[at + 9 : at + 10]
                        own = own + jnp.where(same[k // 2], twin, 0.0)
                    value = jnp.where(masks[k], own, value)
                for c in range(3):
                    plane_ref[a, c, pl.ds(3 * first + q, rows, stride=3), :] = value[:, c * 128 : (c + 1) * 128]
    for a in range(3):
        for c in range(3):
            out_ref[0, a, :, c * 128 : (c + 1) * 128] = plane_ref[a, c].astype(BF16)


def build_operator(packed):
    blocks = packed.shape[2] // BLOCK
    return pl.pallas_call(
        operator_kernel,
        grid=(blocks,),
        in_specs=[pl.BlockSpec((3, 40, BLOCK), lambda i: (0, 0, i))],
        out_specs=pl.BlockSpec((1, 3, 3 * WIN, ROWS), lambda i: (i, 0, 0, 0)),
        out_shape=jax.ShapeDtypeStruct((blocks, 3, 3 * WIN, ROWS), BF16),
        scratch_shapes=[pltpu.VMEM((3, 3, 3 * WIN, 128), F32)],
        compiler_params=pltpu.CompilerParams(vmem_limit_bytes=24 * 2**20),
        cost_estimate=pl.CostEstimate(flops=10**9, bytes_accessed=20 * 10**6, transcendentals=0),
    )(packed)


def star_step(window, operator_ref, partners, total_ref):
    window = window.T
    applied = [
        jnp.dot(window, operator_ref[0, a], preferred_element_type=F32).astype(BF16) for a in range(3)
    ]
    applied = jnp.concatenate(applied, axis=0)
    total_ref[...] += jnp.dot(applied, jnp.concatenate(partners, axis=1), preferred_element_type=F32)


def first_kernel(t_ref, far_ref, p0, p1, p2, p3, p4, out_ref):
    g = pl.program_id(0)

    @pl.when(g == 0)
    def _():
        out_ref[...] = jnp.zeros_like(out_ref)

    start = pl.multiple_of((g + 1) * ROWS - 3 * HALO, 3 * HALO)
    window = far_ref[pl.ds(start, 3 * WIN), :]
    star_step(window, t_ref, [r[...] for r in (p0, p1, p2, p3, p4)], out_ref)


def second_kernel(head, t_ref, before_ref, far_a, far_b, own, a0, a1, a2, a3, b0, b1, b2, b3, out_ref, padded, total):
    g = pl.program_id(0)
    steps = pl.num_programs(0)
    edge = 3 * HALO

    @pl.when(g == 0)
    def _():
        rows_a = far_a.shape[0]
        rows_b = far_b.shape[0] - 2 * edge
        padded[0:edge, :] = far_b[rows_b : rows_b + edge, :]
        padded[edge : edge + rows_a, :] = far_a[...]
        padded[edge + rows_a : edge + rows_a + rows_b, :] = far_b[0:rows_b, :]
        padded[edge + rows_a + rows_b :, :] = far_b[rows_b + edge :, :]
        total[...] = before_ref[...]

    block = lax.rem(g + head, head + steps - 1)
    start = pl.multiple_of(block * ROWS, ROWS)
    window = padded[pl.ds(start, 3 * WIN), :]
    in_first = jnp.logical_or(g == 0, g == steps - 1)

    @pl.when(in_first)
    def _():
        star_step(window, t_ref, [a0[...], a1[...], own[...], a2[...], a3[...]], total)

    @pl.when(jnp.logical_not(in_first))
    def _():
        star_step(window, t_ref, [b0[...], b1[...], own[...], b2[...], b3[...]], total)

    @pl.when(g == steps - 1)
    def _():
        for s in range(4):
            for a in range(3):
                out_ref[s, a * 32 : (a + 1) * 32, :] = total[a * 128 + s * 32 : a * 128 + (s + 1) * 32, :].astype(BF16)


def star_products(operator, own, firsts, seconds):
    blocks = operator.shape[0]
    width = own.shape[1]
    head = SPLIT - 1
    op_block = (1, 3, 3 * WIN, ROWS)
    shape = (3 * width, SLOTS * width)
    whole = lambda x: pl.BlockSpec(x.shape, lambda g: (0,) * x.ndim)
    ahead = pl.BlockSpec((ROWS, width), lambda g: (g + 1, 0))
    cost = lambda n: pl.CostEstimate(flops=n * 4 * 10**8, bytes_accessed=n * 3 * 10**6, transcendentals=0)
    before = pl.pallas_call(
        first_kernel,
        grid=(SPLIT - 2,),
        in_specs=[pl.BlockSpec(op_block, lambda g: (g + 1, 0, 0, 0)), whole(firsts[0])] + [ahead] * 5,
        out_specs=pl.BlockSpec(shape, lambda g: (0, 0)),
        out_shape=jax.ShapeDtypeStruct(shape, F32),
        compiler_params=pltpu.CompilerParams(vmem_limit_bytes=24 * 2**20),
        cost_estimate=cost(SPLIT - 2),
    )(operator, firsts[0], firsts[0], firsts[1], own, firsts[2], firsts[3])
    steps = blocks - (SPLIT - 2)
    at = lambda g: lax.rem(g + head, blocks)
    in_a = pl.BlockSpec((ROWS, width), lambda g: (jnp.where(g == steps - 1, 0, head), 0))
    in_b = pl.BlockSpec((ROWS, width), lambda g: (jnp.clip(g - 1, 0, steps - 3), 0))
    out_shape = (4, shape[0] // 4, shape[1])
    return pl.pallas_call(
        functools.partial(second_kernel, head),
        grid=(steps,),
        in_specs=[
            pl.BlockSpec(op_block, lambda g: (at(g), 0, 0, 0)),
            pl.BlockSpec(shape, lambda g: (0, 0)),
            whole(firsts[0]),
            whole(seconds[0]),
            pl.BlockSpec((ROWS, width), lambda g: (at(g), 0)),
        ]
        + [in_a] * 4
        + [in_b] * 4,
        out_specs=pl.BlockSpec(out_shape, lambda g: (0, 0, 0)),
        out_shape=jax.ShapeDtypeStruct(out_shape, BF16),
        scratch_shapes=[pltpu.VMEM((blocks * ROWS + 6 * HALO, width), BF16), pltpu.VMEM(shape, F32)],
        compiler_params=pltpu.CompilerParams(vmem_limit_bytes=32 * 2**20),
        cost_estimate=cost(steps),
    )(operator, before, firsts[0], seconds[0], own, *firsts, *seconds)


def weigh_kernel(half_width, share_ref, s0, s1, s2, s3, centre_ref, freq_ref, valid_ref, out_ref):
    summed = s0[...].astype(F32) + s1[...].astype(F32) + s2[...].astype(F32) + s3[...].astype(F32)
    squares = summed[0:32] * summed[0:32] + summed[32:64] * summed[32:64] + summed[64:96] * summed[64:96]
    row = lax.broadcasted_iota(jnp.int32, (32, 128), 0) + 32 * share_ref[0]
    lane = lax.broadcasted_iota(jnp.int32, (32, 128), 1)
    centre = jnp.zeros((32, 128), F32)
    out_ref[...] = jnp.zeros_like(out_ref)
    for slot in range(SLOTS):
        part = slice(slot * 128, (slot + 1) * 128)
        offset = centre_ref[...] - freq_ref[0:1, part]
        lorentz = (half_width / math.pi) / (offset * offset + half_width * half_width)
        term = squares[:, part] * lorentz * valid_ref[0:1, part]
        centre += term
        if slot > 0:
            out_ref[slot : slot + 1, :] = jnp.sum(term, axis=0, keepdims=True)
    own = jnp.sum(centre, axis=1, keepdims=True)
    out_ref[0:1, :] = jnp.sum(jnp.where(row == lane, own, 0.0), axis=0, keepdims=True)


def local(vectors, couplings, neighbours, frequency):
    rows_dev, width = vectors.shape
    atoms_dev = rows_dev // 3
    atom_groups = lax.axis_size("atom")
    total_atoms = atoms_dev * atom_groups
    atom_at = lax.axis_index("atom")
    mode_at = lax.axis_index("mode")
    modes = lax.axis_size("mode")
    half_width = WIDTH_MODES / (width * modes)
    edge = 3 * HALO
    cut = SPLIT * ROWS

    below = shifted(vectors[rows_dev - edge :], "atom", 1)
    above = shifted(vectors[:edge], "atom", -1)
    own_a = vectors[:cut]
    own_b = vectors[cut:]
    own_b_far = jnp.concatenate([own_b, below, above], axis=0)
    up1a = shifted(own_a, "mode", -1)
    dn1a = shifted(own_a, "mode", 1)
    up1b = shifted(own_b_far, "mode", -1)
    dn1b = shifted(own_b, "mode", 1)
    up2a = shifted(up1a, "mode", -1)
    dn2a = shifted(dn1a, "mode", 1)
    up2b = shifted(up1b, "mode", -1)
    dn2b = shifted(dn1b, "mode", 1)

    atom_ids = lax.broadcasted_iota(jnp.int32, neighbours.shape, 1)
    block_first = atom_at * atoms_dev + (atom_ids // BLOCK) * BLOCK
    target = jnp.mod(neighbours - block_first + HALO, total_atoms).astype(F32)
    packed = jnp.transpose(couplings, (2, 0, 1, 3, 4)).reshape(3, 36, atoms_dev)
    packed = jnp.concatenate([packed, jnp.broadcast_to(target, (3, 4, atoms_dev))], axis=1)
    operator = build_operator(packed)

    partial = star_products(operator, vectors, [up2a, up1a, dn1a, dn2a], [up2b, up1b, dn1b, dn2b])

    share = lambda k: lax.dynamic_index_in_dim(partial, lax.rem(atom_at + k, atom_groups), 0, keepdims=False)
    shares = [share(0)] + [shifted(share(k), "atom", k) for k in range(1, 4)]

    freq_rows = frequency.reshape(modes, width)
    blocks = [lax.rem(mode_at + d + modes, modes) for d in (2, 1, 0, -1, -2)]
    slot_freqs = [lax.dynamic_index_in_dim(freq_rows, b, 0, keepdims=False) for b in blocks]
    freq_lanes = jnp.broadcast_to(jnp.concatenate(slot_freqs)[None], (8, SLOTS * width))
    valid = jnp.stack([(b <= blocks[0]).astype(F32) for b in blocks])
    valid = jnp.broadcast_to(jnp.repeat(valid, width)[None], (8, SLOTS * width))
    centre = lax.dynamic_slice_in_dim(slot_freqs[0], atom_at * 32, 32)
    centre = jnp.broadcast_to(centre[:, None], (32, width))
    vmem = pl.BlockSpec(memory_space=pltpu.VMEM)
    terms = pl.pallas_call(
        functools.partial(weigh_kernel, half_width),
        in_specs=[pl.BlockSpec(memory_space=pltpu.SMEM)] + [vmem] * 7,
        out_specs=vmem,
        out_shape=jax.ShapeDtypeStruct((8, width), F32),
    )(jnp.reshape(atom_at, (1,)).astype(jnp.int32), *shares, centre, freq_lanes, valid)

    result = terms[2]
    result = result + shifted(terms[0], "mode", 2) + shifted(terms[1], "mode", 1)
    result = result + shifted(terms[3], "mode", -1) + shifted(terms[4], "mode", -2)
    far = [lax.ppermute(result, "atom", [(i, i ^ k) for i in range(4)]) for k in range(1, 4)]
    total = (result + far[0]) + (far[1] + far[2])
    own_freq = slot_freqs[2]
    return math.pi / (3.0 * own_freq * own_freq) * total


def solution(mesh):
    return jax.shard_map(
        local,
        mesh=mesh,
        in_specs=(P("atom", "mode"), P(None, None, None, None, "atom"), P(None, "atom"), P()),
        out_specs=P("mode"),
        check_vma=False,
    )
```

time: 239 us -> 131 us (0.55)
  starting transfers between devices: 100 us -> 48.3 us
  matrix products: 50.2 us -> 0 us
  local copies, waits for them, and re-layouts: 62 us -> 15.1 us
  Pallas kernels: 0 us -> 26 us
  waiting for transfers between devices: 14.2 us -> 36.2 us
  blocking collectives: 7.4 us -> 0 us
    dot_general x9 -> x0, matrix products: 50.2 us -> none  [the longest x4 36.4 us: velocity(): summed = summed + jnp.einsum('iapq,iqm->ipam', coupled[:, slot], picked)]
    ppermute x10 -> x20, starting transfers between devices: 96.6 us -> 48.3 us  [the longest x17 45.5 us: shifted(): lax.ppermute(x, axis, [(i, (i + distance) % count) for i in range(count)])]
    ppermute x10 -> x20, waiting for transfers between devices: 3.51 us -> 36.2 us  [the longest x17 35 us: shifted(): lax.ppermute(x, axis, [(i, (i + distance) % count) for i in range(count)])]
    pallas_call x0 -> x4, Pallas kernels: none -> 26 us  [the longest x1 11.3 us: build_operator(): pl.pallas_call(operator_kernel, grid=(blocks,), in_specs=[pl.BlockSpec((3...]
    gather x4 -> x0, local copies, waits for them, and re-layouts: 19.9 us -> none  [velocity(): picked = jnp.take(padded, local_index[slot], axis=0).astype(jnp.float32)]
    unnamed x38 -> x16, local copies, waits for them, and re-layouts: 22.8 us -> 3.9 us
    all_to_all x1 -> x0, waiting for transfers between devices: 10.7 us -> none  [summed_on_arrival(): lax.all_to_all(parts, axis, split_axis=0, concat_axis=0, tiled=True)]
    all_to_all x1 -> x0, blocking collectives: 7.4 us -> none  [sent_to_all(): return lax.all_to_all(copies, axis, split_axis=0, concat_axis=0, tiled=True)]
  transfers between devices with their start and end apart: 11 -> 20, of which waited for: 3 -> 9; matrix products, arithmetic and copies ran while one was open for 44% -> 9% of each run, Pallas kernels for 0% -> 13%
where the time goes in v1:
time: 131 us; the launch traced here: 130 us
  starting transfers between devices  48.3 us (37%)
  waiting for transfers between devices  36.2 us (28%)
  Pallas kernels  26 us (20%)
  local copies, waits for them, and re-layouts  15.1 us (12%)
  other arithmetic  4.58 us (3%)
    ppermute x17, starting transfers between devices, shifted(): lax.ppermute(x, axis, [(i, (i + distance) % count) for i in range(count)])  45.5 us
    ppermute x17, waiting for transfers between devices, shifted(): lax.ppermute(x, axis, [(i, (i + distance) % count) for i in range(count)])  35 us
    pallas_call x1, Pallas kernels, build_operator(): pl.pallas_call(operator_kernel, grid=(blocks,), in_specs=[pl.BlockSpec((3...  11.3 us
    pallas_call x1, Pallas kernels, star_products(): pl.pallas_call(functools.partial(second_kernel, head), grid=(steps,), in_...  7.34 us
    pallas_call x1, Pallas kernels, star_products(): pl.pallas_call(first_kernel, grid=(SPLIT - 2,), in_specs=[pl.BlockSpec(op...  5.54 us
    unnamed x16, local copies, waits for them, and re-layouts  3.9 us
    ppermute x3, starting transfers between devices, local(): lax.ppermute(result, 'atom', [(i, i ^ k) for i in range(4)])  2.79 us
  transfers between devices with their start and end apart: 20, of which 9 were waited for; matrix products, arithmetic and copies ran while one was open for 9% of the time, Pallas kernels for 13%

profile of v1, /device:TPU:1, one launch (start us, length us, event | category | flops | bytes accessed | tf_op | source)
XLA Modules:
  0.0 130.3 jit_solution(12683694029814599655)
XLA Ops:
  0.0 2.1 %slice.27 = bf16[2688,128]{1,0:T(8,128)(2,1)} slice(bf16[3840,128]{1,0:T(8,128)(2,1)} %own.1), slice={[0:2688], [0:128]} | slice | bytes 1376256 | tf_op jit(solution)/shard_map/slice | solution.py:207
  2.1 11.3 %collective-permute-start = (bf16[2688,128]{1,0:T(8,128)(2,1)}, bf16[2688,128]{1,0:T(8,128)(2,1)S(1)}, u32[]{:S(2)}, u32[]{:S(2)}) collective-permute-start(bf16[2688,128]{1,0:T(8,128)(2,1)} %slice.27), channel_id=1, source_target_pairs={{0,252},{4,0},{8,4},{12,8},{16,12},{20,16},{24,20},{28,24},{32,28}... | collective-permute-start | bytes 2064392 | tf_op jit(solution)/shard_map/ppermute | solution.py:24
  13.4 0.0 collective-permute-start.2
  13.4 0.8 fusion.12
  14.2 1.0 collective-permute-start.5
  15.2 0.8 collective-permute-start.4
  16.0 1.7 %slice.28 = bf16[1152,128]{1,0:T(8,128)(2,1)} slice(bf16[3840,128]{1,0:T(8,128)(2,1)} %own.1), slice={[2688:3840], [0:128]} | slice | bytes 589824 | tf_op jit(solution)/shard_map/slice | solution.py:208
  17.7 0.0 collective-permute-start.8
  17.8 1.2 copy.6
  19.0 0.3 reshape.16
  19.3 0.8 fusion
  20.1 0.9 pad_maximum_fusion.packed_ref
  21.0 0.7 constant_dynamic-update-slice_fusion.4
  21.7 0.1 stack.26
  21.8 6.0 %collective-permute-done.p1.a1 = bf16[2688,128]{1,0:T(8,128)(2,1)S(1)} collective-permute-done((bf16[2688,128]{1,0:T(8,128)(2,1)}, bf16[2688,128]{1,0:T(8,128)(2,1)S(1)}, u32[]{:S(2)}, u32[]{:S(2)}) %collective-permute-start) | collective-permute-done | bytes 688160 | tf_op jit(solution)/shard_map/ppermute | solution.py:24
  27.8 7.8 %collective-permute-start.1 = (bf16[2688,128]{1,0:T(8,128)(2,1)S(1)}, bf16[2688,128]{1,0:T(8,128)(2,1)S(1)}, u32[]{:S(2)}, u32[]{:S(2)}) collective-permute-start(bf16[2688,128]{1,0:T(8,128)(2,1)S(1)} %collective-permute-done.p1.a1), channel_id=1, source_target_pairs={{0,252},{4,0},{8,4},{12,8},{16,12},{20,16},{24,20},{28,24},{32,28}... | collective-permute-start | bytes 2064392 | tf_op jit(solution)/shard_map/ppermute | solution.py:24
  35.6 0.0 collective-permute-done.2.p3.a2
  35.6 0.0 collective-permute-start.3
  35.6 0.0 collective-permute-done.4
  35.7 1.0 pad_maximum_fusion.1
  36.6 7.3 %collective-permute-start.6 = (bf16[1536,128]{1,0:T(8,128)(2,1)S(1)}, bf16[1536,128]{1,0:T(8,128)(2,1)S(1)}, u32[]{:S(2)}, u32[]{:S(2)}) collective-permute-start(bf16[1536,128]{1,0:T(8,128)(2,1)S(1)} %pad_maximum_fusion.1), channel_id=1, source_target_pairs={{0,252},{4,0},{8,4},{12,8},{16,12},{20,16},{24,20},{28,24},{32,28}... | collective-permute-start | bytes 1179656 | tf_op jit(solution)/shard_map/ppermute | solution.py:24
  43.9 0.8 dynamic-slice_bitcast_fusion.4
  44.7 0.7 constant_dynamic-update-slice_fusion.3
  45.4 0.1 broadcast_bitcast_fusion
  45.4 11.8 %collective-permute-done.6.b1 = bf16[1536,128]{1,0:T(8,128)(2,1)S(1)} collective-permute-done((bf16[1536,128]{1,0:T(8,128)(2,1)S(1)}, bf16[1536,128]{1,0:T(8,128)(2,1)S(1)}, u32[]{:S(2)}, u32[]{:S(2)}) %collective-permute-start.6) | collective-permute-done | bytes 393248 | tf_op jit(solution)/shard_map/ppermute | solution.py:24
  57.2 7.9 %collective-permute-start.7 = (bf16[1536,128]{1,0:T(8,128)(2,1)S(1)}, bf16[1536,128]{1,0:T(8,128)(2,1)S(1)}, u32[]{:S(2)}, u32[]{:S(2)}) collective-permute-start(bf16[1536,128]{1,0:T(8,128)(2,1)S(1)} %collective-permute-done.6.b1), channel_id=1, source_target_pairs={{0,252},{4,0},{8,4},{12,8},{16,12},{20,16},{24,20},{28,24},{32,28}... | collective-permute-start | bytes 1179656 | tf_op jit(solution)/shard_map/ppermute | solution.py:24
  65.2 1.1 copy-done.2
  66.2 11.3 %shard_map.46.t_ref = bf16[10,3,768,384]{3,2,1,0:T(8,128)(2,1)S(1)} custom-call(f32[3,40,1280]{2,1,0:T(8,128)S(1)} %copy-done.2), custom_call_target="tpu_custom_call" | custom-call | flops 1000000000 | bytes 20000000 | tf_op jit(solution)/shard_map/pallas_call | solution.py:63
  77.5 0.0 collective-permute-done.8.b2
  77.5 0.3 collective-permute-start.9
  77.8 0.7 constant_dynamic-update-slice_fusion.2
  78.5 0.0 collective-permute-done.1.far_ref.p0.far_a.a0
  78.5 0.0 collective-permute-done.3.p4.a3
  78.5 5.5 %shard_map.47.before_ref = f32[384,640]{1,0:T(8,128)S(1)} custom-call(bf16[10,3,768,384]{3,2,1,0:T(8,128)(2,1)S(1)} %shard_map.46.t_ref, bf16[2688,128]{1,0:T(8,128)(2,1)S(1)} %collective-permute-done.1.far_ref.p0.far_a.a0, bf16[2688,128]{1,0:T(8,128)(2,1)S(1)} %collective-permute-done.1.far_ref.p0.far_a.a0, ...), custom_call_target="tpu_custom_call" | custom-call | flops 2000000000 | bytes 15000000 | tf_op jit(solution)/shard_map/pallas_call | solution.py:140
  84.1 5.2 %collective-permute-done.9.b3 = bf16[1152,128]{1,0:T(8,128)(2,1)S(1)} collective-permute-done((bf16[1152,128]{1,0:T(8,128)(2,1)}, bf16[1152,128]{1,0:T(8,128)(2,1)S(1)}, u32[]{:S(2)}, u32[]{:S(2)}) %collective-permute-start.9) | collective-permute-done | bytes 294944 | tf_op jit(solution)/shard_map/ppermute | solution.py:24
  89.3 0.0 collective-permute-done.7.far_b.b0
  89.3 7.3 %shard_map.48 = bf16[4,96,640]{2,1,0:T(8,128)(2,1)S(1)} custom-call(bf16[10,3,768,384]{3,2,1,0:T(8,128)(2,1)} %copy-done, f32[384,640]{1,0:T(8,128)S(1)} %shard_map.47.before_ref, bf16[2688,128]{1,0:T(8,128)(2,1)S(1)} %collective-permute-done.1.far_ref.p0.far_a.a0, bf16[1536,128]{1,0:T(8,128)(2,1)S(1)} %collective-permute-done.7.far_b.b0, ...), custom_call_target="tpu_custom_call" | custom-call | flops 2000000000 | bytes 15000000 | tf_op jit(solution)/shard_map/pallas_call | solution.py:154
  96.6 0.7 dynamic-slice_bitcast_fusion
  97.4 4.2 %collective-permute-start.10 = (bf16[96,640]{1,0:T(8,128)(2,1)S(1)}, bf16[96,640]{1,0:T(8,128)(2,1)S(1)}, u32[]{:S(2)}, u32[]{:S(2)}) collective-permute-start(bf16[96,640]{1,0:T(8,128)(2,1)S(1)} %get-tuple-element.9), channel_id=1, source_target_pairs={{0,1},{1,2},{2,3},{3,0},{4,5},{5,6},{6,7},{7,4},{8,9},{9,10},{10,1... | collective-permute-start | bytes 368648 | tf_op jit(solution)/shard_map/ppermute | solution.py:24
  101.5 1.1 collective-permute-start.11
  102.6 0.7 constant_dynamic-update-slice_fusion.1
  103.3 0.7 constant_dynamic-update-slice_fusion
  104.0 0.1 collective-permute-done.10.s1
  104.1 4.2 %collective-permute-done.11.s2 = bf16[96,640]{1,0:T(8,128)(2,1)S(1)} collective-permute-done((bf16[96,640]{1,0:T(8,128)(2,1)S(1)}, bf16[96,640]{1,0:T(8,128)(2,1)S(1)}, u32[]{:S(2)}, u32[]{:S(2)}) %collective-permute-start.11) | collective-permute-done | bytes 122912 | tf_op jit(solution)/shard_map/ppermute | solution.py:24
  108.3 0.6 collective-permute-done.12.s3
  108.8 0.7 broadcast_in_dim.29.centre_ref
  109.5 0.6 broadcast_in_dim.30.freq_ref
  110.1 0.6 broadcast_in_dim.33.valid_ref
  110.7 1.9 %shard_map.49 = f32[8,128]{1,0:T(8,128)} custom-call(s32[1]{0:T(128)} %bitcast.2.share_ref, bf16[96,640]{1,0:T(8,128)(2,1)} %get-tuple-element.10.s0, bf16[96,640]{1,0:T(8,128)(2,1)} %copy-done.3, bf16[96,640]{1,0:T(8,128)(2,1)} %copy-done.4, bf16[96,640]{1,0:T(8,128)(2,1)} %copy-done.5, f32[32,128]{1,0:T(8,128)} %broadcast_in_dim.29.centre_ref, ...), custom_call_target="tpu_custom_call" | custom-call | tf_op jit(solution)/shard_map/pallas_call | solution.py:240
  112.6 0.8 slice_bitcast_fusion.3
  113.4 0.8 collective-permute-start.15
  114.3 1.1 collective-permute-start.14
  115.4 1.9 %collective-permute-start.13 = (f32[128]{0:T(128)S(1)}, f32[128]{0:T(128)S(1)}, u32[]{:S(2)}, u32[]{:S(2)}) collective-permute-start(f32[128]{0:T(128)S(1)} %get-tuple-element.11), channel_id=1, source_target_pairs={{0,8},{4,12},{8,16},{12,20},{16,24},{20,28},{24,32},{28,36},{32,40... | collective-permute-start | bytes 1544 | tf_op jit(solution)/shard_map/ppermute | solution.py:24
  117.2 0.0 collective-permute-done.16
  117.3 0.0 collective-permute-done.15
  117.3 5.1 %collective-permute-done.14 = f32[128]{0:T(128)S(1)} collective-permute-done((f32[128]{0:T(128)S(1)}, f32[128]{0:T(128)S(1)}, u32[]{:S(2)}, u32[]{:S(2)}) %collective-permute-start.14) | collective-permute-done | bytes 544 | tf_op jit(solution)/shard_map/ppermute | solution.py:24
  122.4 2.0 %collective-permute-done.13 = f32[128]{0:T(128)S(1)} collective-permute-done((f32[128]{0:T(128)S(1)}, f32[128]{0:T(128)S(1)}, u32[]{:S(2)}, u32[]{:S(2)}) %collective-permute-start.13) | collective-permute-done | bytes 544 | tf_op jit(solution)/shard_map/ppermute | solution.py:24
  124.4 0.7 fusion.11
  125.1 0.4 collective-permute-start.18
  125.5 2.4 %collective-permute-start.19 = (f32[128]{0:T(128)S(1)}, f32[128]{0:T(128)S(1)}, u32[]{:S(2)}, u32[]{:S(2)}) collective-permute-start(f32[128]{0:T(128)S(1)} %fusion.11), channel_id=1, source_target_pairs={{0,3},{1,2},{2,1},{3,0},{4,7},{5,6},{6,5},{7,4},{8,11},{9,10},{10,... | collective-permute-start | bytes 1544 | tf_op jit(solution)/shard_map/ppermute | solution.py:250
  127.9 0.0 collective-permute-done.18
  127.9 1.2 collective-permute-done.19
  129.1 0.0 collective-permute-done.17
  129.1 1.2 divide_multiply_fusion
  (20 shorter events, 0.1 us)
Async XLA Ops:
  0.0 78.5 %copy-start.1 = (bf16[3840,128]{1,0:T(8,128)(2,1)S(1)}, bf16[3840,128]{1,0:T(8,128)(2,1)}, u32[]{:S(2)}) copy-start(bf16[3840,128]{1,0:T(8,128)(2,1)} %own.1) | copy-start | bytes 2949124
  2.1 25.7 %collective-permute-start = (bf16[2688,128]{1,0:T(8,128)(2,1)}, bf16[2688,128]{1,0:T(8,128)(2,1)S(1)}, u32[]{:S(2)}, u32[]{:S(2)}) collective-permute-start(bf16[2688,128]{1,0:T(8,128)(2,1)} %slice.27), channel_id=1, source_target_pairs={{0,252},{4,0},{8,4},{12,8},{16,12},{20,16},{24,20},{28,24},{32,28}... | collective-permute-start | bytes 2064392 | tf_op jit(solution)/shard_map/ppermute | solution.py:24
  13.4 22.2 %collective-permute-start.2 = (bf16[2688,128]{1,0:T(8,128)(2,1)}, bf16[2688,128]{1,0:T(8,128)(2,1)}, u32[]{:S(2)}, u32[]{:S(2)}) collective-permute-start(bf16[2688,128]{1,0:T(8,128)(2,1)} %slice.27), channel_id=1, source_target_pairs={{0,4},{4,8},{8,12},{12,16},{16,20},{20,24},{24,28},{28,32},{32,36}... | collective-permute-start | bytes 2064392 | tf_op jit(solution)/shard_map/ppermute | solution.py:24
  14.2 21.4 %collective-permute-start.5 = (bf16[192,128]{1,0:T(8,128)(2,1)S(1)}, bf16[192,128]{1,0:T(8,128)(2,1)S(1)}, u32[]{:S(2)}, u32[]{:S(2)}) collective-permute-start(bf16[192,128]{1,0:T(8,128)(2,1)S(1)} %get-tuple-element.6), channel_id=1, source_target_pairs={{0,3},{1,0},{2,1},{3,2},{4,7},{5,4},{6,5},{7,6},{8,11},{9,8},{10,9... | collective-permute-start | bytes 147464 | tf_op jit(solution)/shard_map/ppermute | solution.py:24
  15.2 20.4 %collective-permute-start.4 = (bf16[192,128]{1,0:T(8,128)(2,1)S(1)}, bf16[192,128]{1,0:T(8,128)(2,1)S(1)}, u32[]{:S(2)}, u32[]{:S(2)}) collective-permute-start(bf16[192,128]{1,0:T(8,128)(2,1)S(1)} %get-tuple-element.5), channel_id=1, source_target_pairs={{0,1},{1,2},{2,3},{3,0},{4,5},{5,6},{6,7},{7,4},{8,9},{9,10},{10,1... | collective-permute-start | bytes 147464 | tf_op jit(solution)/shard_map/ppermute | solution.py:24
  17.7 59.8 %collective-permute-start.8 = (bf16[1152,128]{1,0:T(8,128)(2,1)}, bf16[1152,128]{1,0:T(8,128)(2,1)}, u32[]{:S(2)}, u32[]{:S(2)}) collective-permute-start(bf16[1152,128]{1,0:T(8,128)(2,1)} %slice.28), channel_id=1, source_target_pairs={{0,4},{4,8},{8,12},{12,16},{16,20},{20,24},{24,28},{28,32},{32,36}... | collective-permute-start | bytes 884744 | tf_op jit(solution)/shard_map/ppermute | solution.py:24
  27.8 50.7 %collective-permute-start.1 = (bf16[2688,128]{1,0:T(8,128)(2,1)S(1)}, bf16[2688,128]{1,0:T(8,128)(2,1)S(1)}, u32[]{:S(2)}, u32[]{:S(2)}) collective-permute-start(bf16[2688,128]{1,0:T(8,128)(2,1)S(1)} %collective-permute-done.p1.a1), channel_id=1, source_target_pairs={{0,252},{4,0},{8,4},{12,8},{16,12},{20,16},{24,20},{28,24},{32,28}... | collective-permute-start | bytes 2064392 | tf_op jit(solution)/shard_map/ppermute | solution.py:24
  35.6 42.9 %collective-permute-start.3 = (bf16[2688,128]{1,0:T(8,128)(2,1)}, bf16[2688,128]{1,0:T(8,128)(2,1)S(1)}, u32[]{:S(2)}, u32[]{:S(2)}) collective-permute-start(bf16[2688,128]{1,0:T(8,128)(2,1)} %collective-permute-done.2.p3.a2), channel_id=1, source_target_pairs={{0,4},{4,8},{8,12},{12,16},{16,20},{20,24},{24,28},{28,32},{32,36}... | collective-permute-start | bytes 2064392 | tf_op jit(solution)/shard_map/ppermute | solution.py:24
  36.6 20.6 %collective-permute-start.6 = (bf16[1536,128]{1,0:T(8,128)(2,1)S(1)}, bf16[1536,128]{1,0:T(8,128)(2,1)S(1)}, u32[]{:S(2)}, u32[]{:S(2)}) collective-permute-start(bf16[1536,128]{1,0:T(8,128)(2,1)S(1)} %pad_maximum_fusion.1), channel_id=1, source_target_pairs={{0,252},{4,0},{8,4},{12,8},{16,12},{20,16},{24,20},{28,24},{32,28}... | collective-permute-start | bytes 1179656 | tf_op jit(solution)/shard_map/ppermute | solution.py:24
  57.2 32.0 %collective-permute-start.7 = (bf16[1536,128]{1,0:T(8,128)(2,1)S(1)}, bf16[1536,128]{1,0:T(8,128)(2,1)S(1)}, u32[]{:S(2)}, u32[]{:S(2)}) collective-permute-start(bf16[1536,128]{1,0:T(8,128)(2,1)S(1)} %collective-permute-done.6.b1), channel_id=1, source_target_pairs={{0,252},{4,0},{8,4},{12,8},{16,12},{20,16},{24,20},{28,24},{32,28}... | collective-permute-start | bytes 1179656 | tf_op jit(solution)/shard_map/ppermute | solution.py:24
  65.2 1.1 copy-start.2
  77.5 11.8 %copy-start = (bf16[10,3,768,384]{3,2,1,0:T(8,128)(2,1)}, bf16[10,3,768,384]{3,2,1,0:T(8,128)(2,1)S(1)}, u32[]{:S(2)}) copy-start(bf16[10,3,768,384]{3,2,1,0:T(8,128)(2,1)S(1)} %shard_map.46.t_ref) | copy-start | bytes 53084164
  77.5 11.8 %collective-permute-start.9 = (bf16[1152,128]{1,0:T(8,128)(2,1)}, bf16[1152,128]{1,0:T(8,128)(2,1)S(1)}, u32[]{:S(2)}, u32[]{:S(2)}) collective-permute-start(bf16[1152,128]{1,0:T(8,128)(2,1)} %collective-permute-done.8.b2), channel_id=1, source_target_pairs={{0,4},{4,8},{8,12},{12,16},{16,20},{20,24},{24,28},{28,32},{32,36}... | collective-permute-start | bytes 884744 | tf_op jit(solution)/shard_map/ppermute | solution.py:24
  97.4 6.8 %collective-permute-start.10 = (bf16[96,640]{1,0:T(8,128)(2,1)S(1)}, bf16[96,640]{1,0:T(8,128)(2,1)S(1)}, u32[]{:S(2)}, u32[]{:S(2)}) collective-permute-start(bf16[96,640]{1,0:T(8,128)(2,1)S(1)} %get-tuple-element.9), channel_id=1, source_target_pairs={{0,1},{1,2},{2,3},{3,0},{4,5},{5,6},{6,7},{7,4},{8,9},{9,10},{10,1... | collective-permute-start | bytes 368648 | tf_op jit(solution)/shard_map/ppermute | solution.py:24
  101.5 6.7 %collective-permute-start.11 = (bf16[96,640]{1,0:T(8,128)(2,1)S(1)}, bf16[96,640]{1,0:T(8,128)(2,1)S(1)}, u32[]{:S(2)}, u32[]{:S(2)}) collective-permute-start(bf16[96,640]{1,0:T(8,128)(2,1)S(1)} %get-tuple-element.8), channel_id=1, source_target_pairs={{0,2},{1,3},{2,0},{3,1},{4,6},{5,7},{6,4},{7,5},{8,10},{9,11},{10,... | collective-permute-start | bytes 368648 | tf_op jit(solution)/shard_map/ppermute | solution.py:24
  102.6 6.2 %collective-permute-start.12 = (bf16[96,640]{1,0:T(8,128)(2,1)S(1)}, bf16[96,640]{1,0:T(8,128)(2,1)S(1)}, u32[]{:S(2)}, u32[]{:S(2)}) collective-permute-start(bf16[96,640]{1,0:T(8,128)(2,1)S(1)} %get-tuple-element.7), channel_id=1, source_target_pairs={{0,3},{1,0},{2,1},{3,2},{4,7},{5,4},{6,5},{7,6},{8,11},{9,8},{10,9... | collective-permute-start | bytes 368648 | tf_op jit(solution)/shard_map/ppermute | solution.py:24
  104.1 6.6 %copy-start.3 = (bf16[96,640]{1,0:T(8,128)(2,1)}, bf16[96,640]{1,0:T(8,128)(2,1)S(1)}, u32[]{:S(2)}) copy-start(bf16[96,640]{1,0:T(8,128)(2,1)S(1)} %collective-permute-done.10.s1) | copy-start | bytes 368644
  108.3 2.4 %copy-start.4 = (bf16[96,640]{1,0:T(8,128)(2,1)}, bf16[96,640]{1,0:T(8,128)(2,1)S(1)}, u32[]{:S(2)}) copy-start(bf16[96,640]{1,0:T(8,128)(2,1)S(1)} %collective-permute-done.11.s2) | copy-start | bytes 368644
  108.8 1.9 %copy-start.5 = (bf16[96,640]{1,0:T(8,128)(2,1)}, bf16[96,640]{1,0:T(8,128)(2,1)S(1)}, u32[]{:S(2)}) copy-start(bf16[96,640]{1,0:T(8,128)(2,1)S(1)} %collective-permute-done.12.s3) | copy-start | bytes 368644
  113.4 3.8 %collective-permute-start.16 = (f32[128]{0:T(128)S(1)}, f32[128]{0:T(128)S(1)}, u32[]{:S(2)}, u32[]{:S(2)}) collective-permute-start(f32[128]{0:T(128)S(1)} %get-tuple-element.12), channel_id=1, source_target_pairs={{0,248},{4,252},{8,0},{12,4},{16,8},{20,12},{24,16},{28,20},{32,24... | collective-permute-start | bytes 1544 | tf_op jit(solution)/shard_map/ppermute | solution.py:24
  113.4 3.8 %collective-permute-start.15 = (f32[128]{0:T(128)S(1)}, f32[128]{0:T(128)S(1)}, u32[]{:S(2)}, u32[]{:S(2)}) collective-permute-start(f32[128]{0:T(128)S(1)} %get-tuple-element.13), channel_id=1, source_target_pairs={{0,252},{4,0},{8,4},{12,8},{16,12},{20,16},{24,20},{28,24},{32,28}... | collective-permute-start | bytes 1544 | tf_op jit(solution)/shard_map/ppermute | solution.py:24
  114.3 8.1 %collective-permute-start.14 = (f32[128]{0:T(128)S(1)}, f32[128]{0:T(128)S(1)}, u32[]{:S(2)}, u32[]{:S(2)}) collective-permute-start(f32[128]{0:T(128)S(1)} %get-tuple-element.14), channel_id=1, source_target_pairs={{0,4},{4,8},{8,12},{12,16},{16,20},{20,24},{24,28},{28,32},{32,36}... | collective-permute-start | bytes 1544 | tf_op jit(solution)/shard_map/ppermute | solution.py:24
  115.4 9.0 %collective-permute-start.13 = (f32[128]{0:T(128)S(1)}, f32[128]{0:T(128)S(1)}, u32[]{:S(2)}, u32[]{:S(2)}) collective-permute-start(f32[128]{0:T(128)S(1)} %get-tuple-element.11), channel_id=1, source_target_pairs={{0,8},{4,12},{8,16},{12,20},{16,24},{20,28},{24,32},{28,36},{32,40... | collective-permute-start | bytes 1544 | tf_op jit(solution)/shard_map/ppermute | solution.py:24
  125.1 2.8 %collective-permute-start.18 = (f32[128]{0:T(128)S(1)}, f32[128]{0:T(128)S(1)}, u32[]{:S(2)}, u32[]{:S(2)}) collective-permute-start(f32[128]{0:T(128)S(1)} %fusion.11), channel_id=1, source_target_pairs={{0,2},{1,3},{2,0},{3,1},{4,6},{5,7},{6,4},{7,5},{8,10},{9,11},{10,... | collective-permute-start | bytes 1544 | tf_op jit(solution)/shard_map/ppermute | solution.py:250
  125.5 3.7 %collective-permute-start.19 = (f32[128]{0:T(128)S(1)}, f32[128]{0:T(128)S(1)}, u32[]{:S(2)}, u32[]{:S(2)}) collective-permute-start(f32[128]{0:T(128)S(1)} %fusion.11), channel_id=1, source_target_pairs={{0,3},{1,2},{2,1},{3,0},{4,7},{5,6},{6,5},{7,4},{8,11},{9,10},{10,... | collective-permute-start | bytes 1544 | tf_op jit(solution)/shard_map/ppermute | solution.py:250
  127.9 1.2 collective-permute-start.17

commit v2 on v1

v2 whole, which is shorter than its diff:
```python
import functools
import math

import jax
import jax.numpy as jnp
from jax import lax
from jax.experimental import pallas as pl
from jax.experimental.pallas import tpu as pltpu
from jax.sharding import PartitionSpec as P

HALO = 64
PARTNERS = 4
WIDTH_MODES = 320
BLOCK = 128
WIN = BLOCK + 2 * HALO
ROWS = 3 * BLOCK
SPLIT = 5
SLOTS = 5
F32, BF16 = jnp.float32, jnp.bfloat16


def shifted(x, axis, distance):
    count = lax.axis_size(axis)
    return lax.ppermute(x, axis, [(i, (i + distance) % count) for i in range(count)])


def operator_kernel(total_atoms, place_ref, couplings_ref, neighbours_ref, out_ref, rows_ref):
    i = pl.program_id(0)
    first = (place_ref[0] * pl.num_programs(0) + i) * BLOCK - HALO
    target = neighbours_ref[...] - first
    target = jnp.where(target < 0, target + total_atoms, target)
    target = jnp.where(target >= total_atoms, target - total_atoms, target).astype(F32)
    lane = lax.broadcasted_iota(jnp.int32, (BLOCK, ROWS), 1)
    atom = lax.broadcasted_iota(jnp.int32, (BLOCK, ROWS), 0)
    spread = jnp.zeros((40, ROWS), F32)
    for p in range(3):
        for k in range(4):
            for a in range(3):
                at = (k * 3 + a) * 3
                rows_ref[at : at + 3, :] = couplings_ref[k, a, p]
        rows_ref[36:40, :] = target
        place = jnp.where(lane == 3 * atom + p, 1.0, 0.0).astype(BF16)
        spread += jnp.dot(rows_ref[...].astype(BF16), place, preferred_element_type=F32)
    reach = [spread[36 + k : 37 + k] for k in range(4)]
    same = [reach[0] == reach[1], reach[2] == reach[3]]
    own = {}
    for k in range(4):
        for at in range(k * 9, k * 9 + 9):
            own[at] = spread[at : at + 1]
            if k % 2 == 0:
                own[at] = own[at] + jnp.where(same[k // 2], spread[at + 9 : at + 10], 0.0)
    for first_row, slots in ((0, (2, 3)), (HALO, (0, 1, 2, 3)), (2 * HALO, (0, 1, 2, 3)), (3 * HALO, (0, 1))):
        row = lax.broadcasted_iota(jnp.int32, (HALO, ROWS), 0).astype(F32) + float(first_row)
        masks = {k: row == reach[k] for k in slots}
        for a in range(3):
            for q in range(3):
                value = jnp.zeros((HALO, ROWS), F32)
                for k in reversed(slots):
                    value = jnp.where(masks[k], own[(k * 3 + a) * 3 + q], value)
                start = q * WIN + first_row
                out_ref[0, a, start : start + HALO, :] = value.astype(BF16)


def build_operator(place, couplings, neighbours, total_atoms):
    blocks = neighbours.shape[1] // BLOCK
    return pl.pallas_call(
        functools.partial(operator_kernel, total_atoms),
        grid=(blocks,),
        in_specs=[
            pl.BlockSpec(memory_space=pltpu.SMEM),
            pl.BlockSpec((4, 3, 3, 3, BLOCK), lambda i: (0, 0, 0, 0, i)),
            pl.BlockSpec((4, BLOCK), lambda i: (0, i)),
        ],
        out_specs=pl.BlockSpec((1, 3, 3 * WIN, ROWS), lambda i: (i, 0, 0, 0)),
        out_shape=jax.ShapeDtypeStruct((blocks, 3, 3 * WIN, ROWS), BF16),
        scratch_shapes=[pltpu.VMEM((40, BLOCK), F32)],
        compiler_params=pltpu.CompilerParams(vmem_limit_bytes=24 * 2**20),
        cost_estimate=pl.CostEstimate(flops=4 * 10**9, bytes_accessed=20 * 10**6, transcendentals=0),
    )(place, couplings, neighbours)


def copy_kernel(moves, *refs):
    sems = refs[-1]
    copies = [
        pltpu.make_async_copy(refs[src].at[pl.ds(s0, n)], refs[dst].at[pl.ds(d0, n)], sems.at[c])
        for c, (src, s0, dst, d0, n) in enumerate(moves)
    ]
    for copy in copies:
        copy.start()
    for copy in copies:
        copy.wait()


def copied_rows(inputs, lengths, moves):
    width = inputs[0].shape[1]
    moves = [(i, s, len(inputs) + o, d, n) for i, s, o, d, n in moves]
    return pl.pallas_call(
        functools.partial(copy_kernel, moves),
        in_specs=[pl.BlockSpec(memory_space=pl.ANY)] * len(inputs),
        out_specs=[pl.BlockSpec(memory_space=pl.ANY)] * len(lengths),
        out_shape=[jax.ShapeDtypeStruct((n, width), inputs[0].dtype) for n in lengths],
        scratch_shapes=[pltpu.SemaphoreType.DMA((len(moves),))],
    )(*inputs)


def star_step(planes_ref, start, operator_ref, partners, total_ref):
    window = [planes_ref[pl.ds(start + q, WIN, stride=3), :].astype(BF16) for q in range(3)]
    window = jnp.concatenate(window, axis=0).T
    applied = [jnp.dot(window, operator_ref[0, a], preferred_element_type=F32).astype(BF16) for a in range(3)]
    applied = jnp.concatenate(applied, axis=0)
    total_ref[...] += jnp.dot(applied, jnp.concatenate(partners, axis=1), preferred_element_type=F32)


def first_kernel(t_ref, far_ref, p0, p1, p2, p3, p4, out_ref, planes):
    g = pl.program_id(0)

    @pl.when(g == 0)
    def _():
        out_ref[...] = jnp.zeros_like(out_ref)
        planes[...] = far_ref[...].astype(F32)

    start = (g + 1) * ROWS - 3 * HALO
    star_step(planes, start, t_ref, [r[...] for r in (p0, p1, p2, p3, p4)], out_ref)


def second_kernel(
    head, place_ref, t_ref, before_ref, far_a, far_b, own, a0, a1, a2, a3, b0, b1, b2, b3, o0, o1, o2, o3, planes, total
):
    g = pl.program_id(0)
    steps = pl.num_programs(0)
    edge = 3 * HALO

    @pl.when(g == 0)
    def _():
        rows_a = far_a.shape[0]
        rows_b = far_b.shape[0] - 2 * edge
        planes[0:edge, :] = far_b[rows_b : rows_b + edge, :].astype(F32)
        planes[edge : edge + rows_a, :] = far_a[...].astype(F32)
        planes[edge + rows_a : edge + rows_a + rows_b, :] = far_b[0:rows_b, :].astype(F32)
        planes[edge + rows_a + rows_b :, :] = far_b[rows_b + edge :, :].astype(F32)
        total[...] = before_ref[...]

    block = lax.rem(g + head, head + steps - 1)
    in_first = jnp.logical_or(g == 0, g == steps - 1)

    @pl.when(in_first)
    def _():
        star_step(planes, block * ROWS, t_ref, [a0[...], a1[...], own[...], a2[...], a3[...]], total)

    @pl.when(jnp.logical_not(in_first))
    def _():
        star_step(planes, block * ROWS, t_ref, [b0[...], b1[...], own[...], b2[...], b3[...]], total)

    @pl.when(g == steps - 1)
    def _():
        for k, out in enumerate((o0, o1, o2, o3)):
            share = jnp.bitwise_xor(place_ref[0], k)
            for a in range(3):
                rows = pl.ds(pl.multiple_of(a * 128 + share * 32, 32), 32)
                out[a * 32 : (a + 1) * 32, :] = total[rows, :].astype(BF16)


def star_products(place, operator, own, firsts, seconds):
    blocks = operator.shape[0]
    width = own.shape[1]
    head = SPLIT - 1
    op_block = (1, 3, 3 * WIN, ROWS)
    shape = (3 * width, SLOTS * width)
    whole = lambda x: pl.BlockSpec(x.shape, lambda g: (0,) * x.ndim)
    ahead = pl.BlockSpec((ROWS, width), lambda g: (g + 1, 0))
    cost = lambda n: pl.CostEstimate(flops=n * 10**9, bytes_accessed=n * 3 * 10**6, transcendentals=0)
    before = pl.pallas_call(
        first_kernel,
        grid=(SPLIT - 2,),
        in_specs=[pl.BlockSpec(op_block, lambda g: (g + 1, 0, 0, 0)), whole(firsts[0])] + [ahead] * 5,
        out_specs=pl.BlockSpec(shape, lambda g: (0, 0)),
        out_shape=jax.ShapeDtypeStruct(shape, F32),
        scratch_shapes=[pltpu.VMEM(firsts[0].shape, F32)],
        compiler_params=pltpu.CompilerParams(vmem_limit_bytes=24 * 2**20),
        cost_estimate=cost(SPLIT - 2),
    )(operator, firsts[0], firsts[0], firsts[1], own, firsts[2], firsts[3])
    steps = blocks - (SPLIT - 2)
    at = lambda g: lax.rem(g + head, blocks)
    in_a = pl.BlockSpec((ROWS, width), lambda g: (jnp.where(g == steps - 1, 0, head), 0))
    in_b = pl.BlockSpec((ROWS, width), lambda g: (jnp.clip(g - 1, 0, steps - 3), 0))
    out_shape = (shape[0] // 4, shape[1])
    return pl.pallas_call(
        functools.partial(second_kernel, head),
        grid=(steps,),
        in_specs=[
            pl.BlockSpec(memory_space=pltpu.SMEM),
            pl.BlockSpec(op_block, lambda g: (at(g), 0, 0, 0)),
            pl.BlockSpec(shape, lambda g: (0, 0)),
            whole(firsts[0]),
            whole(seconds[0]),
            pl.BlockSpec((ROWS, width), lambda g: (at(g), 0)),
        ]
        + [in_a] * 4
        + [in_b] * 4,
        out_specs=[pl.BlockSpec(out_shape, lambda g: (0, 0))] * 4,
        out_shape=[jax.ShapeDtypeStruct(out_shape, BF16)] * 4,
        scratch_shapes=[pltpu.VMEM((blocks * ROWS + 6 * HALO, width), F32), pltpu.VMEM(shape, F32)],
        compiler_params=pltpu.CompilerParams(vmem_limit_bytes=32 * 2**20),
        cost_estimate=cost(steps),
    )(place, operator, before, firsts[0], seconds[0], own, *firsts, *seconds)


RETURNS = (1, -1, 2, -2)


def weigh_kernel(half_width, place_ref, s0, s1, s2, s3, freq_ref, o0, o1, o2, o3, stay_ref, rows_ref):
    atom, mode = place_ref[0], place_ref[1]
    modes = freq_ref.shape[0]
    summed = s0[...].astype(F32) + s1[...].astype(F32) + s2[...].astype(F32) + s3[...].astype(F32)
    squares = summed[0:32] * summed[0:32] + summed[32:64] * summed[32:64] + summed[64:96] * summed[64:96]
    row = lax.broadcasted_iota(jnp.int32, (32, 128), 0) + 32 * atom
    lane = lax.broadcasted_iota(jnp.int32, (32, 128), 1)
    wrapped = lambda b: jnp.where(b >= modes, b - modes, jnp.where(b < 0, b + modes, b))
    top = wrapped(mode + 2)
    top_freq = freq_ref[pl.ds(top, 1), :]
    centre = jnp.sum(jnp.where(row == lane, top_freq, 0.0), axis=1, keepdims=True)
    own = jnp.zeros((32, 128), F32)
    for slot in range(SLOTS):
        block = wrapped(mode + 2 - slot)
        offset = centre - freq_ref[pl.ds(block, 1), :]
        lorentz = (half_width / math.pi) / (offset * offset + half_width * half_width)
        term = jnp.where(block <= top, squares[:, slot * 128 : (slot + 1) * 128] * lorentz, 0.0)
        own += term
        if slot == 2:
            stay_ref[...] = jnp.sum(term, axis=0, keepdims=True)
        elif slot > 0:
            at = RETURNS.index(2 - slot)
            rows_ref[at : at + 1, :] = jnp.sum(term, axis=0, keepdims=True)
    own = jnp.sum(own, axis=1, keepdims=True)
    at = RETURNS.index(2)
    rows_ref[at : at + 1, :] = jnp.sum(jnp.where(row == lane, own, 0.0), axis=0, keepdims=True)
    for k, out in enumerate((o0, o1, o2, o3)):
        out[...] = rows_ref[pl.ds(jnp.bitwise_xor(atom, k), 1), :]


def swapped(x, k):
    return lax.ppermute(x, "atom", [(i, i ^ k) for i in range(4)])


def local(vectors, couplings, neighbours, frequency):
    rows_dev, width = vectors.shape
    atoms_dev = rows_dev // 3
    atom_groups = lax.axis_size("atom")
    modes = lax.axis_size("mode")
    half_width = WIDTH_MODES / (width * modes)
    place = jnp.stack([lax.axis_index("atom"), lax.axis_index("mode")]).astype(jnp.int32)
    edge = 3 * HALO
    cut = SPLIT * ROWS

    own_a, own_b, tail, front = copied_rows(
        [vectors],
        [cut, rows_dev - cut, edge, edge],
        [(0, 0, 0, 0, cut), (0, cut, 1, 0, rows_dev - cut), (0, rows_dev - edge, 2, 0, edge), (0, 0, 3, 0, edge)],
    )
    below = shifted(tail, "atom", 1)
    above = shifted(front, "atom", -1)
    up1a = shifted(own_a, "mode", -1)
    dn1a = shifted(own_a, "mode", 1)
    rest = rows_dev - cut
    [own_b_far] = copied_rows(
        [own_b, below, above],
        [rest + 2 * edge],
        [(0, 0, 0, 0, rest), (1, 0, 0, rest, edge), (2, 0, 0, rest + edge, edge)],
    )
    up1b = shifted(own_b_far, "mode", -1)
    dn1b = shifted(own_b, "mode", 1)
    couplings, own_b_far = lax.optimization_barrier((couplings, own_b_far))
    operator = build_operator(place, couplings, neighbours, atoms_dev * atom_groups)
    up1a, dn1a, operator = lax.optimization_barrier((up1a, dn1a, operator))
    up2a = shifted(up1a, "mode", -1)
    dn2a = shifted(dn1a, "mode", 1)
    up2b = shifted(up1b, "mode", -1)
    dn2b = shifted(dn1b, "mode", 1)

    shares = star_products(place, operator, vectors, [up2a, up1a, dn1a, dn2a], [up2b, up1b, dn1b, dn2b])
    shares = [shares[0]] + [swapped(shares[k], k) for k in range(1, 4)]

    vmem = pl.BlockSpec(memory_space=pltpu.VMEM)
    row = jax.ShapeDtypeStruct((1, width), F32)
    *terms, stay = pl.pallas_call(
        functools.partial(weigh_kernel, half_width),
        in_specs=[pl.BlockSpec(memory_space=pltpu.SMEM)] + [vmem] * 5,
        out_specs=[vmem] * 5,
        out_shape=[row] * 5,
        scratch_shapes=[pltpu.VMEM((4, width), F32)],
    )(place, *shares, frequency.reshape(modes, width))
    carried = terms[0]
    for k in range(1, 4):
        carried = carried + swapped(terms[k], k)
    route = [(b * 4 + s, (b + RETURNS[s]) % modes * 4 + s) for b in range(modes) for s in range(4)]
    result = stay + lax.ppermute(carried, ("mode", "atom"), route)
    far = [swapped(result, k) for k in range(1, 4)]
    total = (result + far[0]) + (far[1] + far[2])
    own_freq = lax.dynamic_slice_in_dim(frequency, place[1] * width, width)
    return math.pi / (3.0 * own_freq * own_freq) * total.reshape(width)


def solution(mesh):
    return jax.shard_map(
        local,
        mesh=mesh,
        in_specs=(P("atom", "mode"), P(None, None, None, None, "atom"), P(None, "atom"), P()),
        out_specs=P("mode"),
        check_vma=False,
    )
```

time: 131 us -> 158 us (1.21)
  Pallas kernels: 26 us -> 77.5 us
  local copies, waits for them, and re-layouts: 15.1 us -> 4.5 us
  waiting for transfers between devices: 36.2 us -> 27.5 us
  starting transfers between devices: 48.3 us -> 45.5 us
  other arithmetic: 4.58 us -> 2.63 us
    pallas_call x1 -> x3, Pallas kernels: 11.3 us -> 63.3 us  [the longest x2 52.9 us: copied_rows(): pl.pallas_call(functools.partial(copy_kernel, moves), in_specs=[pl.BlockS...]
    ppermute x17 -> x10, starting transfers between devices: 45.5 us -> 27.5 us  [shifted(): lax.ppermute(x, axis, [(i, (i + distance) % count) for i in range(count)])]
    ppermute x17 -> x10, waiting for transfers between devices: 35 us -> 17.4 us  [shifted(): lax.ppermute(x, axis, [(i, (i + distance) % count) for i in range(count)])]
    ppermute x3 -> x10, starting transfers between devices: 2.79 us -> 18 us  [the longest x9 15.2 us: swapped(): return lax.ppermute(x, 'atom', [(i, i ^ k) for i in range(4)])]
    ppermute x3 -> x10, waiting for transfers between devices: 1.22 us -> 10.2 us  [the longest x9 9.44 us: swapped(): return lax.ppermute(x, 'atom', [(i, i ^ k) for i in range(4)])]
    slice x3 -> x0, local copies, waits for them, and re-layouts: 4.59 us -> none  [the longest x1 2.07 us: local(): own_a = vectors[:cut]]
    pallas_call x1, Pallas kernels: 5.54 us -> 2.62 us  [star_products(): pl.pallas_call(first_kernel, grid=(SPLIT - 2,), in_specs=[pl.BlockSpec(op...]
    broadcast_in_dim x6 -> x0, local copies, waits for them, and re-layouts: 2.71 us -> none  [the longest x2 1.43 us: local(): centre = jnp.broadcast_to(centre[:, None], (32, width))]
  transfers between devices with their start and end apart: 20 -> 20, of which waited for: 9 -> 10; matrix products, arithmetic and copies ran while one was open for 9% -> 1% of each run, Pallas kernels for 13% -> 20%
where the time goes in v2:
time: 158 us
  Pallas kernels  77.5 us (49%)
  starting transfers between devices  45.5 us (29%)
  waiting for transfers between devices  27.5 us (17%)
  local copies, waits for them, and re-layouts  4.5 us (3%)
  other arithmetic  2.63 us (2%)
    pallas_call x2, Pallas kernels, copied_rows(): pl.pallas_call(functools.partial(copy_kernel, moves), in_specs=[pl.BlockS...  52.9 us
    ppermute x10, starting transfers between devices, shifted(): lax.ppermute(x, axis, [(i, (i + distance) % count) for i in range(count)])  27.5 us
    ppermute x10, waiting for transfers between devices, shifted(): lax.ppermute(x, axis, [(i, (i + distance) % count) for i in range(count)])  17.4 us
    ppermute x9, starting transfers between devices, swapped(): return lax.ppermute(x, 'atom', [(i, i ^ k) for i in range(4)])  15.2 us
    pallas_call x1, Pallas kernels, build_operator(): pl.pallas_call(functools.partial(operator_kernel, total_atoms), grid=(blo...  10.4 us
    pallas_call x1, Pallas kernels, star_products(): pl.pallas_call(functools.partial(second_kernel, head), grid=(steps,), in_...  9.75 us
    ppermute x9, waiting for transfers between devices, swapped(): return lax.ppermute(x, 'atom', [(i, i ^ k) for i in range(4)])  9.44 us
    unnamed x20, local copies, waits for them, and re-layouts  3.26 us
  transfers between devices with their start and end apart: 20, of which 10 were waited for; matrix products, arithmetic and copies ran while one was open for 1% of the time, Pallas kernels for 20%

profile of v2, /device:TPU:1, one launch (start us, length us, event | category | flops | bytes accessed | tf_op | source)
XLA Modules:
  0.0 157.8 jit_solution(4194436279669955248)
XLA Ops:
  0.0 33.9 %shard_map.46 = (bf16[1920,128]{1,0:T(8,128)(2,1)}, bf16[1920,128]{1,0:T(8,128)(2,1)}, bf16[192,128]{1,0:T(8,128)(2,1)}, bf16[192,128]{1,0:T(8,128)(2,1)}) custom-call(bf16[3840,128]{1,0:T(8,128)(2,1)} %own.1), custom_call_target="tpu_custom_call" | custom-call | tf_op jit(solution)/shard_map/pallas_call | solution.py:97
  33.9 2.7 %collective-permute-start.2 = (bf16[192,128]{1,0:T(8,128)(2,1)}, bf16[192,128]{1,0:T(8,128)(2,1)S(1)}, u32[]{:S(2)}, u32[]{:S(2)}) collective-permute-start(bf16[192,128]{1,0:T(8,128)(2,1)} %get-tuple-element.24), channel_id=1, source_target_pairs={{0,1},{1,2},{2,3},{3,0},{4,5},{5,6},{6,7},{7,4},{8,9},{9,10},{10,1... | collective-permute-start | bytes 147464 | tf_op jit(solution)/shard_map/ppermute | solution.py:24
  36.6 0.7 collective-permute-start.3
  37.3 0.9 collective-permute-start.1
  38.2 8.6 %collective-permute-start = (bf16[1920,128]{1,0:T(8,128)(2,1)}, bf16[1920,128]{1,0:T(8,128)(2,1)S(1)}, u32[]{:S(2)}, u32[]{:S(2)}) collective-permute-start(bf16[1920,128]{1,0:T(8,128)(2,1)} %get-tuple-element.22), channel_id=1, source_target_pairs={{0,252},{4,0},{8,4},{12,8},{16,12},{20,16},{24,20},{28,24},{32,28}... | collective-permute-start | bytes 1474568 | tf_op jit(solution)/shard_map/ppermute | solution.py:24
  46.8 0.0 collective-permute-start.8
  46.8 0.0 collective-permute-done.2.refs_1_
  46.8 0.0 collective-permute-done.3.refs_2_
  46.8 0.6 copy-done.8
  47.4 0.6 copy-done.9
  48.0 19.0 %shard_map.47 = bf16[2304,128]{1,0:T(8,128)(2,1)} custom-call(bf16[1920,128]{1,0:T(8,128)(2,1)} %get-tuple-element.23.refs_0_, bf16[192,128]{1,0:T(8,128)(2,1)} %copy-done.8, bf16[192,128]{1,0:T(8,128)(2,1)} %copy-done.9), custom_call_target="tpu_custom_call" | custom-call | tf_op jit(solution)/shard_map/pallas_call | solution.py:97
  67.0 7.3 %collective-permute-start.6 = (bf16[2304,128]{1,0:T(8,128)(2,1)}, bf16[2304,128]{1,0:T(8,128)(2,1)S(1)}, u32[]{:S(2)}, u32[]{:S(2)}) collective-permute-start(bf16[2304,128]{1,0:T(8,128)(2,1)} %shard_map.47), channel_id=1, source_target_pairs={{0,252},{4,0},{8,4},{12,8},{16,12},{20,16},{24,20},{28,24},{32,28}... | collective-permute-start | bytes 1769480 | tf_op jit(solution)/shard_map/ppermute | solution.py:24
  74.3 0.1 pad_add_fusion.place_ref
  74.4 1.2 copy.5.couplings_ref
  75.6 0.0 copy-start.3
  75.6 0.7 copy-done.3
  76.3 10.4 %shard_map.48.t_ref = bf16[10,3,768,384]{3,2,1,0:T(8,128)(2,1)S(1)} custom-call(s32[2]{0:T(128)S(1)} %pad_add_fusion.place_ref, f32[4,3,3,3,1280]{4,3,2,1,0:T(4,128)S(1)} %copy.5.couplings_ref, s32[4,1280]{1,0:T(4,128)S(1)} %copy-done.3), custom_call_target="tpu_custom_call" | custom-call | flops 4000000000 | bytes 20000000 | tf_op jit(solution)/shard_map/pallas_call | solution.py:66
  86.7 0.0 copy-start
  86.8 0.0 collective-permute-done.1.p3.a2
  86.8 0.0 collective-permute-done.p1.a1
  86.8 0.1 collective-permute-start.4
  86.9 1.5 collective-permute-start.5
  88.3 0.0 collective-permute-done.6.b1
  88.3 5.8 %collective-permute-start.7 = (bf16[2304,128]{1,0:T(8,128)(2,1)S(1)}, bf16[2304,128]{1,0:T(8,128)(2,1)S(1)}, u32[]{:S(2)}, u32[]{:S(2)}) collective-permute-start(bf16[2304,128]{1,0:T(8,128)(2,1)S(1)} %collective-permute-done.6.b1), channel_id=1, source_target_pairs={{0,252},{4,0},{8,4},{12,8},{16,12},{20,16},{24,20},{28,24},{32,28}... | collective-permute-start | bytes 1769480 | tf_op jit(solution)/shard_map/ppermute | solution.py:24
  94.1 0.0 collective-permute-done.8.b2
  94.1 0.0 collective-permute-start.9
  94.1 3.6 %collective-permute-done.4.far_ref.p0.far_a.a0 = bf16[1920,128]{1,0:T(8,128)(2,1)S(1)} collective-permute-done((bf16[1920,128]{1,0:T(8,128)(2,1)S(1)}, bf16[1920,128]{1,0:T(8,128)(2,1)S(1)}, u32[]{:S(2)}, u32[]{:S(2)}) %collective-permute-start.4) | collective-permute-done | bytes 491552 | tf_op jit(solution)/shard_map/ppermute | solution.py:24
  97.8 5.8 %collective-permute-done.5.p4.a3 = bf16[1920,128]{1,0:T(8,128)(2,1)S(1)} collective-permute-done((bf16[1920,128]{1,0:T(8,128)(2,1)S(1)}, bf16[1920,128]{1,0:T(8,128)(2,1)S(1)}, u32[]{:S(2)}, u32[]{:S(2)}) %collective-permute-start.5) | collective-permute-done | bytes 491552 | tf_op jit(solution)/shard_map/ppermute | solution.py:24
  103.6 0.0 copy-done.1
  103.6 2.6 %shard_map.49.before_ref = f32[384,640]{1,0:T(8,128)S(1)} custom-call(bf16[10,3,768,384]{3,2,1,0:T(8,128)(2,1)S(1)} %shard_map.48.t_ref, bf16[1920,128]{1,0:T(8,128)(2,1)S(1)} %collective-permute-done.4.far_ref.p0.far_a.a0, bf16[1920,128]{1,0:T(8,128)(2,1)S(1)} %collective-permute-done.4.far_ref.p0.far_a.a0, ...), custom_call_target="tpu_custom_call" | custom-call | flops 3000000000 | bytes 9000000 | tf_op jit(solution)/shard_map/pallas_call | solution.py:172
  106.2 7.9 %collective-permute-done.9.b3 = bf16[1920,128]{1,0:T(8,128)(2,1)S(1)} collective-permute-done((bf16[1920,128]{1,0:T(8,128)(2,1)S(1)}, bf16[1920,128]{1,0:T(8,128)(2,1)S(1)}, u32[]{:S(2)}, u32[]{:S(2)}) %collective-permute-start.9) | collective-permute-done | bytes 491552 | tf_op jit(solution)/shard_map/ppermute | solution.py:24
  114.1 0.0 collective-permute-done.7.far_b.b0
  114.1 0.0 copy-done.4
  114.1 0.0 copy-done
  114.2 9.7 %shard_map.50 = (bf16[96,640]{1,0:T(8,128)(2,1)S(1)}, bf16[96,640]{1,0:T(8,128)(2,1)S(1)}, bf16[96,640]{1,0:T(8,128)(2,1)S(1)}, bf16[96,640]{1,0:T(8,128)(2,1)S(1)}) custom-call(s32[2]{0:T(128)S(1)} %pad_add_fusion.place_ref, bf16[10,3,768,384]{3,2,1,0:T(8,128)(2,1)} %copy-done, f32[384,640]{1,0:T(8,128)S(1)} %shard_map.49.before_ref, ...), custom_call_target="tpu_custom_call" | custom-call | flops 7000000000 | bytes 21000000 | tf_op jit(solution)/shard_map/pallas_call | solution.py:187
  123.9 0.0 copy-start.2
  123.9 0.6 copy-done.2
  124.5 2.7 %collective-permute-start.10 = (bf16[96,640]{1,0:T(8,128)(2,1)S(1)}, bf16[96,640]{1,0:T(8,128)(2,1)S(1)}, u32[]{:S(2)}, u32[]{:S(2)}) collective-permute-start(bf16[96,640]{1,0:T(8,128)(2,1)S(1)} %get-tuple-element.31), channel_id=1, source_target_pairs={{0,1},{1,0},{2,3},{3,2},{4,5},{5,4},{6,7},{7,6},{8,9},{9,8},{10,11... | collective-permute-start | bytes 368648 | tf_op jit(solution)/shard_map/ppermute | solution.py:242
  127.3 0.0 collective-permute-start.11
  127.3 1.6 %collective-permute-start.12 = (bf16[96,640]{1,0:T(8,128)(2,1)S(1)}, bf16[96,640]{1,0:T(8,128)(2,1)S(1)}, u32[]{:S(2)}, u32[]{:S(2)}) collective-permute-start(bf16[96,640]{1,0:T(8,128)(2,1)S(1)} %get-tuple-element.33), channel_id=1, source_target_pairs={{0,3},{1,2},{2,1},{3,0},{4,7},{5,6},{6,5},{7,4},{8,11},{9,10},{10,... | collective-permute-start | bytes 368648 | tf_op jit(solution)/shard_map/ppermute | solution.py:242
  128.9 0.0 collective-permute-done.10.s1
  128.9 3.3 %collective-permute-done.11.s2 = bf16[96,640]{1,0:T(8,128)(2,1)S(1)} collective-permute-done((bf16[96,640]{1,0:T(8,128)(2,1)S(1)}, bf16[96,640]{1,0:T(8,128)(2,1)S(1)}, u32[]{:S(2)}, u32[]{:S(2)}) %collective-permute-start.11) | collective-permute-done | bytes 122912 | tf_op jit(solution)/shard_map/ppermute | solution.py:242
  132.2 2.7 %collective-permute-done.12.s3 = bf16[96,640]{1,0:T(8,128)(2,1)S(1)} collective-permute-done((bf16[96,640]{1,0:T(8,128)(2,1)S(1)}, bf16[96,640]{1,0:T(8,128)(2,1)S(1)}, u32[]{:S(2)}, u32[]{:S(2)}) %collective-permute-start.12) | collective-permute-done | bytes 122912 | tf_op jit(solution)/shard_map/ppermute | solution.py:242
  134.9 0.0 copy-done.5
  134.9 0.0 copy-done.6
  134.9 0.7 copy-done.7
  135.6 1.9 %shard_map.51 = (f32[1,128]{1,0:T(1,128)}, f32[1,128]{1,0:T(1,128)}, f32[1,128]{1,0:T(1,128)}, f32[1,128]{1,0:T(1,128)}, f32[1,128]{1,0:T(1,128)}) custom-call(s32[2]{0:T(128)} %copy-done.4, bf16[96,640]{1,0:T(8,128)(2,1)} %copy-done.2, bf16[96,640]{1,0:T(8,128)(2,1)} %copy-done.5, bf16[96,640]{1,0:T(8,128)(2,1)} %copy-done.6, bf16[96,640]{1,0:T(8,128)(2,1)} %copy-done.7, ...), custom_call_target="tpu_custom_call" | custom-call | tf_op jit(solution)/shard_map/pallas_call | solution.py:285
  137.5 0.3 collective-permute-start.13
  137.8 0.1 collective-permute-start.14
  137.9 1.8 %collective-permute-start.15 = (f32[1,128]{1,0:T(1,128)}, f32[1,128]{1,0:T(1,128)S(1)}, u32[]{:S(2)}, u32[]{:S(2)}) collective-permute-start(f32[1,128]{1,0:T(1,128)} %get-tuple-element.38), channel_id=1, source_target_pairs={{0,3},{1,2},{2,1},{3,0},{4,7},{5,6},{6,5},{7,4},{8,11},{9,10},{10,... | collective-permute-start | bytes 1544 | tf_op jit(solution)/shard_map/ppermute | solution.py:242
  139.6 0.0 collective-permute-done.13
  139.6 0.7 collective-permute-done.14
  140.4 0.7 collective-permute-done.15
  141.1 0.6 add_add_fusion
  141.7 2.7 %collective-permute-start.16 = (f32[1,128]{1,0:T(1,128)S(1)}, f32[1,128]{1,0:T(1,128)S(1)}, u32[]{:S(2)}, u32[]{:S(2)}) collective-permute-start(f32[1,128]{1,0:T(1,128)S(1)} %add_add_fusion), channel_id=1, source_target_pairs={{0,4},{1,253},{2,10},{3,251},{4,8},{5,1},{6,14},{7,255},{8,12},{9,... | collective-permute-start | bytes 1544 | tf_op jit(solution)/shard_map/ppermute | solution.py:296
  144.4 0.7 collective-permute-done.16
  145.1 0.7 add.28
  145.8 8.3 %collective-permute-start.19 = (f32[1,128]{1,0:T(1,128)S(1)}, f32[1,128]{1,0:T(1,128)S(1)}, u32[]{:S(2)}, u32[]{:S(2)}) collective-permute-start(f32[1,128]{1,0:T(1,128)S(1)} %add.28), channel_id=1, source_target_pairs={{0,3},{1,2},{2,1},{3,0},{4,7},{5,6},{6,5},{7,4},{8,11},{9,10},{10,... | collective-permute-start | bytes 1544 | tf_op jit(solution)/shard_map/ppermute | solution.py:242
  154.1 0.0 collective-permute-start.18
  154.1 0.4 collective-permute-start.17
  154.5 0.8 collective-permute-done.19
  155.3 1.2 collective-permute-done.18
  156.5 0.0 collective-permute-done.17
  156.5 1.3 divide_multiply_fusion
  (7 shorter events, 0.0 us)
Async XLA Ops:
  0.0 103.6 %copy-start.1 = (bf16[3840,128]{1,0:T(8,128)(2,1)S(1)}, bf16[3840,128]{1,0:T(8,128)(2,1)}, u32[]{:S(2)}) copy-start(bf16[3840,128]{1,0:T(8,128)(2,1)} %own.1) | copy-start | bytes 2949124
  33.9 12.9 %collective-permute-start.2 = (bf16[192,128]{1,0:T(8,128)(2,1)}, bf16[192,128]{1,0:T(8,128)(2,1)S(1)}, u32[]{:S(2)}, u32[]{:S(2)}) collective-permute-start(bf16[192,128]{1,0:T(8,128)(2,1)} %get-tuple-element.24), channel_id=1, source_target_pairs={{0,1},{1,2},{2,3},{3,0},{4,5},{5,6},{6,7},{7,4},{8,9},{9,10},{10,1... | collective-permute-start | bytes 147464 | tf_op jit(solution)/shard_map/ppermute | solution.py:24
  36.6 10.2 %collective-permute-start.3 = (bf16[192,128]{1,0:T(8,128)(2,1)}, bf16[192,128]{1,0:T(8,128)(2,1)S(1)}, u32[]{:S(2)}, u32[]{:S(2)}) collective-permute-start(bf16[192,128]{1,0:T(8,128)(2,1)} %get-tuple-element.25), channel_id=1, source_target_pairs={{0,3},{1,0},{2,1},{3,2},{4,7},{5,4},{6,5},{7,6},{8,11},{9,8},{10,9... | collective-permute-start | bytes 147464 | tf_op jit(solution)/shard_map/ppermute | solution.py:24
  37.3 49.4 %collective-permute-start.1 = (bf16[1920,128]{1,0:T(8,128)(2,1)}, bf16[1920,128]{1,0:T(8,128)(2,1)S(1)}, u32[]{:S(2)}, u32[]{:S(2)}) collective-permute-start(bf16[1920,128]{1,0:T(8,128)(2,1)} %get-tuple-element.22), channel_id=1, source_target_pairs={{0,4},{4,8},{8,12},{12,16},{16,20},{20,24},{24,28},{28,32},{32,36}... | collective-permute-start | bytes 1474568 | tf_op jit(solution)/shard_map/ppermute | solution.py:24
  38.2 48.5 %collective-permute-start = (bf16[1920,128]{1,0:T(8,128)(2,1)}, bf16[1920,128]{1,0:T(8,128)(2,1)S(1)}, u32[]{:S(2)}, u32[]{:S(2)}) collective-permute-start(bf16[1920,128]{1,0:T(8,128)(2,1)} %get-tuple-element.22), channel_id=1, source_target_pairs={{0,252},{4,0},{8,4},{12,8},{16,12},{20,16},{24,20},{28,24},{32,28}... | collective-permute-start | bytes 1474568 | tf_op jit(solution)/shard_map/ppermute | solution.py:24
  46.8 47.4 %collective-permute-start.8 = (bf16[1920,128]{1,0:T(8,128)(2,1)}, bf16[1920,128]{1,0:T(8,128)(2,1)S(1)}, u32[]{:S(2)}, u32[]{:S(2)}) collective-permute-start(bf16[1920,128]{1,0:T(8,128)(2,1)} %get-tuple-element.23.refs_0_), channel_id=1, source_target_pairs={{0,4},{4,8},{8,12},{12,16},{16,20},{20,24},{24,28},{28,32},{32,36}... | collective-permute-start | bytes 1474568 | tf_op jit(solution)/shard_map/ppermute | solution.py:24
  46.8 0.6 copy-start.8
  47.4 0.6 copy-start.9
  67.0 21.3 %collective-permute-start.6 = (bf16[2304,128]{1,0:T(8,128)(2,1)}, bf16[2304,128]{1,0:T(8,128)(2,1)S(1)}, u32[]{:S(2)}, u32[]{:S(2)}) collective-permute-start(bf16[2304,128]{1,0:T(8,128)(2,1)} %shard_map.47), channel_id=1, source_target_pairs={{0,252},{4,0},{8,4},{12,8},{16,12},{20,16},{24,20},{28,24},{32,28}... | collective-permute-start | bytes 1769480 | tf_op jit(solution)/shard_map/ppermute | solution.py:24
  74.4 39.8 %copy-start.4 = (s32[2]{0:T(128)}, s32[2]{0:T(128)S(1)}, u32[]{:S(2)}) copy-start(s32[2]{0:T(128)S(1)} %pad_add_fusion.place_ref) | copy-start | bytes 28
  75.6 0.7 copy-start.3
  86.7 27.4 %copy-start = (bf16[10,3,768,384]{3,2,1,0:T(8,128)(2,1)}, bf16[10,3,768,384]{3,2,1,0:T(8,128)(2,1)S(1)}, u32[]{:S(2)}) copy-start(bf16[10,3,768,384]{3,2,1,0:T(8,128)(2,1)S(1)} %shard_map.48.t_ref) | copy-start | bytes 53084164
  86.8 11.0 %collective-permute-start.4 = (bf16[1920,128]{1,0:T(8,128)(2,1)S(1)}, bf16[1920,128]{1,0:T(8,128)(2,1)S(1)}, u32[]{:S(2)}, u32[]{:S(2)}) collective-permute-start(bf16[1920,128]{1,0:T(8,128)(2,1)S(1)} %collective-permute-done.p1.a1), channel_id=1, source_target_pairs={{0,252},{4,0},{8,4},{12,8},{16,12},{20,16},{24,20},{28,24},{32,28}... | collective-permute-start | bytes 1474568 | tf_op jit(solution)/shard_map/ppermute | solution.py:24
  86.9 16.7 %collective-permute-start.5 = (bf16[1920,128]{1,0:T(8,128)(2,1)S(1)}, bf16[1920,128]{1,0:T(8,128)(2,1)S(1)}, u32[]{:S(2)}, u32[]{:S(2)}) collective-permute-start(bf16[1920,128]{1,0:T(8,128)(2,1)S(1)} %collective-permute-done.1.p3.a2), channel_id=1, source_target_pairs={{0,4},{4,8},{8,12},{12,16},{16,20},{20,24},{24,28},{28,32},{32,36}... | collective-permute-start | bytes 1474568 | tf_op jit(solution)/shard_map/ppermute | solution.py:24
  88.3 25.8 %collective-permute-start.7 = (bf16[2304,128]{1,0:T(8,128)(2,1)S(1)}, bf16[2304,128]{1,0:T(8,128)(2,1)S(1)}, u32[]{:S(2)}, u32[]{:S(2)}) collective-permute-start(bf16[2304,128]{1,0:T(8,128)(2,1)S(1)} %collective-permute-done.6.b1), channel_id=1, source_target_pairs={{0,252},{4,0},{8,4},{12,8},{16,12},{20,16},{24,20},{28,24},{32,28}... | collective-permute-start | bytes 1769480 | tf_op jit(solution)/shard_map/ppermute | solution.py:24
  94.1 20.0 %collective-permute-start.9 = (bf16[1920,128]{1,0:T(8,128)(2,1)S(1)}, bf16[1920,128]{1,0:T(8,128)(2,1)S(1)}, u32[]{:S(2)}, u32[]{:S(2)}) collective-permute-start(bf16[1920,128]{1,0:T(8,128)(2,1)S(1)} %collective-permute-done.8.b2), channel_id=1, source_target_pairs={{0,4},{4,8},{8,12},{12,16},{16,20},{20,24},{24,28},{28,32},{32,36}... | collective-permute-start | bytes 1474568 | tf_op jit(solution)/shard_map/ppermute | solution.py:24
  123.9 0.6 copy-start.2
  124.5 4.3 %collective-permute-start.10 = (bf16[96,640]{1,0:T(8,128)(2,1)S(1)}, bf16[96,640]{1,0:T(8,128)(2,1)S(1)}, u32[]{:S(2)}, u32[]{:S(2)}) collective-permute-start(bf16[96,640]{1,0:T(8,128)(2,1)S(1)} %get-tuple-element.31), channel_id=1, source_target_pairs={{0,1},{1,0},{2,3},{3,2},{4,5},{5,4},{6,7},{7,6},{8,9},{9,8},{10,11... | collective-permute-start | bytes 368648 | tf_op jit(solution)/shard_map/ppermute | solution.py:242
  127.3 5.0 %collective-permute-start.11 = (bf16[96,640]{1,0:T(8,128)(2,1)S(1)}, bf16[96,640]{1,0:T(8,128)(2,1)S(1)}, u32[]{:S(2)}, u32[]{:S(2)}) collective-permute-start(bf16[96,640]{1,0:T(8,128)(2,1)S(1)} %get-tuple-element.32), channel_id=1, source_target_pairs={{0,2},{1,3},{2,0},{3,1},{4,6},{5,7},{6,4},{7,5},{8,10},{9,11},{10,... | collective-permute-start | bytes 368648 | tf_op jit(solution)/shard_map/ppermute | solution.py:242
  127.3 7.7 %collective-permute-start.12 = (bf16[96,640]{1,0:T(8,128)(2,1)S(1)}, bf16[96,640]{1,0:T(8,128)(2,1)S(1)}, u32[]{:S(2)}, u32[]{:S(2)}) collective-permute-start(bf16[96,640]{1,0:T(8,128)(2,1)S(1)} %get-tuple-element.33), channel_id=1, source_target_pairs={{0,3},{1,2},{2,1},{3,0},{4,7},{5,6},{6,5},{7,4},{8,11},{9,10},{10,... | collective-permute-start | bytes 368648 | tf_op jit(solution)/shard_map/ppermute | solution.py:242
  128.9 6.0 %copy-start.5 = (bf16[96,640]{1,0:T(8,128)(2,1)}, bf16[96,640]{1,0:T(8,128)(2,1)S(1)}, u32[]{:S(2)}) copy-start(bf16[96,640]{1,0:T(8,128)(2,1)S(1)} %collective-permute-done.10.s1) | copy-start | bytes 368644
  132.2 2.7 %copy-start.6 = (bf16[96,640]{1,0:T(8,128)(2,1)}, bf16[96,640]{1,0:T(8,128)(2,1)S(1)}, u32[]{:S(2)}) copy-start(bf16[96,640]{1,0:T(8,128)(2,1)S(1)} %collective-permute-done.11.s2) | copy-start | bytes 368644
  134.9 0.7 copy-start.7
  137.5 2.2 %collective-permute-start.13 = (f32[1,128]{1,0:T(1,128)}, f32[1,128]{1,0:T(1,128)S(1)}, u32[]{:S(2)}, u32[]{:S(2)}) collective-permute-start(f32[1,128]{1,0:T(1,128)} %get-tuple-element.36), channel_id=1, source_target_pairs={{0,1},{1,0},{2,3},{3,2},{4,5},{5,4},{6,7},{7,6},{8,9},{9,8},{10,11... | collective-permute-start | bytes 1544 | tf_op jit(solution)/shard_map/ppermute | solution.py:242
  137.8 2.6 %collective-permute-start.14 = (f32[1,128]{1,0:T(1,128)}, f32[1,128]{1,0:T(1,128)S(1)}, u32[]{:S(2)}, u32[]{:S(2)}) collective-permute-start(f32[1,128]{1,0:T(1,128)} %get-tuple-element.37), channel_id=1, source_target_pairs={{0,2},{1,3},{2,0},{3,1},{4,6},{5,7},{6,4},{7,5},{8,10},{9,11},{10,... | collective-permute-start | bytes 1544 | tf_op jit(solution)/shard_map/ppermute | solution.py:242
  137.9 3.2 %collective-permute-start.15 = (f32[1,128]{1,0:T(1,128)}, f32[1,128]{1,0:T(1,128)S(1)}, u32[]{:S(2)}, u32[]{:S(2)}) collective-permute-start(f32[1,128]{1,0:T(1,128)} %get-tuple-element.38), channel_id=1, source_target_pairs={{0,3},{1,2},{2,1},{3,0},{4,7},{5,6},{6,5},{7,4},{8,11},{9,10},{10,... | collective-permute-start | bytes 1544 | tf_op jit(solution)/shard_map/ppermute | solution.py:242
  141.7 3.4 %collective-permute-start.16 = (f32[1,128]{1,0:T(1,128)S(1)}, f32[1,128]{1,0:T(1,128)S(1)}, u32[]{:S(2)}, u32[]{:S(2)}) collective-permute-start(f32[1,128]{1,0:T(1,128)S(1)} %add_add_fusion), channel_id=1, source_target_pairs={{0,4},{1,253},{2,10},{3,251},{4,8},{5,1},{6,14},{7,255},{8,12},{9,... | collective-permute-start | bytes 1544 | tf_op jit(solution)/shard_map/ppermute | solution.py:296
  145.8 9.6 %collective-permute-start.19 = (f32[1,128]{1,0:T(1,128)S(1)}, f32[1,128]{1,0:T(1,128)S(1)}, u32[]{:S(2)}, u32[]{:S(2)}) collective-permute-start(f32[1,128]{1,0:T(1,128)S(1)} %add.28), channel_id=1, source_target_pairs={{0,3},{1,2},{2,1},{3,0},{4,7},{5,6},{6,5},{7,4},{8,11},{9,10},{10,... | collective-permute-start | bytes 1544 | tf_op jit(solution)/shard_map/ppermute | solution.py:242
  154.1 2.4 %collective-permute-start.18 = (f32[1,128]{1,0:T(1,128)S(1)}, f32[1,128]{1,0:T(1,128)S(1)}, u32[]{:S(2)}, u32[]{:S(2)}) collective-permute-start(f32[1,128]{1,0:T(1,128)S(1)} %add.28), channel_id=1, source_target_pairs={{0,2},{1,3},{2,0},{3,1},{4,6},{5,7},{6,4},{7,5},{8,10},{9,11},{10,... | collective-permute-start | bytes 1544 | tf_op jit(solution)/shard_map/ppermute | solution.py:242
  154.1 2.4 %collective-permute-start.17 = (f32[1,128]{1,0:T(1,128)S(1)}, f32[1,128]{1,0:T(1,128)S(1)}, u32[]{:S(2)}, u32[]{:S(2)}) collective-permute-start(f32[1,128]{1,0:T(1,128)S(1)} %add.28), channel_id=1, source_target_pairs={{0,1},{1,0},{2,3},{3,2},{4,5},{5,4},{6,7},{7,6},{8,9},{9,8},{10,11... | collective-permute-start | bytes 1544 | tf_op jit(solution)/shard_map/ppermute | solution.py:242

commit v3 on v2

--- a/solution.py
+++ b/solution.py
@@ -49,16 +49,22 @@
             own[at] = spread[at : at + 1]
             if k % 2 == 0:
                 own[at] = own[at] + jnp.where(same[k // 2], spread[at + 9 : at + 10], 0.0)
-    for first_row, slots in ((0, (2, 3)), (HALO, (0, 1, 2, 3)), (2 * HALO, (0, 1, 2, 3)), (3 * HALO, (0, 1))):
-        row = lax.broadcasted_iota(jnp.int32, (HALO, ROWS), 0).astype(F32) + float(first_row)
-        masks = {k: row == reach[k] for k in slots}
-        for a in range(3):
-            for q in range(3):
-                value = jnp.zeros((HALO, ROWS), F32)
-                for k in reversed(slots):
-                    value = jnp.where(masks[k], own[(k * 3 + a) * 3 + q], value)
-                start = q * WIN + first_row
-                out_ref[0, a, start : start + HALO, :] = value.astype(BF16)
+    tile = 16
+    for c in range(3):
+        lanes = slice(c * 128, (c + 1) * 128)
+        wide = {at: jnp.broadcast_to(own[at][:, lanes], (tile, 128)) for at in own}
+        goal = [jnp.broadcast_to(reach[k][:, lanes], (tile, 128)) for k in range(4)]
+        for first_row in range(0, WIN, tile):
+            slots = ((2, 3), (0, 1, 2, 3), (0, 1, 2, 3), (0, 1))[first_row // HALO]
+            row = lax.broadcasted_iota(jnp.int32, (tile, 128), 0).astype(F32) + float(first_row)
+            masks = {k: row == goal[k] for k in slots}
+            for a in range(3):
+                for q in range(3):
+                    value = jnp.zeros((tile, 128), F32)
+                    for k in reversed(slots):
+                        value = jnp.where(masks[k], wide[(k * 3 + a) * 3 + q], value)
+                    start = q * WIN + first_row
+                    out_ref[0, a, start : start + tile, lanes] = value.astype(BF16)
 
 
 def build_operator(place, couplings, neighbours, total_atoms):
@@ -80,15 +86,8 @@
 
 
 def copy_kernel(moves, *refs):
-    sems = refs[-1]
-    copies = [
-        pltpu.make_async_copy(refs[src].at[pl.ds(s0, n)], refs[dst].at[pl.ds(d0, n)], sems.at[c])
-        for c, (src, s0, dst, d0, n) in enumerate(moves)
-    ]
-    for copy in copies:
-        copy.start()
-    for copy in copies:
-        copy.wait()
+    for src, s0, dst, d0, n in moves:
+        refs[dst][d0 : d0 + n, :] = refs[src][s0 : s0 + n, :]
 
 
 def copied_rows(inputs, lengths, moves):
@@ -96,10 +95,7 @@
     moves = [(i, s, len(inputs) + o, d, n) for i, s, o, d, n in moves]
     return pl.pallas_call(
         functools.partial(copy_kernel, moves),
-        in_specs=[pl.BlockSpec(memory_space=pl.ANY)] * len(inputs),
-        out_specs=[pl.BlockSpec(memory_space=pl.ANY)] * len(lengths),
         out_shape=[jax.ShapeDtypeStruct((n, width), inputs[0].dtype) for n in lengths],
-        scratch_shapes=[pltpu.SemaphoreType.DMA((len(moves),))],
     )(*inputs)
 
 
@@ -261,19 +257,13 @@
     above = shifted(front, "atom", -1)
     up1a = shifted(own_a, "mode", -1)
     dn1a = shifted(own_a, "mode", 1)
-    rest = rows_dev - cut
-    [own_b_far] = copied_rows(
-        [own_b, below, above],
-        [rest + 2 * edge],
-        [(0, 0, 0, 0, rest), (1, 0, 0, rest, edge), (2, 0, 0, rest + edge, edge)],
-    )
+    own_b_far = jnp.concatenate([own_b, below, above], axis=0)
     up1b = shifted(own_b_far, "mode", -1)
     dn1b = shifted(own_b, "mode", 1)
-    couplings, own_b_far = lax.optimization_barrier((couplings, own_b_far))
-    operator = build_operator(place, couplings, neighbours, atoms_dev * atom_groups)
-    up1a, dn1a, operator = lax.optimization_barrier((up1a, dn1a, operator))
     up2a = shifted(up1a, "mode", -1)
     dn2a = shifted(dn1a, "mode", 1)
+    couplings, up1b, dn1b = lax.optimization_barrier((couplings, up1b, dn1b))
+    operator = build_operator(place, couplings, neighbours, atoms_dev * atom_groups)
     up2b = shifted(up1b, "mode", -1)
     dn2b = shifted(dn1b, "mode", 1)
 

time: 158 us -> 107 us (0.68)
  Pallas kernels: 77.5 us -> 25.6 us
  waiting for transfers between devices: 27.5 us -> 22.3 us
  starting transfers between devices: 45.5 us -> 48.8 us
    pallas_call x2 -> x1, Pallas kernels: 52.9 us -> 2.22 us  [copied_rows(): pl.pallas_call(functools.partial(copy_kernel, moves), out_shape=[jax.Shap...]
    ppermute x10, waiting for transfers between devices: 17.4 us -> 11.9 us  [shifted(): lax.ppermute(x, axis, [(i, (i + distance) % count) for i in range(count)])]
    ppermute x10, starting transfers between devices: 27.5 us -> 31 us  [shifted(): lax.ppermute(x, axis, [(i, (i + distance) % count) for i in range(count)])]
    ppermute x9, starting transfers between devices: 15.2 us -> 12.8 us  [swapped(): return lax.ppermute(x, 'atom', [(i, i ^ k) for i in range(4)])]
    ppermute x1, starting transfers between devices: 2.7 us -> 5.1 us  [local(): result = stay + lax.ppermute(carried, ('mode', 'atom'), route)]
    unnamed x20 -> x16, local copies, waits for them, and re-layouts: 3.26 us -> 4.72 us
  transfers between devices with their start and end apart: 20 -> 20, of which waited for: 10 -> 9; matrix products, arithmetic and copies ran while one was open for 1% -> 2% of each run, Pallas kernels for 20% -> 11%
where the time goes in v3:
time: 107 us
  starting transfers between devices  48.8 us (46%)
  Pallas kernels  25.6 us (24%)
  waiting for transfers between devices  22.3 us (21%)
  local copies, waits for them, and re-layouts  5.96 us (6%)
  other arithmetic  3.78 us (4%)
    ppermute x10, starting transfers between devices, shifted(): lax.ppermute(x, axis, [(i, (i + distance) % count) for i in range(count)])  31 us
    ppermute x9, starting transfers between devices, swapped(): return lax.ppermute(x, 'atom', [(i, i ^ k) for i in range(4)])  12.8 us
    ppermute x10, waiting for transfers between devices, shifted(): lax.ppermute(x, axis, [(i, (i + distance) % count) for i in range(count)])  11.9 us
    pallas_call x1, Pallas kernels, star_products(): pl.pallas_call(functools.partial(second_kernel, head), grid=(steps,), in_...  9.78 us
    ppermute x9, waiting for transfers between devices, swapped(): return lax.ppermute(x, 'atom', [(i, i ^ k) for i in range(4)])  9.66 us
    pallas_call x1, Pallas kernels, build_operator(): pl.pallas_call(functools.partial(operator_kernel, total_atoms), grid=(blo...  9.04 us
    ppermute x1, starting transfers between devices, local(): result = stay + lax.ppermute(carried, ('mode', 'atom'), route)  5.1 us
    unnamed x16, local copies, waits for them, and re-layouts  4.72 us
  transfers between devices with their start and end apart: 20, of which 9 were waited for; matrix products, arithmetic and copies ran while one was open for 2% of the time, Pallas kernels for 11%

profile of v3, /device:TPU:1, one launch (start us, length us, event | category | flops | bytes accessed | tf_op | source)
XLA Modules:
  0.0 106.5 jit_solution(16510472569276070528)
XLA Ops:
  0.0 2.2 %shard_map.46 = (bf16[1920,128]{1,0:T(8,128)(2,1)}, bf16[1920,128]{1,0:T(8,128)(2,1)}, bf16[192,128]{1,0:T(8,128)(2,1)}, bf16[192,128]{1,0:T(8,128)(2,1)}) custom-call(bf16[3840,128]{1,0:T(8,128)(2,1)} %own.1), custom_call_target="tpu_custom_call" | custom-call | tf_op jit(solution)/shard_map/pallas_call | solution.py:96
  2.2 2.6 %collective-permute-start = (bf16[192,128]{1,0:T(8,128)(2,1)}, bf16[192,128]{1,0:T(8,128)(2,1)S(1)}, u32[]{:S(2)}, u32[]{:S(2)}) collective-permute-start(bf16[192,128]{1,0:T(8,128)(2,1)} %get-tuple-element.22), channel_id=1, source_target_pairs={{0,1},{1,2},{2,3},{3,0},{4,5},{5,6},{6,7},{7,4},{8,9},{9,10},{10,1... | collective-permute-start | bytes 147464 | tf_op jit(solution)/shard_map/ppermute | solution.py:24
  4.8 0.6 collective-permute-start.1
  5.5 1.0 collective-permute-start.6
  6.5 8.6 %collective-permute-start.4 = (bf16[1920,128]{1,0:T(8,128)(2,1)}, bf16[1920,128]{1,0:T(8,128)(2,1)S(1)}, u32[]{:S(2)}, u32[]{:S(2)}) collective-permute-start(bf16[1920,128]{1,0:T(8,128)(2,1)} %get-tuple-element.25), channel_id=1, source_target_pairs={{0,252},{4,0},{8,4},{12,8},{16,12},{20,16},{24,20},{28,24},{32,28}... | collective-permute-start | bytes 1474568 | tf_op jit(solution)/shard_map/ppermute | solution.py:24
  15.0 0.0 collective-permute-done
  15.0 0.0 collective-permute-done.1
  15.0 0.0 copy-start.3
  15.0 1.1 %pad_maximum_fusion = bf16[2304,128]{1,0:T(8,128)(2,1)S(1)} fusion(bf16[192,128]{1,0:T(8,128)(2,1)S(1)} %collective-permute-done.1, bf16[192,128]{1,0:T(8,128)(2,1)S(1)} %collective-permute-done, bf16[1920,128]{1,0:T(8,128)(2,1)} %get-tuple-element.21), kind=kLoop, calls=%fused_computation | loop fusion | flops 1769472 | bytes 1179648 | tf_op jit(solution)/shard_map/concatenate | solution.py:260
  16.1 3.8 %collective-permute-start.2 = (bf16[2304,128]{1,0:T(8,128)(2,1)S(1)}, bf16[2304,128]{1,0:T(8,128)(2,1)}, u32[]{:S(2)}, u32[]{:S(2)}) collective-permute-start(bf16[2304,128]{1,0:T(8,128)(2,1)S(1)} %pad_maximum_fusion), channel_id=1, source_target_pairs={{0,252},{4,0},{8,4},{12,8},{16,12},{20,16},{24,20},{28,24},{32,28}... | collective-permute-start | bytes 1769480 | tf_op jit(solution)/shard_map/ppermute | solution.py:24
  19.9 0.0 collective-permute-start.3
  19.9 6.0 %collective-permute-done.6.p3.a2 = bf16[1920,128]{1,0:T(8,128)(2,1)S(1)} collective-permute-done((bf16[1920,128]{1,0:T(8,128)(2,1)}, bf16[1920,128]{1,0:T(8,128)(2,1)S(1)}, u32[]{:S(2)}, u32[]{:S(2)}) %collective-permute-start.6) | collective-permute-done | bytes 491552 | tf_op jit(solution)/shard_map/ppermute | solution.py:24
  25.9 0.0 collective-permute-start.7
  25.9 0.0 collective-permute-done.4.p1.a1
  25.9 7.2 %collective-permute-start.5 = (bf16[1920,128]{1,0:T(8,128)(2,1)S(1)}, bf16[1920,128]{1,0:T(8,128)(2,1)S(1)}, u32[]{:S(2)}, u32[]{:S(2)}) collective-permute-start(bf16[1920,128]{1,0:T(8,128)(2,1)S(1)} %collective-permute-done.4.p1.a1), channel_id=1, source_target_pairs={{0,252},{4,0},{8,4},{12,8},{16,12},{20,16},{24,20},{28,24},{32,28}... | collective-permute-start | bytes 1474568 | tf_op jit(solution)/shard_map/ppermute | solution.py:24
  33.1 0.1 pad_add_fusion.place_ref
  33.1 0.0 copy-start.4
  33.1 5.9 %collective-permute-done.3.b2 = bf16[1920,128]{1,0:T(8,128)(2,1)S(1)} collective-permute-done((bf16[1920,128]{1,0:T(8,128)(2,1)}, bf16[1920,128]{1,0:T(8,128)(2,1)S(1)}, u32[]{:S(2)}, u32[]{:S(2)}) %collective-permute-start.3) | collective-permute-done | bytes 491552 | tf_op jit(solution)/shard_map/ppermute | solution.py:24
  39.1 0.0 collective-permute-done.2.b1
  39.1 0.0 collective-permute-start.9
  39.1 7.2 %collective-permute-start.8 = (bf16[2304,128]{1,0:T(8,128)(2,1)}, bf16[2304,128]{1,0:T(8,128)(2,1)S(1)}, u32[]{:S(2)}, u32[]{:S(2)}) collective-permute-start(bf16[2304,128]{1,0:T(8,128)(2,1)} %collective-permute-done.2.b1), channel_id=1, source_target_pairs={{0,252},{4,0},{8,4},{12,8},{16,12},{20,16},{24,20},{28,24},{32,28}... | collective-permute-start | bytes 1769480 | tf_op jit(solution)/shard_map/ppermute | solution.py:24
  46.2 1.2 %copy.5.couplings_ref = f32[4,3,3,3,1280]{4,3,2,1,0:T(4,128)S(1)} copy(f32[4,3,3,3,1280]{4,0,3,2,1:T(4,128)} %param.5) | data formatting | bytes 1105920 | tf_op jit(solution)/shard_map/optimization_barrier | solution.py:265
  47.5 0.0 copy-done.3
  47.5 0.0 copy-start.1
  47.5 9.0 %shard_map.47.t_ref = bf16[10,3,768,384]{3,2,1,0:T(8,128)(2,1)S(1)} custom-call(s32[2]{0:T(128)S(1)} %pad_add_fusion.place_ref, f32[4,3,3,3,1280]{4,3,2,1,0:T(4,128)S(1)} %copy.5.couplings_ref, s32[4,1280]{1,0:T(4,128)S(1)} %copy-done.3), custom_call_target="tpu_custom_call" | custom-call | flops 4000000000 | bytes 20000000 | tf_op jit(solution)/shard_map/pallas_call | solution.py:72
  56.6 0.0 copy-start
  56.6 0.0 collective-permute-done.7.p4.a3
  56.6 0.0 collective-permute-done.5.far_ref.p0.far_a.a0
  56.6 0.0 copy-done.1
  56.6 2.6 %shard_map.48.before_ref = f32[384,640]{1,0:T(8,128)S(1)} custom-call(bf16[10,3,768,384]{3,2,1,0:T(8,128)(2,1)S(1)} %shard_map.47.t_ref, bf16[1920,128]{1,0:T(8,128)(2,1)S(1)} %collective-permute-done.5.far_ref.p0.far_a.a0, bf16[1920,128]{1,0:T(8,128)(2,1)S(1)} %collective-permute-done.5.far_ref.p0.far_a.a0, ...), custom_call_target="tpu_custom_call" | custom-call | flops 3000000000 | bytes 9000000 | tf_op jit(solution)/shard_map/pallas_call | solution.py:168
  59.3 3.4 %copy-done = bf16[10,3,768,384]{3,2,1,0:T(8,128)(2,1)} copy-done((bf16[10,3,768,384]{3,2,1,0:T(8,128)(2,1)}, bf16[10,3,768,384]{3,2,1,0:T(8,128)(2,1)S(1)}, u32[]{:S(2)}) %copy-start) | copy-done | bytes 17694744
  62.7 0.0 collective-permute-done.9.b3
  62.7 0.0 collective-permute-done.8.far_b.b0
  62.7 0.0 copy-done.4
  62.7 9.8 %shard_map.49 = (bf16[96,640]{1,0:T(8,128)(2,1)S(1)}, bf16[96,640]{1,0:T(8,128)(2,1)S(1)}, bf16[96,640]{1,0:T(8,128)(2,1)S(1)}, bf16[96,640]{1,0:T(8,128)(2,1)S(1)}) custom-call(s32[2]{0:T(128)S(1)} %pad_add_fusion.place_ref, bf16[10,3,768,384]{3,2,1,0:T(8,128)(2,1)} %copy-done, f32[384,640]{1,0:T(8,128)S(1)} %shard_map.48.before_ref, ...), custom_call_target="tpu_custom_call" | custom-call | flops 7000000000 | bytes 21000000 | tf_op jit(solution)/shard_map/pallas_call | solution.py:183
  72.5 0.0 copy-start.2
  72.5 0.6 copy-done.2
  73.1 2.8 %collective-permute-start.10 = (bf16[96,640]{1,0:T(8,128)(2,1)S(1)}, bf16[96,640]{1,0:T(8,128)(2,1)S(1)}, u32[]{:S(2)}, u32[]{:S(2)}) collective-permute-start(bf16[96,640]{1,0:T(8,128)(2,1)S(1)} %get-tuple-element.29), channel_id=1, source_target_pairs={{0,1},{1,0},{2,3},{3,2},{4,5},{5,4},{6,7},{7,6},{8,9},{9,8},{10,11... | collective-permute-start | bytes 368648 | tf_op jit(solution)/shard_map/ppermute | solution.py:238
  75.9 0.3 collective-permute-start.11
  76.3 1.3 %collective-permute-start.12 = (bf16[96,640]{1,0:T(8,128)(2,1)S(1)}, bf16[96,640]{1,0:T(8,128)(2,1)S(1)}, u32[]{:S(2)}, u32[]{:S(2)}) collective-permute-start(bf16[96,640]{1,0:T(8,128)(2,1)S(1)} %get-tuple-element.31), channel_id=1, source_target_pairs={{0,3},{1,2},{2,1},{3,0},{4,7},{5,6},{6,5},{7,4},{8,11},{9,10},{10,... | collective-permute-start | bytes 368648 | tf_op jit(solution)/shard_map/ppermute | solution.py:238
  77.6 0.0 collective-permute-done.10.s1
  77.6 3.3 %collective-permute-done.11.s2 = bf16[96,640]{1,0:T(8,128)(2,1)S(1)} collective-permute-done((bf16[96,640]{1,0:T(8,128)(2,1)S(1)}, bf16[96,640]{1,0:T(8,128)(2,1)S(1)}, u32[]{:S(2)}, u32[]{:S(2)}) %collective-permute-start.11) | collective-permute-done | bytes 122912 | tf_op jit(solution)/shard_map/ppermute | solution.py:238
  80.9 2.7 %collective-permute-done.12.s3 = bf16[96,640]{1,0:T(8,128)(2,1)S(1)} collective-permute-done((bf16[96,640]{1,0:T(8,128)(2,1)S(1)}, bf16[96,640]{1,0:T(8,128)(2,1)S(1)}, u32[]{:S(2)}, u32[]{:S(2)}) %collective-permute-start.12) | collective-permute-done | bytes 122912 | tf_op jit(solution)/shard_map/ppermute | solution.py:238
  83.6 0.0 copy-done.5
  83.6 0.0 copy-done.6
  83.6 0.6 copy-done.7
  84.3 1.9 %shard_map.50 = (f32[1,128]{1,0:T(1,128)}, f32[1,128]{1,0:T(1,128)}, f32[1,128]{1,0:T(1,128)}, f32[1,128]{1,0:T(1,128)}, f32[1,128]{1,0:T(1,128)}) custom-call(s32[2]{0:T(128)} %copy-done.4, bf16[96,640]{1,0:T(8,128)(2,1)} %copy-done.2, bf16[96,640]{1,0:T(8,128)(2,1)} %copy-done.5, bf16[96,640]{1,0:T(8,128)(2,1)} %copy-done.6, bf16[96,640]{1,0:T(8,128)(2,1)} %copy-done.7, ...), custom_call_target="tpu_custom_call" | custom-call | tf_op jit(solution)/shard_map/pallas_call | solution.py:275
  86.2 0.3 collective-permute-start.13
  86.5 0.3 collective-permute-start.14
  86.8 1.5 %collective-permute-start.15 = (f32[1,128]{1,0:T(1,128)}, f32[1,128]{1,0:T(1,128)S(1)}, u32[]{:S(2)}, u32[]{:S(2)}) collective-permute-start(f32[1,128]{1,0:T(1,128)} %get-tuple-element.36), channel_id=1, source_target_pairs={{0,3},{1,2},{2,1},{3,0},{4,7},{5,6},{6,5},{7,4},{8,11},{9,10},{10,... | collective-permute-start | bytes 1544 | tf_op jit(solution)/shard_map/ppermute | solution.py:238
  88.3 0.0 collective-permute-done.13
  88.3 0.6 collective-permute-done.14
  88.9 1.0 collective-permute-done.15
  90.0 0.7 add_add_fusion
  90.7 5.1 %collective-permute-start.16 = (f32[1,128]{1,0:T(1,128)S(1)}, f32[1,128]{1,0:T(1,128)S(1)}, u32[]{:S(2)}, u32[]{:S(2)}) collective-permute-start(f32[1,128]{1,0:T(1,128)S(1)} %add_add_fusion), channel_id=1, source_target_pairs={{0,4},{1,253},{2,10},{3,251},{4,8},{5,1},{6,14},{7,255},{8,12},{9,... | collective-permute-start | bytes 1544 | tf_op jit(solution)/shard_map/ppermute | solution.py:286
  95.8 0.7 collective-permute-done.16
  96.5 0.7 add.28
  97.1 5.7 %collective-permute-start.19 = (f32[1,128]{1,0:T(1,128)S(1)}, f32[1,128]{1,0:T(1,128)S(1)}, u32[]{:S(2)}, u32[]{:S(2)}) collective-permute-start(f32[1,128]{1,0:T(1,128)S(1)} %add.28), channel_id=1, source_target_pairs={{0,3},{1,2},{2,1},{3,0},{4,7},{5,6},{6,5},{7,4},{8,11},{9,10},{10,... | collective-permute-start | bytes 1544 | tf_op jit(solution)/shard_map/ppermute | solution.py:238
  102.9 0.0 collective-permute-start.18
  102.9 0.4 collective-permute-start.17
  103.3 0.8 collective-permute-done.19
  104.1 1.2 %collective-permute-done.18 = f32[1,128]{1,0:T(1,128)S(1)} collective-permute-done((f32[1,128]{1,0:T(1,128)S(1)}, f32[1,128]{1,0:T(1,128)S(1)}, u32[]{:S(2)}, u32[]{:S(2)}) %collective-permute-start.18) | collective-permute-done | bytes 544 | tf_op jit(solution)/shard_map/ppermute | solution.py:238
  105.2 0.0 collective-permute-done.17
  105.2 1.3 %divide_multiply_fusion = f32[128]{0:T(128)} fusion(f32[1,128]{1,0:T(1,128)S(1)} %collective-permute-done.18, f32[1,128]{1,0:T(1,128)S(1)} %collective-permute-done.19, f32[1,128]{1,0:T(1,128)S(1)} %add.28, f32[1,128]{1,0:T(1,128)S(1)} %collective-permute-done.17, f32[8192]{0:T(1024)} %param.7, s32[]{:T(128)S(6)} %select_n.3), kind=kLoop, calls=%fused_computation.2 | loop fusion | flops 896 | bytes 3076 | tf_op jit(solution)/shard_map/mul | solution.py:290
  (3 shorter events, 0.0 us)
Async XLA Ops:
  2.2 12.8 %collective-permute-start = (bf16[192,128]{1,0:T(8,128)(2,1)}, bf16[192,128]{1,0:T(8,128)(2,1)S(1)}, u32[]{:S(2)}, u32[]{:S(2)}) collective-permute-start(bf16[192,128]{1,0:T(8,128)(2,1)} %get-tuple-element.22), channel_id=1, source_target_pairs={{0,1},{1,2},{2,3},{3,0},{4,5},{5,6},{6,7},{7,4},{8,9},{9,10},{10,1... | collective-permute-start | bytes 147464 | tf_op jit(solution)/shard_map/ppermute | solution.py:24
  4.8 10.2 %collective-permute-start.1 = (bf16[192,128]{1,0:T(8,128)(2,1)}, bf16[192,128]{1,0:T(8,128)(2,1)S(1)}, u32[]{:S(2)}, u32[]{:S(2)}) collective-permute-start(bf16[192,128]{1,0:T(8,128)(2,1)} %get-tuple-element.23), channel_id=1, source_target_pairs={{0,3},{1,0},{2,1},{3,2},{4,7},{5,4},{6,5},{7,6},{8,11},{9,8},{10,9... | collective-permute-start | bytes 147464 | tf_op jit(solution)/shard_map/ppermute | solution.py:24
  5.5 20.4 %collective-permute-start.6 = (bf16[1920,128]{1,0:T(8,128)(2,1)}, bf16[1920,128]{1,0:T(8,128)(2,1)S(1)}, u32[]{:S(2)}, u32[]{:S(2)}) collective-permute-start(bf16[1920,128]{1,0:T(8,128)(2,1)} %get-tuple-element.25), channel_id=1, source_target_pairs={{0,4},{4,8},{8,12},{12,16},{16,20},{20,24},{24,28},{28,32},{32,36}... | collective-permute-start | bytes 1474568 | tf_op jit(solution)/shard_map/ppermute | solution.py:24
  6.5 19.4 %collective-permute-start.4 = (bf16[1920,128]{1,0:T(8,128)(2,1)}, bf16[1920,128]{1,0:T(8,128)(2,1)S(1)}, u32[]{:S(2)}, u32[]{:S(2)}) collective-permute-start(bf16[1920,128]{1,0:T(8,128)(2,1)} %get-tuple-element.25), channel_id=1, source_target_pairs={{0,252},{4,0},{8,4},{12,8},{16,12},{20,16},{24,20},{28,24},{32,28}... | collective-permute-start | bytes 1474568 | tf_op jit(solution)/shard_map/ppermute | solution.py:24
  15.0 32.5 %copy-start.3 = (s32[4,1280]{1,0:T(4,128)S(1)}, s32[4,1280]{1,0:T(4,128)}, u32[]{:S(2)}) copy-start(s32[4,1280]{1,0:T(4,128)} %neighbours_ref.1) | copy-start | bytes 61444
  16.1 22.9 %collective-permute-start.2 = (bf16[2304,128]{1,0:T(8,128)(2,1)S(1)}, bf16[2304,128]{1,0:T(8,128)(2,1)}, u32[]{:S(2)}, u32[]{:S(2)}) collective-permute-start(bf16[2304,128]{1,0:T(8,128)(2,1)S(1)} %pad_maximum_fusion), channel_id=1, source_target_pairs={{0,252},{4,0},{8,4},{12,8},{16,12},{20,16},{24,20},{28,24},{32,28}... | collective-permute-start | bytes 1769480 | tf_op jit(solution)/shard_map/ppermute | solution.py:24
  19.9 19.1 %collective-permute-start.3 = (bf16[1920,128]{1,0:T(8,128)(2,1)}, bf16[1920,128]{1,0:T(8,128)(2,1)S(1)}, u32[]{:S(2)}, u32[]{:S(2)}) collective-permute-start(bf16[1920,128]{1,0:T(8,128)(2,1)} %get-tuple-element.21), channel_id=1, source_target_pairs={{0,4},{4,8},{8,12},{12,16},{16,20},{20,24},{24,28},{28,32},{32,36}... | collective-permute-start | bytes 1474568 | tf_op jit(solution)/shard_map/ppermute | solution.py:24
  25.9 30.7 %collective-permute-start.7 = (bf16[1920,128]{1,0:T(8,128)(2,1)S(1)}, bf16[1920,128]{1,0:T(8,128)(2,1)S(1)}, u32[]{:S(2)}, u32[]{:S(2)}) collective-permute-start(bf16[1920,128]{1,0:T(8,128)(2,1)S(1)} %collective-permute-done.6.p3.a2), channel_id=1, source_target_pairs={{0,4},{4,8},{8,12},{12,16},{16,20},{20,24},{24,28},{28,32},{32,36}... | collective-permute-start | bytes 1474568 | tf_op jit(solution)/shard_map/ppermute | solution.py:24
  25.9 30.7 %collective-permute-start.5 = (bf16[1920,128]{1,0:T(8,128)(2,1)S(1)}, bf16[1920,128]{1,0:T(8,128)(2,1)S(1)}, u32[]{:S(2)}, u32[]{:S(2)}) collective-permute-start(bf16[1920,128]{1,0:T(8,128)(2,1)S(1)} %collective-permute-done.4.p1.a1), channel_id=1, source_target_pairs={{0,252},{4,0},{8,4},{12,8},{16,12},{20,16},{24,20},{28,24},{32,28}... | collective-permute-start | bytes 1474568 | tf_op jit(solution)/shard_map/ppermute | solution.py:24
  33.1 29.5 %copy-start.4 = (s32[2]{0:T(128)}, s32[2]{0:T(128)S(1)}, u32[]{:S(2)}) copy-start(s32[2]{0:T(128)S(1)} %pad_add_fusion.place_ref) | copy-start | bytes 28
  39.1 23.6 %collective-permute-start.9 = (bf16[1920,128]{1,0:T(8,128)(2,1)S(1)}, bf16[1920,128]{1,0:T(8,128)(2,1)S(1)}, u32[]{:S(2)}, u32[]{:S(2)}) collective-permute-start(bf16[1920,128]{1,0:T(8,128)(2,1)S(1)} %collective-permute-done.3.b2), channel_id=1, source_target_pairs={{0,4},{4,8},{8,12},{12,16},{16,20},{20,24},{24,28},{28,32},{32,36}... | collective-permute-start | bytes 1474568 | tf_op jit(solution)/shard_map/ppermute | solution.py:24
  39.1 23.6 %collective-permute-start.8 = (bf16[2304,128]{1,0:T(8,128)(2,1)}, bf16[2304,128]{1,0:T(8,128)(2,1)S(1)}, u32[]{:S(2)}, u32[]{:S(2)}) collective-permute-start(bf16[2304,128]{1,0:T(8,128)(2,1)} %collective-permute-done.2.b1), channel_id=1, source_target_pairs={{0,252},{4,0},{8,4},{12,8},{16,12},{20,16},{24,20},{28,24},{32,28}... | collective-permute-start | bytes 1769480 | tf_op jit(solution)/shard_map/ppermute | solution.py:24
  47.5 9.1 %copy-start.1 = (bf16[3840,128]{1,0:T(8,128)(2,1)S(1)}, bf16[3840,128]{1,0:T(8,128)(2,1)}, u32[]{:S(2)}) copy-start(bf16[3840,128]{1,0:T(8,128)(2,1)} %own.1) | copy-start | bytes 2949124
  56.6 6.1 %copy-start = (bf16[10,3,768,384]{3,2,1,0:T(8,128)(2,1)}, bf16[10,3,768,384]{3,2,1,0:T(8,128)(2,1)S(1)}, u32[]{:S(2)}) copy-start(bf16[10,3,768,384]{3,2,1,0:T(8,128)(2,1)S(1)} %shard_map.47.t_ref) | copy-start | bytes 53084164
  72.5 0.6 copy-start.2
  73.1 4.5 %collective-permute-start.10 = (bf16[96,640]{1,0:T(8,128)(2,1)S(1)}, bf16[96,640]{1,0:T(8,128)(2,1)S(1)}, u32[]{:S(2)}, u32[]{:S(2)}) collective-permute-start(bf16[96,640]{1,0:T(8,128)(2,1)S(1)} %get-tuple-element.29), channel_id=1, source_target_pairs={{0,1},{1,0},{2,3},{3,2},{4,5},{5,4},{6,7},{7,6},{8,9},{9,8},{10,11... | collective-permute-start | bytes 368648 | tf_op jit(solution)/shard_map/ppermute | solution.py:238
  75.9 5.0 %collective-permute-start.11 = (bf16[96,640]{1,0:T(8,128)(2,1)S(1)}, bf16[96,640]{1,0:T(8,128)(2,1)S(1)}, u32[]{:S(2)}, u32[]{:S(2)}) collective-permute-start(bf16[96,640]{1,0:T(8,128)(2,1)S(1)} %get-tuple-element.30), channel_id=1, source_target_pairs={{0,2},{1,3},{2,0},{3,1},{4,6},{5,7},{6,4},{7,5},{8,10},{9,11},{10,... | collective-permute-start | bytes 368648 | tf_op jit(solution)/shard_map/ppermute | solution.py:238
  76.3 7.4 %collective-permute-start.12 = (bf16[96,640]{1,0:T(8,128)(2,1)S(1)}, bf16[96,640]{1,0:T(8,128)(2,1)S(1)}, u32[]{:S(2)}, u32[]{:S(2)}) collective-permute-start(bf16[96,640]{1,0:T(8,128)(2,1)S(1)} %get-tuple-element.31), channel_id=1, source_target_pairs={{0,3},{1,2},{2,1},{3,0},{4,7},{5,6},{6,5},{7,4},{8,11},{9,10},{10,... | collective-permute-start | bytes 368648 | tf_op jit(solution)/shard_map/ppermute | solution.py:238
  77.6 6.0 %copy-start.5 = (bf16[96,640]{1,0:T(8,128)(2,1)}, bf16[96,640]{1,0:T(8,128)(2,1)S(1)}, u32[]{:S(2)}) copy-start(bf16[96,640]{1,0:T(8,128)(2,1)S(1)} %collective-permute-done.10.s1) | copy-start | bytes 368644
  80.9 2.7 %copy-start.6 = (bf16[96,640]{1,0:T(8,128)(2,1)}, bf16[96,640]{1,0:T(8,128)(2,1)S(1)}, u32[]{:S(2)}) copy-start(bf16[96,640]{1,0:T(8,128)(2,1)S(1)} %collective-permute-done.11.s2) | copy-start | bytes 368644
  83.6 0.6 copy-start.7
  86.2 2.1 %collective-permute-start.13 = (f32[1,128]{1,0:T(1,128)}, f32[1,128]{1,0:T(1,128)S(1)}, u32[]{:S(2)}, u32[]{:S(2)}) collective-permute-start(f32[1,128]{1,0:T(1,128)} %get-tuple-element.34), channel_id=1, source_target_pairs={{0,1},{1,0},{2,3},{3,2},{4,5},{5,4},{6,7},{7,6},{8,9},{9,8},{10,11... | collective-permute-start | bytes 1544 | tf_op jit(solution)/shard_map/ppermute | solution.py:238
  86.5 2.4 %collective-permute-start.14 = (f32[1,128]{1,0:T(1,128)}, f32[1,128]{1,0:T(1,128)S(1)}, u32[]{:S(2)}, u32[]{:S(2)}) collective-permute-start(f32[1,128]{1,0:T(1,128)} %get-tuple-element.35), channel_id=1, source_target_pairs={{0,2},{1,3},{2,0},{3,1},{4,6},{5,7},{6,4},{7,5},{8,10},{9,11},{10,... | collective-permute-start | bytes 1544 | tf_op jit(solution)/shard_map/ppermute | solution.py:238
  86.8 3.2 %collective-permute-start.15 = (f32[1,128]{1,0:T(1,128)}, f32[1,128]{1,0:T(1,128)S(1)}, u32[]{:S(2)}, u32[]{:S(2)}) collective-permute-start(f32[1,128]{1,0:T(1,128)} %get-tuple-element.36), channel_id=1, source_target_pairs={{0,3},{1,2},{2,1},{3,0},{4,7},{5,6},{6,5},{7,4},{8,11},{9,10},{10,... | collective-permute-start | bytes 1544 | tf_op jit(solution)/shard_map/ppermute | solution.py:238
  90.7 5.8 %collective-permute-start.16 = (f32[1,128]{1,0:T(1,128)S(1)}, f32[1,128]{1,0:T(1,128)S(1)}, u32[]{:S(2)}, u32[]{:S(2)}) collective-permute-start(f32[1,128]{1,0:T(1,128)S(1)} %add_add_fusion), channel_id=1, source_target_pairs={{0,4},{1,253},{2,10},{3,251},{4,8},{5,1},{6,14},{7,255},{8,12},{9,... | collective-permute-start | bytes 1544 | tf_op jit(solution)/shard_map/ppermute | solution.py:286
  97.1 6.9 %collective-permute-start.19 = (f32[1,128]{1,0:T(1,128)S(1)}, f32[1,128]{1,0:T(1,128)S(1)}, u32[]{:S(2)}, u32[]{:S(2)}) collective-permute-start(f32[1,128]{1,0:T(1,128)S(1)} %add.28), channel_id=1, source_target_pairs={{0,3},{1,2},{2,1},{3,0},{4,7},{5,6},{6,5},{7,4},{8,11},{9,10},{10,... | collective-permute-start | bytes 1544 | tf_op jit(solution)/shard_map/ppermute | solution.py:238
  102.9 2.4 %collective-permute-start.18 = (f32[1,128]{1,0:T(1,128)S(1)}, f32[1,128]{1,0:T(1,128)S(1)}, u32[]{:S(2)}, u32[]{:S(2)}) collective-permute-start(f32[1,128]{1,0:T(1,128)S(1)} %add.28), channel_id=1, source_target_pairs={{0,2},{1,3},{2,0},{3,1},{4,6},{5,7},{6,4},{7,5},{8,10},{9,11},{10,... | collective-permute-start | bytes 1544 | tf_op jit(solution)/shard_map/ppermute | solution.py:238
  102.9 2.4 %collective-permute-start.17 = (f32[1,128]{1,0:T(1,128)S(1)}, f32[1,128]{1,0:T(1,128)S(1)}, u32[]{:S(2)}, u32[]{:S(2)}) collective-permute-start(f32[1,128]{1,0:T(1,128)S(1)} %add.28), channel_id=1, source_target_pairs={{0,1},{1,0},{2,3},{3,2},{4,5},{5,4},{6,7},{7,6},{8,9},{9,8},{10,11... | collective-permute-start | bytes 1544 | tf_op jit(solution)/shard_map/ppermute | solution.py:238

commit v4 on v3

--- a/solution.py
+++ b/solution.py
@@ -14,7 +14,7 @@
 BLOCK = 128
 WIN = BLOCK + 2 * HALO
 ROWS = 3 * BLOCK
-SPLIT = 5
+HEAD, TAIL = 2, 3
 SLOTS = 5
 F32, BF16 = jnp.float32, jnp.bfloat16
 
@@ -107,45 +107,47 @@
     total_ref[...] += jnp.dot(applied, jnp.concatenate(partners, axis=1), preferred_element_type=F32)
 
 
-def first_kernel(t_ref, far_ref, p0, p1, p2, p3, p4, out_ref, planes):
+def first_kernel(t_ref, far_ref, below_ref, above_ref, p0, p1, p2, p3, p4, out_ref, planes):
     g = pl.program_id(0)
+    tail, edge = TAIL * ROWS, 3 * HALO
 
     @pl.when(g == 0)
     def _():
         out_ref[...] = jnp.zeros_like(out_ref)
-        planes[...] = far_ref[...].astype(F32)
-
-    start = (g + 1) * ROWS - 3 * HALO
+        planes[0:tail, :] = far_ref[0:tail, :].astype(F32)
+        planes[tail : tail + edge, :] = above_ref[...].astype(F32)
+        planes[tail + edge : tail + 2 * edge, :] = below_ref[...].astype(F32)
+        planes[tail + 2 * edge :, :] = far_ref[tail:, :].astype(F32)
+
+    start = jnp.where(g < TAIL - 1, (g + 1) * ROWS - edge, tail + edge)
     star_step(planes, start, t_ref, [r[...] for r in (p0, p1, p2, p3, p4)], out_ref)
 
 
 def second_kernel(
-    head, place_ref, t_ref, before_ref, far_a, far_b, own, a0, a1, a2, a3, b0, b1, b2, b3, o0, o1, o2, o3, planes, total
+    place_ref, t_ref, before_ref, far_a, far_b, own, a0, a1, a2, a3, b0, b1, b2, b3, o0, o1, o2, o3, planes, total
 ):
     g = pl.program_id(0)
     steps = pl.num_programs(0)
-    edge = 3 * HALO
+    tail, head = TAIL * ROWS, HEAD * ROWS
+    rows_b = far_b.shape[0]
 
     @pl.when(g == 0)
     def _():
-        rows_a = far_a.shape[0]
-        rows_b = far_b.shape[0] - 2 * edge
-        planes[0:edge, :] = far_b[rows_b : rows_b + edge, :].astype(F32)
-        planes[edge : edge + rows_a, :] = far_a[...].astype(F32)
-        planes[edge + rows_a : edge + rows_a + rows_b, :] = far_b[0:rows_b, :].astype(F32)
-        planes[edge + rows_a + rows_b :, :] = far_b[rows_b + edge :, :].astype(F32)
+        planes[0:head, :] = far_a[tail:, :].astype(F32)
+        planes[head : head + rows_b, :] = far_b[...].astype(F32)
+        planes[head + rows_b :, :] = far_a[0:tail, :].astype(F32)
         total[...] = before_ref[...]
 
-    block = lax.rem(g + head, head + steps - 1)
+    start = (g + 1) * ROWS - 3 * HALO
     in_first = jnp.logical_or(g == 0, g == steps - 1)
 
     @pl.when(in_first)
     def _():
-        star_step(planes, block * ROWS, t_ref, [a0[...], a1[...], own[...], a2[...], a3[...]], total)
+        star_step(planes, start, t_ref, [a0[...], a1[...], own[...], a2[...], a3[...]], total)
 
     @pl.when(jnp.logical_not(in_first))
     def _():
-        star_step(planes, block * ROWS, t_ref, [b0[...], b1[...], own[...], b2[...], b3[...]], total)
+        star_step(planes, start, t_ref, [b0[...], b1[...], own[...], b2[...], b3[...]], total)
 
     @pl.when(g == steps - 1)
     def _():
@@ -156,46 +158,46 @@
                 out[a * 32 : (a + 1) * 32, :] = total[rows, :].astype(BF16)
 
 
-def star_products(place, operator, own, firsts, seconds):
+def star_products(place, operator, own, below, above, firsts, seconds):
     blocks = operator.shape[0]
     width = own.shape[1]
-    head = SPLIT - 1
     op_block = (1, 3, 3 * WIN, ROWS)
     shape = (3 * width, SLOTS * width)
     whole = lambda x: pl.BlockSpec(x.shape, lambda g: (0,) * x.ndim)
-    ahead = pl.BlockSpec((ROWS, width), lambda g: (g + 1, 0))
     cost = lambda n: pl.CostEstimate(flops=n * 10**9, bytes_accessed=n * 3 * 10**6, transcendentals=0)
+    at = lambda g: lax.rem(g + blocks - TAIL + 1, blocks)
+    in_a = pl.BlockSpec((ROWS, width), lambda g: (g + 1, 0))
     before = pl.pallas_call(
         first_kernel,
-        grid=(SPLIT - 2,),
-        in_specs=[pl.BlockSpec(op_block, lambda g: (g + 1, 0, 0, 0)), whole(firsts[0])] + [ahead] * 5,
+        grid=(TAIL,),
+        in_specs=[pl.BlockSpec(op_block, lambda g: (at(g), 0, 0, 0)), whole(firsts[0]), whole(below), whole(above)]
+        + [in_a, in_a, pl.BlockSpec((ROWS, width), lambda g: (at(g), 0)), in_a, in_a],
         out_specs=pl.BlockSpec(shape, lambda g: (0, 0)),
         out_shape=jax.ShapeDtypeStruct(shape, F32),
-        scratch_shapes=[pltpu.VMEM(firsts[0].shape, F32)],
+        scratch_shapes=[pltpu.VMEM((firsts[0].shape[0] + 6 * HALO, width), F32)],
         compiler_params=pltpu.CompilerParams(vmem_limit_bytes=24 * 2**20),
-        cost_estimate=cost(SPLIT - 2),
-    )(operator, firsts[0], firsts[0], firsts[1], own, firsts[2], firsts[3])
-    steps = blocks - (SPLIT - 2)
-    at = lambda g: lax.rem(g + head, blocks)
-    in_a = pl.BlockSpec((ROWS, width), lambda g: (jnp.where(g == steps - 1, 0, head), 0))
+        cost_estimate=cost(TAIL),
+    )(operator, firsts[0], below, above, firsts[0], firsts[1], own, firsts[2], firsts[3])
+    steps = blocks - TAIL
+    in_a = pl.BlockSpec((ROWS, width), lambda g: (jnp.where(g == steps - 1, 0, TAIL + HEAD - 1), 0))
     in_b = pl.BlockSpec((ROWS, width), lambda g: (jnp.clip(g - 1, 0, steps - 3), 0))
     out_shape = (shape[0] // 4, shape[1])
     return pl.pallas_call(
-        functools.partial(second_kernel, head),
+        second_kernel,
         grid=(steps,),
         in_specs=[
             pl.BlockSpec(memory_space=pltpu.SMEM),
-            pl.BlockSpec(op_block, lambda g: (at(g), 0, 0, 0)),
+            pl.BlockSpec(op_block, lambda g: (g + 1, 0, 0, 0)),
             pl.BlockSpec(shape, lambda g: (0, 0)),
             whole(firsts[0]),
             whole(seconds[0]),
-            pl.BlockSpec((ROWS, width), lambda g: (at(g), 0)),
+            pl.BlockSpec((ROWS, width), lambda g: (g + 1, 0)),
         ]
         + [in_a] * 4
         + [in_b] * 4,
         out_specs=[pl.BlockSpec(out_shape, lambda g: (0, 0))] * 4,
         out_shape=[jax.ShapeDtypeStruct(out_shape, BF16)] * 4,
-        scratch_shapes=[pltpu.VMEM((blocks * ROWS + 6 * HALO, width), F32), pltpu.VMEM(shape, F32)],
+        scratch_shapes=[pltpu.VMEM((blocks * ROWS, width), F32), pltpu.VMEM(shape, F32)],
         compiler_params=pltpu.CompilerParams(vmem_limit_bytes=32 * 2**20),
         cost_estimate=cost(steps),
     )(place, operator, before, firsts[0], seconds[0], own, *firsts, *seconds)
@@ -246,28 +248,29 @@
     half_width = WIDTH_MODES / (width * modes)
     place = jnp.stack([lax.axis_index("atom"), lax.axis_index("mode")]).astype(jnp.int32)
     edge = 3 * HALO
-    cut = SPLIT * ROWS
-
-    own_a, own_b, tail, front = copied_rows(
+    head, tail = HEAD * ROWS, TAIL * ROWS
+    rest = rows_dev - head - tail
+    own_a, own_b = copied_rows(
         [vectors],
-        [cut, rows_dev - cut, edge, edge],
-        [(0, 0, 0, 0, cut), (0, cut, 1, 0, rows_dev - cut), (0, rows_dev - edge, 2, 0, edge), (0, 0, 3, 0, edge)],
+        [head + tail, rest],
+        [(0, rows_dev - tail, 0, 0, tail), (0, 0, 0, tail, head), (0, head, 1, 0, rest)],
     )
-    below = shifted(tail, "atom", 1)
-    above = shifted(front, "atom", -1)
     up1a = shifted(own_a, "mode", -1)
     dn1a = shifted(own_a, "mode", 1)
-    own_b_far = jnp.concatenate([own_b, below, above], axis=0)
-    up1b = shifted(own_b_far, "mode", -1)
+    up1b = shifted(own_b, "mode", -1)
     dn1b = shifted(own_b, "mode", 1)
+    operator = build_operator(place, couplings, neighbours, atoms_dev * atom_groups)
+    up1a, dn1a, operator = lax.optimization_barrier((up1a, dn1a, operator))
     up2a = shifted(up1a, "mode", -1)
     dn2a = shifted(dn1a, "mode", 1)
-    couplings, up1b, dn1b = lax.optimization_barrier((couplings, up1b, dn1b))
-    operator = build_operator(place, couplings, neighbours, atoms_dev * atom_groups)
     up2b = shifted(up1b, "mode", -1)
     dn2b = shifted(dn1b, "mode", 1)
-
-    shares = star_products(place, operator, vectors, [up2a, up1a, dn1a, dn2a], [up2b, up1b, dn1b, dn2b])
+    below = shifted(up2a[tail - edge : tail], "atom", 1)
+    above = shifted(up2a[tail : tail + edge], "atom", -1)
+
+    shares = star_products(
+        place, operator, vectors, below, above, [up2a, up1a, dn1a, dn2a], [up2b, up1b, dn1b, dn2b]
+    )
     shares = [shares[0]] + [swapped(shares[k], k) for k in range(1, 4)]
 
     vmem = pl.BlockSpec(memory_space=pltpu.VMEM)

time: 107 us -> 104 us (0.972)
  local copies, waits for them, and re-layouts: 5.96 us -> 3.3 us
  other arithmetic: 3.78 us -> 2.62 us
    ppermute x9, starting transfers between devices: 12.8 us -> 15.5 us  [swapped(): return lax.ppermute(x, 'atom', [(i, i ^ k) for i in range(4)])]
    ppermute x1, starting transfers between devices: 5.1 us -> 3.38 us  [local(): result = stay + lax.ppermute(carried, ('mode', 'atom'), route)]
    unnamed x16 -> x17, local copies, waits for them, and re-layouts: 4.72 us -> 3.29 us
    optimization_barrier x1 -> x0, local copies, waits for them, and re-layouts: 1.24 us -> none  [local(): couplings, up1b, dn1b = lax.optimization_barrier((couplings, up1b, dn1b))]
    concatenate x1 -> x0, other arithmetic: 1.08 us -> none  [local(): own_b_far = jnp.concatenate([own_b, below, above], axis=0)]
  transfers between devices with their start and end apart: 20 -> 20, of which waited for: 9 -> 11; matrix products, arithmetic and copies ran while one was open for 2% -> 1% of each run, Pallas kernels for 11% -> 11%
where the time goes in v4:
time: 104 us; the launch traced here: 103 us
  starting transfers between devices  49.3 us (47%)
  Pallas kernels  25.7 us (25%)
  waiting for transfers between devices  22.2 us (21%)
  local copies, waits for them, and re-layouts  3.3 us (3%)
  other arithmetic  2.62 us (3%)
    ppermute x10, starting transfers between devices, shifted(): lax.ppermute(x, axis, [(i, (i + distance) % count) for i in range(count)])  30.5 us
    ppermute x9, starting transfers between devices, swapped(): return lax.ppermute(x, 'atom', [(i, i ^ k) for i in range(4)])  15.5 us
    ppermute x10, waiting for transfers between devices, shifted(): lax.ppermute(x, axis, [(i, (i + distance) % count) for i in range(count)])  12 us
    pallas_call x1, Pallas kernels, star_products(): pl.pallas_call(second_kernel, grid=(steps,), in_specs=[pl.BlockSpec(memor...  9.88 us
    ppermute x9, waiting for transfers between devices, swapped(): return lax.ppermute(x, 'atom', [(i, i ^ k) for i in range(4)])  9.49 us
    pallas_call x1, Pallas kernels, build_operator(): pl.pallas_call(functools.partial(operator_kernel, total_atoms), grid=(blo...  9.02 us
    ppermute x1, starting transfers between devices, local(): result = stay + lax.ppermute(carried, ('mode', 'atom'), route)  3.38 us
    unnamed x17, local copies, waits for them, and re-layouts  3.29 us
  transfers between devices with their start and end apart: 20, of which 11 were waited for; matrix products, arithmetic and copies ran while one was open for 1% of the time, Pallas kernels for 11%

profile of v4, /device:TPU:1, one launch (start us, length us, event | category | flops | bytes accessed | tf_op | source)
XLA Modules:
  0.0 103.3 jit_solution(12883260116535119850)
XLA Ops:
  0.0 0.0 copy-start.1
  0.0 2.3 %shard_map.46 = (bf16[1920,128]{1,0:T(8,128)(2,1)}, bf16[1920,128]{1,0:T(8,128)(2,1)}) custom-call(bf16[3840,128]{1,0:T(8,128)(2,1)} %own.1), custom_call_target="tpu_custom_call" | custom-call | tf_op jit(solution)/shard_map/pallas_call | solution.py:96
  2.3 2.5 %collective-permute-start.1 = (bf16[1920,128]{1,0:T(8,128)(2,1)}, bf16[1920,128]{1,0:T(8,128)(2,1)S(1)}, u32[]{:S(2)}, u32[]{:S(2)}) collective-permute-start(bf16[1920,128]{1,0:T(8,128)(2,1)} %get-tuple-element.19), channel_id=1, source_target_pairs={{0,4},{4,8},{8,12},{12,16},{16,20},{20,24},{24,28},{28,32},{32,36}... | collective-permute-start | bytes 1474568 | tf_op jit(solution)/shard_map/ppermute | solution.py:24
  4.7 8.9 %collective-permute-start = (bf16[1920,128]{1,0:T(8,128)(2,1)}, bf16[1920,128]{1,0:T(8,128)(2,1)S(1)}, u32[]{:S(2)}, u32[]{:S(2)}) collective-permute-start(bf16[1920,128]{1,0:T(8,128)(2,1)} %get-tuple-element.19), channel_id=1, source_target_pairs={{0,252},{4,0},{8,4},{12,8},{16,12},{20,16},{24,20},{28,24},{32,28}... | collective-permute-start | bytes 1474568 | tf_op jit(solution)/shard_map/ppermute | solution.py:24
  13.6 0.0 collective-permute-start.8
  13.6 7.2 %collective-permute-start.6 = (bf16[1920,128]{1,0:T(8,128)(2,1)}, bf16[1920,128]{1,0:T(8,128)(2,1)}, u32[]{:S(2)}, u32[]{:S(2)}) collective-permute-start(bf16[1920,128]{1,0:T(8,128)(2,1)} %get-tuple-element.23), channel_id=1, source_target_pairs={{0,252},{4,0},{8,4},{12,8},{16,12},{20,16},{24,20},{28,24},{32,28}... | collective-permute-start | bytes 1474568 | tf_op jit(solution)/shard_map/ppermute | solution.py:24
  20.8 1.2 %copy.5.couplings_ref = f32[4,3,3,3,1280]{4,3,2,1,0:T(4,128)S(1)} copy(f32[4,3,3,3,1280]{4,0,3,2,1:T(4,128)} %param.5) | data formatting | bytes 1105920 | tf_op args[1]
  22.0 0.1 pad_add_fusion.place_ref
  22.1 0.0 copy-start.3
  22.1 0.7 copy-done.3
  22.8 9.0 %shard_map.47.t_ref = bf16[10,3,768,384]{3,2,1,0:T(8,128)(2,1)S(1)} custom-call(s32[2]{0:T(128)S(1)} %pad_add_fusion.place_ref, f32[4,3,3,3,1280]{4,3,2,1,0:T(4,128)S(1)} %copy.5.couplings_ref, s32[4,1280]{1,0:T(4,128)S(1)} %copy-done.3), custom_call_target="tpu_custom_call" | custom-call | flops 4000000000 | bytes 20000000 | tf_op jit(solution)/shard_map/pallas_call | solution.py:72
  31.9 0.0 copy-start
  31.9 0.0 collective-permute-done.1.p3.a2
  31.9 0.0 collective-permute-done.p1.a1
  31.9 0.1 collective-permute-start.2
  32.0 1.5 %collective-permute-start.5 = (bf16[1920,128]{1,0:T(8,128)(2,1)S(1)}, bf16[1920,128]{1,0:T(8,128)(2,1)S(1)}, u32[]{:S(2)}, u32[]{:S(2)}) collective-permute-start(bf16[1920,128]{1,0:T(8,128)(2,1)S(1)} %collective-permute-done.1.p3.a2), channel_id=1, source_target_pairs={{0,4},{4,8},{8,12},{12,16},{16,20},{20,24},{24,28},{28,32},{32,36}... | collective-permute-start | bytes 1474568 | tf_op jit(solution)/shard_map/ppermute | solution.py:24
  33.4 1.9 %collective-permute-done.8.b2 = bf16[1920,128]{1,0:T(8,128)(2,1)} collective-permute-done((bf16[1920,128]{1,0:T(8,128)(2,1)}, bf16[1920,128]{1,0:T(8,128)(2,1)}, u32[]{:S(2)}, u32[]{:S(2)}) %collective-permute-start.8) | collective-permute-done | bytes 491552 | tf_op jit(solution)/shard_map/ppermute | solution.py:24
  35.4 0.0 collective-permute-start.9
  35.4 0.0 collective-permute-done.6.b1
  35.4 7.2 %collective-permute-start.7 = (bf16[1920,128]{1,0:T(8,128)(2,1)}, bf16[1920,128]{1,0:T(8,128)(2,1)S(1)}, u32[]{:S(2)}, u32[]{:S(2)}) collective-permute-start(bf16[1920,128]{1,0:T(8,128)(2,1)} %collective-permute-done.6.b1), channel_id=1, source_target_pairs={{0,252},{4,0},{8,4},{12,8},{16,12},{20,16},{24,20},{28,24},{32,28}... | collective-permute-start | bytes 1474568 | tf_op jit(solution)/shard_map/ppermute | solution.py:24
  42.6 2.2 %collective-permute-done.2.far_ref.p0.far_a.a0 = bf16[1920,128]{1,0:T(8,128)(2,1)S(1)} collective-permute-done((bf16[1920,128]{1,0:T(8,128)(2,1)S(1)}, bf16[1920,128]{1,0:T(8,128)(2,1)S(1)}, u32[]{:S(2)}, u32[]{:S(2)}) %collective-permute-start.2) | collective-permute-done | bytes 491552 | tf_op jit(solution)/shard_map/ppermute | solution.py:24
  44.8 3.0 %collective-permute-start.4 = (bf16[192,128]{1,0:T(8,128)(2,1)S(1)}, bf16[192,128]{1,0:T(8,128)(2,1)S(1)}, u32[]{:S(2)}, u32[]{:S(2)}) collective-permute-start(bf16[192,128]{1,0:T(8,128)(2,1)S(1)} %get-tuple-element.33), channel_id=1, source_target_pairs={{0,3},{1,0},{2,1},{3,2},{4,7},{5,4},{6,5},{7,6},{8,11},{9,8},{10,9... | collective-permute-start | bytes 147464 | tf_op jit(solution)/shard_map/ppermute | solution.py:24
  47.7 0.3 collective-permute-start.3
  48.0 0.0 collective-permute-done.5.p4.a3
  48.0 2.0 %collective-permute-done.4.above_ref = bf16[192,128]{1,0:T(8,128)(2,1)S(1)} collective-permute-done((bf16[192,128]{1,0:T(8,128)(2,1)S(1)}, bf16[192,128]{1,0:T(8,128)(2,1)S(1)}, u32[]{:S(2)}, u32[]{:S(2)}) %collective-permute-start.4) | collective-permute-done | bytes 49184 | tf_op jit(solution)/shard_map/ppermute | solution.py:24
  50.0 0.0 collective-permute-done.3.below_ref
  50.0 0.0 copy-done.1
  50.0 2.6 %shard_map.48.before_ref = f32[384,640]{1,0:T(8,128)S(1)} custom-call(bf16[10,3,768,384]{3,2,1,0:T(8,128)(2,1)S(1)} %shard_map.47.t_ref, bf16[1920,128]{1,0:T(8,128)(2,1)S(1)} %collective-permute-done.2.far_ref.p0.far_a.a0, bf16[192,128]{1,0:T(8,128)(2,1)S(1)} %collective-permute-done.3.below_ref, bf16[192,128]{1,0:T(8,128)(2,1)S(1)} %collective-permute-done.4.above_ref, ...), custom_call_target="tpu_custom_call" | custom-call | flops 3000000000 | bytes 9000000 | tf_op jit(solution)/shard_map/pallas_call | solution.py:170
  52.7 5.9 %collective-permute-done.9.b3 = bf16[1920,128]{1,0:T(8,128)(2,1)S(1)} collective-permute-done((bf16[1920,128]{1,0:T(8,128)(2,1)}, bf16[1920,128]{1,0:T(8,128)(2,1)S(1)}, u32[]{:S(2)}, u32[]{:S(2)}) %collective-permute-start.9) | collective-permute-done | bytes 491552 | tf_op jit(solution)/shard_map/ppermute | solution.py:24
  58.6 0.0 collective-permute-done.7.far_b.b0
  58.6 0.0 copy-done.4
  58.6 0.0 copy-done
  58.6 9.9 %shard_map.49 = (bf16[96,640]{1,0:T(8,128)(2,1)S(1)}, bf16[96,640]{1,0:T(8,128)(2,1)S(1)}, bf16[96,640]{1,0:T(8,128)(2,1)S(1)}, bf16[96,640]{1,0:T(8,128)(2,1)S(1)}) custom-call(s32[2]{0:T(128)S(1)} %pad_add_fusion.place_ref, bf16[10,3,768,384]{3,2,1,0:T(8,128)(2,1)} %copy-done, f32[384,640]{1,0:T(8,128)S(1)} %shard_map.48.before_ref, ...), custom_call_target="tpu_custom_call" | custom-call | flops 7000000000 | bytes 21000000 | tf_op jit(solution)/shard_map/pallas_call | solution.py:185
  68.5 0.0 copy-start.2
  68.5 0.6 copy-done.2
  69.1 3.5 %collective-permute-start.10 = (bf16[96,640]{1,0:T(8,128)(2,1)S(1)}, bf16[96,640]{1,0:T(8,128)(2,1)S(1)}, u32[]{:S(2)}, u32[]{:S(2)}) collective-permute-start(bf16[96,640]{1,0:T(8,128)(2,1)S(1)} %get-tuple-element.25), channel_id=1, source_target_pairs={{0,1},{1,0},{2,3},{3,2},{4,5},{5,4},{6,7},{7,6},{8,9},{9,8},{10,11... | collective-permute-start | bytes 368648 | tf_op jit(solution)/shard_map/ppermute | solution.py:240
  72.6 0.3 collective-permute-start.11
  72.9 1.3 %collective-permute-start.12 = (bf16[96,640]{1,0:T(8,128)(2,1)S(1)}, bf16[96,640]{1,0:T(8,128)(2,1)S(1)}, u32[]{:S(2)}, u32[]{:S(2)}) collective-permute-start(bf16[96,640]{1,0:T(8,128)(2,1)S(1)} %get-tuple-element.27), channel_id=1, source_target_pairs={{0,3},{1,2},{2,1},{3,0},{4,7},{5,6},{6,5},{7,4},{8,11},{9,10},{10,... | collective-permute-start | bytes 368648 | tf_op jit(solution)/shard_map/ppermute | solution.py:240
  74.3 0.0 collective-permute-done.10.s1
  74.3 0.0 copy-start.5
  74.3 3.3 %collective-permute-done.11.s2 = bf16[96,640]{1,0:T(8,128)(2,1)S(1)} collective-permute-done((bf16[96,640]{1,0:T(8,128)(2,1)S(1)}, bf16[96,640]{1,0:T(8,128)(2,1)S(1)}, u32[]{:S(2)}, u32[]{:S(2)}) %collective-permute-start.11) | collective-permute-done | bytes 122912 | tf_op jit(solution)/shard_map/ppermute | solution.py:240
  77.6 0.0 copy-start.6
  77.6 2.7 %collective-permute-done.12.s3 = bf16[96,640]{1,0:T(8,128)(2,1)S(1)} collective-permute-done((bf16[96,640]{1,0:T(8,128)(2,1)S(1)}, bf16[96,640]{1,0:T(8,128)(2,1)S(1)}, u32[]{:S(2)}, u32[]{:S(2)}) %collective-permute-start.12) | collective-permute-done | bytes 122912 | tf_op jit(solution)/shard_map/ppermute | solution.py:240
  80.3 0.0 copy-done.5
  80.3 0.0 copy-done.6
  80.3 0.7 copy-done.7
  81.0 1.9 %shard_map.50 = (f32[1,128]{1,0:T(1,128)}, f32[1,128]{1,0:T(1,128)}, f32[1,128]{1,0:T(1,128)}, f32[1,128]{1,0:T(1,128)}, f32[1,128]{1,0:T(1,128)}) custom-call(s32[2]{0:T(128)} %copy-done.4, bf16[96,640]{1,0:T(8,128)(2,1)} %copy-done.2, bf16[96,640]{1,0:T(8,128)(2,1)} %copy-done.5, bf16[96,640]{1,0:T(8,128)(2,1)} %copy-done.6, bf16[96,640]{1,0:T(8,128)(2,1)} %copy-done.7, ...), custom_call_target="tpu_custom_call" | custom-call | tf_op jit(solution)/shard_map/pallas_call | solution.py:278
  82.9 0.3 collective-permute-start.13
  83.2 0.3 collective-permute-start.14
  83.5 1.5 %collective-permute-start.15 = (f32[1,128]{1,0:T(1,128)}, f32[1,128]{1,0:T(1,128)S(1)}, u32[]{:S(2)}, u32[]{:S(2)}) collective-permute-start(f32[1,128]{1,0:T(1,128)} %get-tuple-element.32), channel_id=1, source_target_pairs={{0,3},{1,2},{2,1},{3,0},{4,7},{5,6},{6,5},{7,4},{8,11},{9,10},{10,... | collective-permute-start | bytes 1544 | tf_op jit(solution)/shard_map/ppermute | solution.py:240
  85.0 0.0 collective-permute-done.13
  85.0 0.6 collective-permute-done.14
  85.6 0.9 collective-permute-done.15
  86.5 0.7 add_add_fusion
  87.2 3.4 %collective-permute-start.16 = (f32[1,128]{1,0:T(1,128)S(1)}, f32[1,128]{1,0:T(1,128)S(1)}, u32[]{:S(2)}, u32[]{:S(2)}) collective-permute-start(f32[1,128]{1,0:T(1,128)S(1)} %add_add_fusion), channel_id=1, source_target_pairs={{0,4},{1,253},{2,10},{3,251},{4,8},{5,1},{6,14},{7,255},{8,12},{9,... | collective-permute-start | bytes 1544 | tf_op jit(solution)/shard_map/ppermute | solution.py:289
  90.6 0.7 collective-permute-done.16
  91.3 0.6 add.28
  91.9 7.7 %collective-permute-start.19 = (f32[1,128]{1,0:T(1,128)S(1)}, f32[1,128]{1,0:T(1,128)S(1)}, u32[]{:S(2)}, u32[]{:S(2)}) collective-permute-start(f32[1,128]{1,0:T(1,128)S(1)} %add.28), channel_id=1, source_target_pairs={{0,3},{1,2},{2,1},{3,0},{4,7},{5,6},{6,5},{7,4},{8,11},{9,10},{10,... | collective-permute-start | bytes 1544 | tf_op jit(solution)/shard_map/ppermute | solution.py:240
  99.6 0.0 collective-permute-start.18
  99.6 0.4 collective-permute-start.17
  100.0 0.8 collective-permute-done.19
  100.8 1.2 %collective-permute-done.18 = f32[1,128]{1,0:T(1,128)S(1)} collective-permute-done((f32[1,128]{1,0:T(1,128)S(1)}, f32[1,128]{1,0:T(1,128)S(1)}, u32[]{:S(2)}, u32[]{:S(2)}) %collective-permute-start.18) | collective-permute-done | bytes 544 | tf_op jit(solution)/shard_map/ppermute | solution.py:240
  102.0 0.0 collective-permute-done.17
  102.0 1.3 %divide_multiply_fusion = f32[128]{0:T(128)} fusion(f32[1,128]{1,0:T(1,128)S(1)} %collective-permute-done.18, f32[1,128]{1,0:T(1,128)S(1)} %collective-permute-done.19, f32[1,128]{1,0:T(1,128)S(1)} %add.28, f32[1,128]{1,0:T(1,128)S(1)} %collective-permute-done.17, f32[8192]{0:T(1024)} %param.7, s32[]{:T(128)S(6)} %select_n.3), kind=kLoop, calls=%fused_computation.1 | loop fusion | flops 896 | bytes 3076 | tf_op jit(solution)/shard_map/mul | solution.py:293
  (3 shorter events, 0.0 us)
Async XLA Ops:
  0.0 50.0 %copy-start.1 = (bf16[3840,128]{1,0:T(8,128)(2,1)S(1)}, bf16[3840,128]{1,0:T(8,128)(2,1)}, u32[]{:S(2)}) copy-start(bf16[3840,128]{1,0:T(8,128)(2,1)} %own.1) | copy-start | bytes 2949124
  2.3 29.6 %collective-permute-start.1 = (bf16[1920,128]{1,0:T(8,128)(2,1)}, bf16[1920,128]{1,0:T(8,128)(2,1)S(1)}, u32[]{:S(2)}, u32[]{:S(2)}) collective-permute-start(bf16[1920,128]{1,0:T(8,128)(2,1)} %get-tuple-element.19), channel_id=1, source_target_pairs={{0,4},{4,8},{8,12},{12,16},{16,20},{20,24},{24,28},{28,32},{32,36}... | collective-permute-start | bytes 1474568 | tf_op jit(solution)/shard_map/ppermute | solution.py:24
  4.7 27.2 %collective-permute-start = (bf16[1920,128]{1,0:T(8,128)(2,1)}, bf16[1920,128]{1,0:T(8,128)(2,1)S(1)}, u32[]{:S(2)}, u32[]{:S(2)}) collective-permute-start(bf16[1920,128]{1,0:T(8,128)(2,1)} %get-tuple-element.19), channel_id=1, source_target_pairs={{0,252},{4,0},{8,4},{12,8},{16,12},{20,16},{24,20},{28,24},{32,28}... | collective-permute-start | bytes 1474568 | tf_op jit(solution)/shard_map/ppermute | solution.py:24
  13.6 21.8 %collective-permute-start.8 = (bf16[1920,128]{1,0:T(8,128)(2,1)}, bf16[1920,128]{1,0:T(8,128)(2,1)}, u32[]{:S(2)}, u32[]{:S(2)}) collective-permute-start(bf16[1920,128]{1,0:T(8,128)(2,1)} %get-tuple-element.23), channel_id=1, source_target_pairs={{0,4},{4,8},{8,12},{12,16},{16,20},{20,24},{24,28},{28,32},{32,36}... | collective-permute-start | bytes 1474568 | tf_op jit(solution)/shard_map/ppermute | solution.py:24
  13.6 21.8 %collective-permute-start.6 = (bf16[1920,128]{1,0:T(8,128)(2,1)}, bf16[1920,128]{1,0:T(8,128)(2,1)}, u32[]{:S(2)}, u32[]{:S(2)}) collective-permute-start(bf16[1920,128]{1,0:T(8,128)(2,1)} %get-tuple-element.23), channel_id=1, source_target_pairs={{0,252},{4,0},{8,4},{12,8},{16,12},{20,16},{24,20},{28,24},{32,28}... | collective-permute-start | bytes 1474568 | tf_op jit(solution)/shard_map/ppermute | solution.py:24
  22.1 0.7 copy-start.3
  22.8 35.7 %copy-start.4 = (s32[2]{0:T(128)}, s32[2]{0:T(128)S(1)}, u32[]{:S(2)}) copy-start(s32[2]{0:T(128)S(1)} %pad_add_fusion.place_ref) | copy-start | bytes 28
  31.9 26.7 %copy-start = (bf16[10,3,768,384]{3,2,1,0:T(8,128)(2,1)}, bf16[10,3,768,384]{3,2,1,0:T(8,128)(2,1)S(1)}, u32[]{:S(2)}) copy-start(bf16[10,3,768,384]{3,2,1,0:T(8,128)(2,1)S(1)} %shard_map.47.t_ref) | copy-start | bytes 53084164
  31.9 12.9 %collective-permute-start.2 = (bf16[1920,128]{1,0:T(8,128)(2,1)S(1)}, bf16[1920,128]{1,0:T(8,128)(2,1)S(1)}, u32[]{:S(2)}, u32[]{:S(2)}) collective-permute-start(bf16[1920,128]{1,0:T(8,128)(2,1)S(1)} %collective-permute-done.p1.a1), channel_id=1, source_target_pairs={{0,252},{4,0},{8,4},{12,8},{16,12},{20,16},{24,20},{28,24},{32,28}... | collective-permute-start | bytes 1474568 | tf_op jit(solution)/shard_map/ppermute | solution.py:24
  32.0 16.0 %collective-permute-start.5 = (bf16[1920,128]{1,0:T(8,128)(2,1)S(1)}, bf16[1920,128]{1,0:T(8,128)(2,1)S(1)}, u32[]{:S(2)}, u32[]{:S(2)}) collective-permute-start(bf16[1920,128]{1,0:T(8,128)(2,1)S(1)} %collective-permute-done.1.p3.a2), channel_id=1, source_target_pairs={{0,4},{4,8},{8,12},{12,16},{16,20},{20,24},{24,28},{28,32},{32,36}... | collective-permute-start | bytes 1474568 | tf_op jit(solution)/shard_map/ppermute | solution.py:24
  35.4 23.2 %collective-permute-start.9 = (bf16[1920,128]{1,0:T(8,128)(2,1)}, bf16[1920,128]{1,0:T(8,128)(2,1)S(1)}, u32[]{:S(2)}, u32[]{:S(2)}) collective-permute-start(bf16[1920,128]{1,0:T(8,128)(2,1)} %collective-permute-done.8.b2), channel_id=1, source_target_pairs={{0,4},{4,8},{8,12},{12,16},{16,20},{20,24},{24,28},{28,32},{32,36}... | collective-permute-start | bytes 1474568 | tf_op jit(solution)/shard_map/ppermute | solution.py:24
  35.4 23.2 %collective-permute-start.7 = (bf16[1920,128]{1,0:T(8,128)(2,1)}, bf16[1920,128]{1,0:T(8,128)(2,1)S(1)}, u32[]{:S(2)}, u32[]{:S(2)}) collective-permute-start(bf16[1920,128]{1,0:T(8,128)(2,1)} %collective-permute-done.6.b1), channel_id=1, source_target_pairs={{0,252},{4,0},{8,4},{12,8},{16,12},{20,16},{24,20},{28,24},{32,28}... | collective-permute-start | bytes 1474568 | tf_op jit(solution)/shard_map/ppermute | solution.py:24
  44.8 5.2 %collective-permute-start.4 = (bf16[192,128]{1,0:T(8,128)(2,1)S(1)}, bf16[192,128]{1,0:T(8,128)(2,1)S(1)}, u32[]{:S(2)}, u32[]{:S(2)}) collective-permute-start(bf16[192,128]{1,0:T(8,128)(2,1)S(1)} %get-tuple-element.33), channel_id=1, source_target_pairs={{0,3},{1,0},{2,1},{3,2},{4,7},{5,4},{6,5},{7,6},{8,11},{9,8},{10,9... | collective-permute-start | bytes 147464 | tf_op jit(solution)/shard_map/ppermute | solution.py:24
  47.7 2.3 %collective-permute-start.3 = (bf16[192,128]{1,0:T(8,128)(2,1)S(1)}, bf16[192,128]{1,0:T(8,128)(2,1)S(1)}, u32[]{:S(2)}, u32[]{:S(2)}) collective-permute-start(bf16[192,128]{1,0:T(8,128)(2,1)S(1)} %get-tuple-element.34), channel_id=1, source_target_pairs={{0,1},{1,2},{2,3},{3,0},{4,5},{5,6},{6,7},{7,4},{8,9},{9,10},{10,1... | collective-permute-start | bytes 147464 | tf_op jit(solution)/shard_map/ppermute | solution.py:24
  68.5 0.7 copy-start.2
  69.1 5.1 %collective-permute-start.10 = (bf16[96,640]{1,0:T(8,128)(2,1)S(1)}, bf16[96,640]{1,0:T(8,128)(2,1)S(1)}, u32[]{:S(2)}, u32[]{:S(2)}) collective-permute-start(bf16[96,640]{1,0:T(8,128)(2,1)S(1)} %get-tuple-element.25), channel_id=1, source_target_pairs={{0,1},{1,0},{2,3},{3,2},{4,5},{5,4},{6,7},{7,6},{8,9},{9,8},{10,11... | collective-permute-start | bytes 368648 | tf_op jit(solution)/shard_map/ppermute | solution.py:240
  72.6 5.0 %collective-permute-start.11 = (bf16[96,640]{1,0:T(8,128)(2,1)S(1)}, bf16[96,640]{1,0:T(8,128)(2,1)S(1)}, u32[]{:S(2)}, u32[]{:S(2)}) collective-permute-start(bf16[96,640]{1,0:T(8,128)(2,1)S(1)} %get-tuple-element.26), channel_id=1, source_target_pairs={{0,2},{1,3},{2,0},{3,1},{4,6},{5,7},{6,4},{7,5},{8,10},{9,11},{10,... | collective-permute-start | bytes 368648 | tf_op jit(solution)/shard_map/ppermute | solution.py:240
  72.9 7.4 %collective-permute-start.12 = (bf16[96,640]{1,0:T(8,128)(2,1)S(1)}, bf16[96,640]{1,0:T(8,128)(2,1)S(1)}, u32[]{:S(2)}, u32[]{:S(2)}) collective-permute-start(bf16[96,640]{1,0:T(8,128)(2,1)S(1)} %get-tuple-element.27), channel_id=1, source_target_pairs={{0,3},{1,2},{2,1},{3,0},{4,7},{5,6},{6,5},{7,4},{8,11},{9,10},{10,... | collective-permute-start | bytes 368648 | tf_op jit(solution)/shard_map/ppermute | solution.py:240
  74.3 6.0 %copy-start.5 = (bf16[96,640]{1,0:T(8,128)(2,1)}, bf16[96,640]{1,0:T(8,128)(2,1)S(1)}, u32[]{:S(2)}) copy-start(bf16[96,640]{1,0:T(8,128)(2,1)S(1)} %collective-permute-done.10.s1) | copy-start | bytes 368644
  77.6 2.7 %copy-start.6 = (bf16[96,640]{1,0:T(8,128)(2,1)}, bf16[96,640]{1,0:T(8,128)(2,1)S(1)}, u32[]{:S(2)}) copy-start(bf16[96,640]{1,0:T(8,128)(2,1)S(1)} %collective-permute-done.11.s2) | copy-start | bytes 368644
  80.3 0.7 copy-start.7
  82.9 2.1 %collective-permute-start.13 = (f32[1,128]{1,0:T(1,128)}, f32[1,128]{1,0:T(1,128)S(1)}, u32[]{:S(2)}, u32[]{:S(2)}) collective-permute-start(f32[1,128]{1,0:T(1,128)} %get-tuple-element.30), channel_id=1, source_target_pairs={{0,1},{1,0},{2,3},{3,2},{4,5},{5,4},{6,7},{7,6},{8,9},{9,8},{10,11... | collective-permute-start | bytes 1544 | tf_op jit(solution)/shard_map/ppermute | solution.py:240
  83.2 2.4 %collective-permute-start.14 = (f32[1,128]{1,0:T(1,128)}, f32[1,128]{1,0:T(1,128)S(1)}, u32[]{:S(2)}, u32[]{:S(2)}) collective-permute-start(f32[1,128]{1,0:T(1,128)} %get-tuple-element.31), channel_id=1, source_target_pairs={{0,2},{1,3},{2,0},{3,1},{4,6},{5,7},{6,4},{7,5},{8,10},{9,11},{10,... | collective-permute-start | bytes 1544 | tf_op jit(solution)/shard_map/ppermute | solution.py:240
  83.5 3.0 %collective-permute-start.15 = (f32[1,128]{1,0:T(1,128)}, f32[1,128]{1,0:T(1,128)S(1)}, u32[]{:S(2)}, u32[]{:S(2)}) collective-permute-start(f32[1,128]{1,0:T(1,128)} %get-tuple-element.32), channel_id=1, source_target_pairs={{0,3},{1,2},{2,1},{3,0},{4,7},{5,6},{6,5},{7,4},{8,11},{9,10},{10,... | collective-permute-start | bytes 1544 | tf_op jit(solution)/shard_map/ppermute | solution.py:240
  87.2 4.1 %collective-permute-start.16 = (f32[1,128]{1,0:T(1,128)S(1)}, f32[1,128]{1,0:T(1,128)S(1)}, u32[]{:S(2)}, u32[]{:S(2)}) collective-permute-start(f32[1,128]{1,0:T(1,128)S(1)} %add_add_fusion), channel_id=1, source_target_pairs={{0,4},{1,253},{2,10},{3,251},{4,8},{5,1},{6,14},{7,255},{8,12},{9,... | collective-permute-start | bytes 1544 | tf_op jit(solution)/shard_map/ppermute | solution.py:289
  91.9 9.0 %collective-permute-start.19 = (f32[1,128]{1,0:T(1,128)S(1)}, f32[1,128]{1,0:T(1,128)S(1)}, u32[]{:S(2)}, u32[]{:S(2)}) collective-permute-start(f32[1,128]{1,0:T(1,128)S(1)} %add.28), channel_id=1, source_target_pairs={{0,3},{1,2},{2,1},{3,0},{4,7},{5,6},{6,5},{7,4},{8,11},{9,10},{10,... | collective-permute-start | bytes 1544 | tf_op jit(solution)/shard_map/ppermute | solution.py:240
  99.6 2.4 %collective-permute-start.18 = (f32[1,128]{1,0:T(1,128)S(1)}, f32[1,128]{1,0:T(1,128)S(1)}, u32[]{:S(2)}, u32[]{:S(2)}) collective-permute-start(f32[1,128]{1,0:T(1,128)S(1)} %add.28), channel_id=1, source_target_pairs={{0,2},{1,3},{2,0},{3,1},{4,6},{5,7},{6,4},{7,5},{8,10},{9,11},{10,... | collective-permute-start | bytes 1544 | tf_op jit(solution)/shard_map/ppermute | solution.py:240
  99.6 2.4 %collective-permute-start.17 = (f32[1,128]{1,0:T(1,128)S(1)}, f32[1,128]{1,0:T(1,128)S(1)}, u32[]{:S(2)}, u32[]{:S(2)}) collective-permute-start(f32[1,128]{1,0:T(1,128)S(1)} %add.28), channel_id=1, source_target_pairs={{0,1},{1,0},{2,3},{3,2},{4,5},{5,4},{6,7},{7,6},{8,9},{9,8},{10,11... | collective-permute-start | bytes 1544 | tf_op jit(solution)/shard_map/ppermute | solution.py:240

commit v5 on v4

v5 whole, which is shorter than its diff:
```python
import functools
import math

import jax
import jax.numpy as jnp
from jax import lax
from jax.experimental import pallas as pl
from jax.experimental.pallas import tpu as pltpu
from jax.sharding import PartitionSpec as P

HALO = 64
PARTNERS = 4
WIDTH_MODES = 320
BLOCK = 128
WIN = BLOCK + 2 * HALO
ROWS = 3 * BLOCK
HEAD, TAIL = 2, 3
SLOTS = 5
TABLE = 40
F32, BF16 = jnp.float32, jnp.bfloat16


def shifted(x, axis, distance):
    count = lax.axis_size(axis)
    return lax.ppermute(x, axis, [(i, (i + distance) % count) for i in range(count)])


def table_kernel(total_atoms, place_ref, couplings_ref, neighbours_ref, out_ref, rows_ref):
    blocks = neighbours_ref.shape[1] // BLOCK
    lane = lax.broadcasted_iota(jnp.int32, (BLOCK, ROWS), 1)
    atom = lax.broadcasted_iota(jnp.int32, (BLOCK, ROWS), 0)
    spread = jnp.zeros((blocks * TABLE, ROWS), F32)
    for p in range(3):
        for i in range(blocks):
            lanes = slice(i * BLOCK, (i + 1) * BLOCK)
            for k in range(4):
                for a in range(3):
                    at = i * TABLE + (k * 3 + a) * 3
                    rows_ref[at : at + 3, :] = couplings_ref[k, a, p, :, lanes]
            target = neighbours_ref[:, lanes] - ((place_ref[0] * blocks + i) * BLOCK - HALO)
            target = jnp.where(target < 0, target + total_atoms, target)
            target = jnp.where(target >= total_atoms, target - total_atoms, target)
            rows_ref[i * TABLE + 36 : (i + 1) * TABLE, :] = target.astype(F32)
        place = jnp.where(lane == 3 * atom + p, 1.0, 0.0).astype(BF16)
        spread += jnp.dot(rows_ref[...].astype(BF16), place, preferred_element_type=F32)
    for i in range(blocks):
        rows = spread[i * TABLE : (i + 1) * TABLE]
        out_ref[i] = rows
        for k in (0, 2):
            same = rows[36 + k : 37 + k] == rows[37 + k : 38 + k]
            twin = jnp.where(same, rows[(k + 1) * 9 : (k + 2) * 9], 0.0)
            out_ref[i, k * 9 : (k + 1) * 9, :] = rows[k * 9 : (k + 1) * 9] + twin


def operator_table(place, couplings, neighbours, total_atoms):
    blocks = neighbours.shape[1] // BLOCK
    vmem = pl.BlockSpec(memory_space=pltpu.VMEM)
    return pl.pallas_call(
        functools.partial(table_kernel, total_atoms),
        in_specs=[pl.BlockSpec(memory_space=pltpu.SMEM), vmem, vmem],
        out_shape=jax.ShapeDtypeStruct((blocks, TABLE, ROWS), F32),
        scratch_shapes=[pltpu.VMEM((blocks * TABLE, BLOCK), F32)],
        compiler_params=pltpu.CompilerParams(vmem_limit_bytes=16 * 2**20),
        cost_estimate=pl.CostEstimate(flops=2 * 10**9, bytes_accessed=3 * 10**6, transcendentals=0),
    )(place, couplings, neighbours)


TILE = 16


def tile_slots(first_row, first_lane):
    low, high = first_lane // 3 + HALO, (first_lane + 127) // 3 + HALO
    meets = lambda lo, hi: first_row <= hi and lo < first_row + TILE
    up = (0, 1) if meets(low + 2, high + HALO) else ()
    return up + ((2, 3) if meets(low - HALO, high - 2) else ())


def fill_operator(table_ref, operator_ref):
    for first_lane in range(0, ROWS, 128):
        lanes = slice(first_lane, first_lane + 128)
        wide = [jnp.broadcast_to(table_ref[0, at : at + 1, lanes], (TILE, 128)).astype(BF16) for at in range(TABLE)]
        for first_row in range(0, WIN, TILE):
            slots = tile_slots(first_row, first_lane)
            if not slots:
                continue
            row = (lax.broadcasted_iota(jnp.int32, (TILE, 128), 0).astype(F32) + float(first_row)).astype(BF16)
            masks = {k: row == wide[36 + k] for k in slots}
            for a in range(3):
                for q in range(3):
                    value = jnp.zeros((TILE, 128), BF16)
                    for k in reversed(slots):
                        value = jnp.where(masks[k], wide[(k * 3 + a) * 3 + q], value)
                    start = q * WIN + first_row
                    operator_ref[start : start + TILE, a * ROWS + first_lane : a * ROWS + first_lane + 128] = value


def copy_kernel(moves, *refs):
    for src, s0, dst, d0, n in moves:
        refs[dst][d0 : d0 + n, :] = refs[src][s0 : s0 + n, :]


def copied_rows(inputs, lengths, moves):
    width = inputs[0].shape[1]
    moves = [(i, s, len(inputs) + o, d, n) for i, s, o, d, n in moves]
    return pl.pallas_call(
        functools.partial(copy_kernel, moves),
        out_shape=[jax.ShapeDtypeStruct((n, width), inputs[0].dtype) for n in lengths],
        compiler_params=pltpu.CompilerParams(vmem_limit_bytes=8 * 2**20),
    )(*inputs)


def star_step(planes_ref, start, table_ref, operator_ref, partners, total_ref):
    fill_operator(table_ref, operator_ref)
    window = [planes_ref[pl.ds(start + q, WIN, stride=3), :].astype(BF16) for q in range(3)]
    window = jnp.concatenate(window, axis=0).T
    applied = jnp.dot(window, operator_ref[...], preferred_element_type=F32).astype(BF16)
    applied = jnp.concatenate([applied[:, a * ROWS : (a + 1) * ROWS] for a in range(3)], axis=0)
    total_ref[...] += jnp.dot(applied, jnp.concatenate(partners, axis=1), preferred_element_type=F32)


def first_kernel(t_ref, far_ref, below_ref, above_ref, p0, p1, p2, p3, p4, out_ref, planes, dense):
    g = pl.program_id(0)
    tail, edge = TAIL * ROWS, 3 * HALO

    @pl.when(g == 0)
    def _():
        out_ref[...] = jnp.zeros_like(out_ref)
        dense[...] = jnp.zeros_like(dense)
        planes[0:tail, :] = far_ref[0:tail, :].astype(F32)
        planes[tail : tail + edge, :] = above_ref[...].astype(F32)
        planes[tail + edge : tail + 2 * edge, :] = below_ref[...].astype(F32)
        planes[tail + 2 * edge :, :] = far_ref[tail:, :].astype(F32)

    start = jnp.where(g < TAIL - 1, (g + 1) * ROWS - edge, tail + edge)
    star_step(planes, start, t_ref, dense, [r[...] for r in (p0, p1, p2, p3, p4)], out_ref)


def second_kernel(
    place_ref, t_ref, before_ref, far_a, far_b, own, a0, a1, a2, a3, b0, b1, b2, b3, o0, o1, o2, o3, planes, total, dense
):
    g = pl.program_id(0)
    steps = pl.num_programs(0)
    tail, head = TAIL * ROWS, HEAD * ROWS
    rows_b = far_b.shape[0]

    @pl.when(g == 0)
    def _():
        planes[0:head, :] = far_a[tail:, :].astype(F32)
        planes[head : head + rows_b, :] = far_b[...].astype(F32)
        planes[head + rows_b :, :] = far_a[0:tail, :].astype(F32)
        total[...] = before_ref[...]
        dense[...] = jnp.zeros_like(dense)

    start = (g + 1) * ROWS - 3 * HALO
    in_first = jnp.logical_or(g == 0, g == steps - 1)

    @pl.when(in_first)
    def _():
        star_step(planes, start, t_ref, dense, [a0[...], a1[...], own[...], a2[...], a3[...]], total)

    @pl.when(jnp.logical_not(in_first))
    def _():
        star_step(planes, start, t_ref, dense, [b0[...], b1[...], own[...], b2[...], b3[...]], total)

    @pl.when(g == steps - 1)
    def _():
        for k, out in enumerate((o0, o1, o2, o3)):
            share = jnp.bitwise_xor(place_ref[0], k)
            for a in range(3):
                rows = pl.ds(pl.multiple_of(a * 128 + share * 32, 32), 32)
                out[a * 32 : (a + 1) * 32, :] = total[rows, :].astype(BF16)


def star_products(place, operator, own, below, above, firsts, seconds):
    blocks = operator.shape[0]
    width = own.shape[1]
    op_block = (1, TABLE, ROWS)
    dense = pltpu.VMEM((3 * WIN, 3 * ROWS), BF16)
    shape = (3 * width, SLOTS * width)
    whole = lambda x: pl.BlockSpec(x.shape, lambda g: (0,) * x.ndim)
    cost = lambda n: pl.CostEstimate(flops=n * 10**9, bytes_accessed=n * 3 * 10**6, transcendentals=0)
    at = lambda g: lax.rem(g + blocks - TAIL + 1, blocks)
    in_a = pl.BlockSpec((ROWS, width), lambda g: (g + 1, 0))
    before = pl.pallas_call(
        first_kernel,
        grid=(TAIL,),
        in_specs=[pl.BlockSpec(op_block, lambda g: (at(g), 0, 0)), whole(firsts[0]), whole(below), whole(above)]
        + [in_a, in_a, pl.BlockSpec((ROWS, width), lambda g: (at(g), 0)), in_a, in_a],
        out_specs=pl.BlockSpec(shape, lambda g: (0, 0)),
        out_shape=jax.ShapeDtypeStruct(shape, F32),
        scratch_shapes=[pltpu.VMEM((firsts[0].shape[0] + 6 * HALO, width), F32), dense],
        compiler_params=pltpu.CompilerParams(vmem_limit_bytes=24 * 2**20),
        cost_estimate=cost(TAIL),
    )(operator, firsts[0], below, above, firsts[0], firsts[1], own, firsts[2], firsts[3])
    steps = blocks - TAIL
    in_a = pl.BlockSpec((ROWS, width), lambda g: (jnp.where(g == steps - 1, 0, TAIL + HEAD - 1), 0))
    in_b = pl.BlockSpec((ROWS, width), lambda g: (jnp.clip(g - 1, 0, steps - 3), 0))
    out_shape = (shape[0] // 4, shape[1])
    return pl.pallas_call(
        second_kernel,
        grid=(steps,),
        in_specs=[
            pl.BlockSpec(memory_space=pltpu.SMEM),
            pl.BlockSpec(op_block, lambda g: (g + 1, 0, 0)),
            pl.BlockSpec(shape, lambda g: (0, 0)),
            whole(firsts[0]),
            whole(seconds[0]),
            pl.BlockSpec((ROWS, width), lambda g: (g + 1, 0)),
        ]
        + [in_a] * 4
        + [in_b] * 4,
        out_specs=[pl.BlockSpec(out_shape, lambda g: (0, 0))] * 4,
        out_shape=[jax.ShapeDtypeStruct(out_shape, BF16)] * 4,
        scratch_shapes=[pltpu.VMEM((blocks * ROWS, width), F32), pltpu.VMEM(shape, F32), dense],
        compiler_params=pltpu.CompilerParams(vmem_limit_bytes=32 * 2**20),
        cost_estimate=cost(steps),
    )(place, operator, before, firsts[0], seconds[0], own, *firsts, *seconds)


RETURNS = (1, -1, 2, -2)


def weigh_kernel(half_width, place_ref, s0, s1, s2, s3, freq_ref, o0, o1, o2, o3, rows_ref):
    atom, mode = place_ref[0], place_ref[1]
    modes = freq_ref.shape[0]
    summed = s0[...].astype(F32) + s1[...].astype(F32) + s2[...].astype(F32) + s3[...].astype(F32)
    squares = summed[0:32] * summed[0:32] + summed[32:64] * summed[32:64] + summed[64:96] * summed[64:96]
    row = lax.broadcasted_iota(jnp.int32, (32, 128), 0) + 32 * atom
    lane = lax.broadcasted_iota(jnp.int32, (32, 128), 1)
    wrapped = lambda b: jnp.where(b >= modes, b - modes, jnp.where(b < 0, b + modes, b))
    top = wrapped(mode + 2)
    top_freq = freq_ref[pl.ds(top, 1), :]
    centre = jnp.sum(jnp.where(row == lane, top_freq, 0.0), axis=1, keepdims=True)
    own = jnp.zeros((32, 128), F32)
    for slot in range(SLOTS):
        block = wrapped(mode + 2 - slot)
        offset = centre - freq_ref[pl.ds(block, 1), :]
        lorentz = (half_width / math.pi) / (offset * offset + half_width * half_width)
        term = jnp.where(block <= top, squares[:, slot * 128 : (slot + 1) * 128] * lorentz, 0.0)
        own += term
        if slot == 2:
            rows_ref[4:5, :] = jnp.sum(term, axis=0, keepdims=True)
        elif slot > 0:
            at = RETURNS.index(2 - slot)
            rows_ref[at : at + 1, :] = jnp.sum(term, axis=0, keepdims=True)
    own = jnp.sum(own, axis=1, keepdims=True)
    at = RETURNS.index(2)
    rows_ref[at : at + 1, :] = jnp.sum(jnp.where(row == lane, own, 0.0), axis=0, keepdims=True)
    for k, out in enumerate((o0, o1, o2, o3)):
        out[0:1, :] = rows_ref[pl.ds(jnp.bitwise_xor(atom, k), 1), :]
        out[1:2, :] = rows_ref[4:5, :]


def swapped(x, k):
    return lax.ppermute(x, "atom", [(i, i ^ k) for i in range(4)])


def local(vectors, couplings, neighbours, frequency):
    rows_dev, width = vectors.shape
    atoms_dev = rows_dev // 3
    atom_groups = lax.axis_size("atom")
    modes = lax.axis_size("mode")
    half_width = WIDTH_MODES / (width * modes)
    place = jnp.stack([lax.axis_index("atom"), lax.axis_index("mode")]).astype(jnp.int32)
    edge = 3 * HALO
    head, tail = HEAD * ROWS, TAIL * ROWS
    rest = rows_dev - head - tail
    own_a, own_b = copied_rows(
        [vectors],
        [head + tail, rest],
        [(0, rows_dev - tail, 0, 0, tail), (0, 0, 0, tail, head), (0, head, 1, 0, rest)],
    )
    up1a = shifted(own_a, "mode", -1)
    dn1a = shifted(own_a, "mode", 1)
    up1b = shifted(own_b, "mode", -1)
    dn1b = shifted(own_b, "mode", 1)
    operator = operator_table(place, couplings, neighbours, atoms_dev * atom_groups)
    up1a, dn1a, operator = lax.optimization_barrier((up1a, dn1a, operator))
    up2a = shifted(up1a, "mode", -1)
    dn2a = shifted(dn1a, "mode", 1)
    up2b = shifted(up1b, "mode", -1)
    dn2b = shifted(dn1b, "mode", 1)
    below = shifted(up2a[tail - edge : tail], "atom", 1)
    above = shifted(up2a[tail : tail + edge], "atom", -1)

    shares = star_products(
        place, operator, vectors, below, above, [up2a, up1a, dn1a, dn2a], [up2b, up1b, dn1b, dn2b]
    )
    shares = [shares[0]] + [swapped(shares[k], k) for k in range(1, 4)]

    own_freq = lax.dynamic_slice_in_dim(frequency, place[1] * width, width)
    factor, seconds_done = lax.optimization_barrier((math.pi / (3.0 * own_freq * own_freq), shares[0]))
    shares[0] = seconds_done
    whole = lambda shape: pl.BlockSpec(shape, lambda g: (0, 0))
    freq_rows = frequency.reshape(modes, width)
    pair = jax.ShapeDtypeStruct((2, width), F32)
    terms = pl.pallas_call(
        functools.partial(weigh_kernel, half_width),
        grid=(1,),
        in_specs=[pl.BlockSpec(memory_space=pltpu.SMEM)] + [whole(x.shape) for x in (*shares, freq_rows)],
        out_specs=[whole(pair.shape)] * 4,
        out_shape=[pair] * 4,
        scratch_shapes=[pltpu.VMEM((5, width), F32)],
        compiler_params=pltpu.CompilerParams(vmem_limit_bytes=4 * 2**20),
    )(place, *shares, freq_rows)
    arrived = [terms[0]] + [swapped(terms[k], k) for k in range(1, 4)]
    carried = (arrived[0] + arrived[1]) + (arrived[2] + arrived[3])
    route = [(b * 4 + s, (b + RETURNS[s]) % modes * 4 + s) for b in range(modes) for s in range(4)]
    result = lax.ppermute(carried[0], ("mode", "atom"), route)
    far = [swapped(result, k) for k in range(1, 4)]
    return factor * (carried[1] + ((result + far[0]) + (far[1] + far[2])))


def solution(mesh):
    return jax.shard_map(
        local,
        mesh=mesh,
        in_specs=(P("atom", "mode"), P(None, None, None, None, "atom"), P(None, "atom"), P()),
        out_specs=P("mode"),
        check_vma=False,
    )
```

time: 104 us -> 94.8 us (0.912)
  Pallas kernels: 25.7 us -> 12.1 us
  starting transfers between devices: 49.3 us -> 55.3 us
  waiting for transfers between devices: 22.2 us -> 24.7 us
  other arithmetic: 2.62 us -> 0.68 us
  local copies, waits for them, and re-layouts: 3.3 us -> 1.87 us
    pallas_call x2, Pallas kernels: 10.9 us -> 1.86 us  [the longest x1 1.11 us: operator_table(): pl.pallas_call(functools.partial(table_kernel, total_atoms), in_specs=[pl...]
    ppermute x10, starting transfers between devices: 30.5 us -> 35.8 us  [shifted(): lax.ppermute(x, axis, [(i, (i + distance) % count) for i in range(count)])]
    ppermute x10, waiting for transfers between devices: 12 us -> 14.7 us  [shifted(): lax.ppermute(x, axis, [(i, (i + distance) % count) for i in range(count)])]
    pallas_call x1, Pallas kernels: 9.88 us -> 7.27 us  [star_products(): pl.pallas_call(second_kernel, grid=(steps,), in_specs=[pl.BlockSpec(memor...]
    pallas_call x1, Pallas kernels: 2.27 us -> 0.06 us  [copied_rows(): pl.pallas_call(functools.partial(copy_kernel, moves), out_shape=[jax.Shap...]
    unnamed x17 -> x11, local copies, waits for them, and re-layouts: 3.29 us -> 1.86 us
    add x2 -> x1, other arithmetic: 1.26 us -> 0.01 us  [local(): carried = arrived[0] + arrived[1] + (arrived[2] + arrived[3])]
  transfers between devices with their start and end apart: 20 -> 20, of which waited for: 11 -> 12; matrix products, arithmetic and copies ran while one was open for 1% -> 0% of each run, Pallas kernels for 11% -> 4%
where the time goes in v5:
time: 94.8 us; the launch traced here: 94.7 us
  starting transfers between devices  55.3 us (58%)
  waiting for transfers between devices  24.7 us (26%)
  Pallas kernels  12.1 us (13%)
  local copies, waits for them, and re-layouts  1.87 us (2%)
    ppermute x10, starting transfers between devices, shifted(): lax.ppermute(x, axis, [(i, (i + distance) % count) for i in range(count)])  35.8 us
    ppermute x9, starting transfers between devices, swapped(): return lax.ppermute(x, 'atom', [(i, i ^ k) for i in range(4)])  15.6 us
    ppermute x10, waiting for transfers between devices, shifted(): lax.ppermute(x, axis, [(i, (i + distance) % count) for i in range(count)])  14.7 us
    ppermute x9, waiting for transfers between devices, swapped(): return lax.ppermute(x, 'atom', [(i, i ^ k) for i in range(4)])  9.21 us
    pallas_call x1, Pallas kernels, star_products(): pl.pallas_call(second_kernel, grid=(steps,), in_specs=[pl.BlockSpec(memor...  7.27 us
    ppermute x1, starting transfers between devices, local(): result = lax.ppermute(carried[0], ('mode', 'atom'), route)  3.86 us
    pallas_call x1, Pallas kernels, star_products(): pl.pallas_call(first_kernel, grid=(TAIL,), in_specs=[pl.BlockSpec(op_bloc...  2.94 us
  transfers between devices with their start and end apart: 20, of which 12 were waited for; matrix products, arithmetic and copies ran while one was open for 0% of the time, Pallas kernels for 4%

profile of v5, /device:TPU:1, one launch (start us, length us, event | category | flops | bytes accessed | tf_op | source)
XLA Modules:
  0.0 94.7 jit_solution(17102634681304113626)
XLA Ops:
  0.0 0.0 copy-start
  0.0 1.2 %copy-done = bf16[3840,128]{1,0:T(8,128)(2,1)S(1)} copy-done((bf16[3840,128]{1,0:T(8,128)(2,1)S(1)}, bf16[3840,128]{1,0:T(8,128)(2,1)}, u32[]{:S(2)}) %copy-start) | copy-done | bytes 983064
  1.2 0.0 copy-start.4
  1.2 0.1 shard_map.46
  1.3 2.5 %collective-permute-start.1 = (bf16[1920,128]{1,0:T(8,128)(2,1)S(1)}, bf16[1920,128]{1,0:T(8,128)(2,1)S(1)}, u32[]{:S(2)}, u32[]{:S(2)}) collective-permute-start(bf16[1920,128]{1,0:T(8,128)(2,1)S(1)} %get-tuple-element.20), channel_id=1, source_target_pairs={{0,4},{4,8},{8,12},{12,16},{16,20},{20,24},{24,28},{28,32},{32,36}... | collective-permute-start | bytes 1474568 | tf_op jit(solution)/shard_map/ppermute | solution.py:25
  3.8 8.9 %collective-permute-start = (bf16[1920,128]{1,0:T(8,128)(2,1)S(1)}, bf16[1920,128]{1,0:T(8,128)(2,1)S(1)}, u32[]{:S(2)}, u32[]{:S(2)}) collective-permute-start(bf16[1920,128]{1,0:T(8,128)(2,1)S(1)} %get-tuple-element.20), channel_id=1, source_target_pairs={{0,252},{4,0},{8,4},{12,8},{16,12},{20,16},{24,20},{28,24},{32,28}... | collective-permute-start | bytes 1474568 | tf_op jit(solution)/shard_map/ppermute | solution.py:25
  12.8 0.0 collective-permute-start.8
  12.8 7.2 %collective-permute-start.6 = (bf16[1920,128]{1,0:T(8,128)(2,1)S(1)}, bf16[1920,128]{1,0:T(8,128)(2,1)S(1)}, u32[]{:S(2)}, u32[]{:S(2)}) collective-permute-start(bf16[1920,128]{1,0:T(8,128)(2,1)S(1)} %get-tuple-element.24), channel_id=1, source_target_pairs={{0,252},{4,0},{8,4},{12,8},{16,12},{20,16},{24,20},{28,24},{32,28}... | collective-permute-start | bytes 1474568 | tf_op jit(solution)/shard_map/ppermute | solution.py:25
  19.9 0.0 copy-done.4
  19.9 0.0 copy-start.3
  19.9 0.2 copy.5.couplings_ref
  20.1 0.1 pad_add_fusion.place_ref
  20.2 0.5 copy-done.3
  20.7 0.0 copy-start.1
  20.7 1.1 %shard_map.47.t_ref = f32[10,40,384]{2,1,0:T(8,128)S(1)} custom-call(s32[2]{0:T(128)S(1)} %pad_add_fusion.place_ref, f32[4,3,3,3,1280]{4,3,2,1,0:T(4,128)S(1)} %copy.5.couplings_ref, s32[4,1280]{1,0:T(4,128)S(1)} %copy-done.3), custom_call_target="tpu_custom_call" | custom-call | flops 2000000000 | bytes 3000000 | tf_op jit(solution)/shard_map/pallas_call | solution.py:58
  21.8 1.8 %collective-permute-done.1.p3.a2 = bf16[1920,128]{1,0:T(8,128)(2,1)S(1)} collective-permute-done((bf16[1920,128]{1,0:T(8,128)(2,1)S(1)}, bf16[1920,128]{1,0:T(8,128)(2,1)S(1)}, u32[]{:S(2)}, u32[]{:S(2)}) %collective-permute-start.1) | collective-permute-done | bytes 491552 | tf_op jit(solution)/shard_map/ppermute | solution.py:25
  23.6 0.0 collective-permute-done.p1.a1
  23.6 7.0 %collective-permute-start.2 = (bf16[1920,128]{1,0:T(8,128)(2,1)S(1)}, bf16[1920,128]{1,0:T(8,128)(2,1)S(1)}, u32[]{:S(2)}, u32[]{:S(2)}) collective-permute-start(bf16[1920,128]{1,0:T(8,128)(2,1)S(1)} %collective-permute-done.p1.a1), channel_id=1, source_target_pairs={{0,252},{4,0},{8,4},{12,8},{16,12},{20,16},{24,20},{28,24},{32,28}... | collective-permute-start | bytes 1474568 | tf_op jit(solution)/shard_map/ppermute | solution.py:25
  30.6 0.0 collective-permute-start.5
  30.6 3.6 %collective-permute-done.8.b2 = bf16[1920,128]{1,0:T(8,128)(2,1)S(1)} collective-permute-done((bf16[1920,128]{1,0:T(8,128)(2,1)S(1)}, bf16[1920,128]{1,0:T(8,128)(2,1)S(1)}, u32[]{:S(2)}, u32[]{:S(2)}) %collective-permute-start.8) | collective-permute-done | bytes 491552 | tf_op jit(solution)/shard_map/ppermute | solution.py:25
  34.1 0.0 collective-permute-start.9
  34.1 0.0 collective-permute-done.6.b1
  34.2 7.2 %collective-permute-start.7 = (bf16[1920,128]{1,0:T(8,128)(2,1)S(1)}, bf16[1920,128]{1,0:T(8,128)(2,1)S(1)}, u32[]{:S(2)}, u32[]{:S(2)}) collective-permute-start(bf16[1920,128]{1,0:T(8,128)(2,1)S(1)} %collective-permute-done.6.b1), channel_id=1, source_target_pairs={{0,252},{4,0},{8,4},{12,8},{16,12},{20,16},{24,20},{28,24},{32,28}... | collective-permute-start | bytes 1474568 | tf_op jit(solution)/shard_map/ppermute | solution.py:25
  41.3 2.4 %collective-permute-done.2.far_ref.p0.far_a.a0 = bf16[1920,128]{1,0:T(8,128)(2,1)S(1)} collective-permute-done((bf16[1920,128]{1,0:T(8,128)(2,1)S(1)}, bf16[1920,128]{1,0:T(8,128)(2,1)S(1)}, u32[]{:S(2)}, u32[]{:S(2)}) %collective-permute-start.2) | collective-permute-done | bytes 491552 | tf_op jit(solution)/shard_map/ppermute | solution.py:25
  43.7 2.7 %collective-permute-start.4 = (bf16[192,128]{1,0:T(8,128)(2,1)S(1)}, bf16[192,128]{1,0:T(8,128)(2,1)S(1)}, u32[]{:S(2)}, u32[]{:S(2)}) collective-permute-start(bf16[192,128]{1,0:T(8,128)(2,1)S(1)} %get-tuple-element.35), channel_id=1, source_target_pairs={{0,3},{1,0},{2,1},{3,2},{4,7},{5,4},{6,5},{7,6},{8,11},{9,8},{10,9... | collective-permute-start | bytes 147464 | tf_op jit(solution)/shard_map/ppermute | solution.py:25
  46.4 0.3 collective-permute-start.3
  46.7 0.0 collective-permute-done.5.p4.a3
  46.7 2.0 %collective-permute-done.4.above_ref = bf16[192,128]{1,0:T(8,128)(2,1)S(1)} collective-permute-done((bf16[192,128]{1,0:T(8,128)(2,1)S(1)}, bf16[192,128]{1,0:T(8,128)(2,1)S(1)}, u32[]{:S(2)}, u32[]{:S(2)}) %collective-permute-start.4) | collective-permute-done | bytes 49184 | tf_op jit(solution)/shard_map/ppermute | solution.py:25
  48.7 0.0 collective-permute-done.3.below_ref
  48.7 0.0 copy-done.1
  48.7 2.9 %shard_map.48.before_ref = f32[384,640]{1,0:T(8,128)S(1)} custom-call(f32[10,40,384]{2,1,0:T(8,128)S(1)} %shard_map.47.t_ref, bf16[1920,128]{1,0:T(8,128)(2,1)S(1)} %collective-permute-done.2.far_ref.p0.far_a.a0, bf16[192,128]{1,0:T(8,128)(2,1)S(1)} %collective-permute-done.3.below_ref, bf16[192,128]{1,0:T(8,128)(2,1)S(1)} %collective-permute-done.4.above_ref, ...), custom_call_target="tpu_custom_call" | custom-call | flops 3000000000 | bytes 9000000 | tf_op jit(solution)/shard_map/pallas_call | solution.py:184
  51.6 0.0 copy-start.2
  51.6 5.0 %collective-permute-done.9.b3 = bf16[1920,128]{1,0:T(8,128)(2,1)S(1)} collective-permute-done((bf16[1920,128]{1,0:T(8,128)(2,1)S(1)}, bf16[1920,128]{1,0:T(8,128)(2,1)S(1)}, u32[]{:S(2)}, u32[]{:S(2)}) %collective-permute-start.9) | collective-permute-done | bytes 491552 | tf_op jit(solution)/shard_map/ppermute | solution.py:25
  56.6 0.0 collective-permute-done.7.far_b.b0
  56.6 7.3 %shard_map.49 = (bf16[96,640]{1,0:T(8,128)(2,1)S(1)}, bf16[96,640]{1,0:T(8,128)(2,1)S(1)}, bf16[96,640]{1,0:T(8,128)(2,1)S(1)}, bf16[96,640]{1,0:T(8,128)(2,1)S(1)}) custom-call(s32[2]{0:T(128)S(1)} %pad_add_fusion.place_ref, f32[10,40,384]{2,1,0:T(8,128)S(1)} %shard_map.47.t_ref, f32[384,640]{1,0:T(8,128)S(1)} %shard_map.48.before_ref, ...), custom_call_target="tpu_custom_call" | custom-call | flops 7000000000 | bytes 21000000 | tf_op jit(solution)/shard_map/pallas_call | solution.py:199
  63.9 4.0 %collective-permute-start.10 = (bf16[96,640]{1,0:T(8,128)(2,1)S(1)}, bf16[96,640]{1,0:T(8,128)(2,1)S(1)}, u32[]{:S(2)}, u32[]{:S(2)}) collective-permute-start(bf16[96,640]{1,0:T(8,128)(2,1)S(1)} %get-tuple-element.28), channel_id=1, source_target_pairs={{0,1},{1,0},{2,3},{3,2},{4,5},{5,4},{6,7},{7,6},{8,9},{9,8},{10,11... | collective-permute-start | bytes 368648 | tf_op jit(solution)/shard_map/ppermute | solution.py:255
  67.9 0.3 collective-permute-start.11
  68.2 1.6 %collective-permute-start.12 = (bf16[96,640]{1,0:T(8,128)(2,1)S(1)}, bf16[96,640]{1,0:T(8,128)(2,1)S(1)}, u32[]{:S(2)}, u32[]{:S(2)}) collective-permute-start(bf16[96,640]{1,0:T(8,128)(2,1)S(1)} %get-tuple-element.30), channel_id=1, source_target_pairs={{0,3},{1,2},{2,1},{3,0},{4,7},{5,6},{6,5},{7,4},{8,11},{9,10},{10,... | collective-permute-start | bytes 368648 | tf_op jit(solution)/shard_map/ppermute | solution.py:255
  69.8 0.0 copy-done.2
  69.8 0.1 fusion
  69.9 0.0 collective-permute-done.10.s1
  69.9 2.6 %collective-permute-done.11.s2 = bf16[96,640]{1,0:T(8,128)(2,1)S(1)} collective-permute-done((bf16[96,640]{1,0:T(8,128)(2,1)S(1)}, bf16[96,640]{1,0:T(8,128)(2,1)S(1)}, u32[]{:S(2)}, u32[]{:S(2)}) %collective-permute-start.11) | collective-permute-done | bytes 122912 | tf_op jit(solution)/shard_map/ppermute | solution.py:255
  72.6 3.0 %collective-permute-done.12.s3 = bf16[96,640]{1,0:T(8,128)(2,1)S(1)} collective-permute-done((bf16[96,640]{1,0:T(8,128)(2,1)S(1)}, bf16[96,640]{1,0:T(8,128)(2,1)S(1)}, u32[]{:S(2)}, u32[]{:S(2)}) %collective-permute-start.12) | collective-permute-done | bytes 122912 | tf_op jit(solution)/shard_map/ppermute | solution.py:255
  75.6 0.8 shard_map.50
  76.4 0.1 collective-permute-start.13
  76.5 0.4 collective-permute-start.14
  76.8 1.7 %collective-permute-start.15 = (f32[2,128]{1,0:T(2,128)S(1)}, f32[2,128]{1,0:T(2,128)S(1)}, u32[]{:S(2)}, u32[]{:S(2)}) collective-permute-start(f32[2,128]{1,0:T(2,128)S(1)} %get-tuple-element.34), channel_id=1, source_target_pairs={{0,3},{1,2},{2,1},{3,0},{4,7},{5,6},{6,5},{7,4},{8,11},{9,10},{10,... | collective-permute-start | bytes 3080 | tf_op jit(solution)/shard_map/ppermute | solution.py:255
  78.6 0.0 collective-permute-done.13
  78.6 0.4 collective-permute-done.14
  79.0 1.2 %collective-permute-done.15 = f32[2,128]{1,0:T(2,128)S(1)} collective-permute-done((f32[2,128]{1,0:T(2,128)S(1)}, f32[2,128]{1,0:T(2,128)S(1)}, u32[]{:S(2)}, u32[]{:S(2)}) %collective-permute-start.15) | collective-permute-done | bytes 1056 | tf_op jit(solution)/shard_map/ppermute | solution.py:255
  80.2 3.9 %collective-permute-start.16 = (f32[128]{0:T(128)S(1)}, f32[128]{0:T(128)S(1)}, u32[]{:S(2)}, u32[]{:S(2)}) collective-permute-start(f32[128]{0:T(128)S(1)} %slice_bitcast_fusion), channel_id=1, source_target_pairs={{0,4},{1,253},{2,10},{3,251},{4,8},{5,1},{6,14},{7,255},{8,12},{9,... | collective-permute-start | bytes 1544 | tf_op jit(solution)/shard_map/ppermute | solution.py:309
  84.0 0.7 collective-permute-done.16
  84.7 7.0 %collective-permute-start.19 = (f32[128]{0:T(128)S(1)}, f32[128]{0:T(128)S(1)}, u32[]{:S(2)}, u32[]{:S(2)}) collective-permute-start(f32[128]{0:T(128)S(1)} %collective-permute-done.16), channel_id=1, source_target_pairs={{0,3},{1,2},{2,1},{3,0},{4,7},{5,6},{6,5},{7,4},{8,11},{9,10},{10,... | collective-permute-start | bytes 1544 | tf_op jit(solution)/shard_map/ppermute | solution.py:255
  91.8 0.0 collective-permute-start.18
  91.8 0.4 collective-permute-start.17
  92.2 0.8 collective-permute-done.19
  93.0 1.2 %collective-permute-done.18 = f32[128]{0:T(128)S(1)} collective-permute-done((f32[128]{0:T(128)S(1)}, f32[128]{0:T(128)S(1)}, u32[]{:S(2)}, u32[]{:S(2)}) %collective-permute-start.18) | collective-permute-done | bytes 544 | tf_op jit(solution)/shard_map/ppermute | solution.py:255
  94.2 0.0 collective-permute-done.17
  94.2 0.5 fusion.1
  (3 shorter events, 0.0 us)
Async XLA Ops:
  0.0 1.2 %copy-start = (bf16[3840,128]{1,0:T(8,128)(2,1)S(1)}, bf16[3840,128]{1,0:T(8,128)(2,1)}, u32[]{:S(2)}) copy-start(bf16[3840,128]{1,0:T(8,128)(2,1)} %own.1) | copy-start | bytes 2949124
  1.2 18.7 %copy-start.4 = (f32[4,3,3,3,1280]{4,0,3,2,1:T(4,128)S(1)}, f32[4,3,3,3,1280]{4,0,3,2,1:T(4,128)}, u32[]{:S(2)}) copy-start(f32[4,3,3,3,1280]{4,0,3,2,1:T(4,128)} %param.5) | copy-start | bytes 1658884
  1.3 22.3 %collective-permute-start.1 = (bf16[1920,128]{1,0:T(8,128)(2,1)S(1)}, bf16[1920,128]{1,0:T(8,128)(2,1)S(1)}, u32[]{:S(2)}, u32[]{:S(2)}) collective-permute-start(bf16[1920,128]{1,0:T(8,128)(2,1)S(1)} %get-tuple-element.20), channel_id=1, source_target_pairs={{0,4},{4,8},{8,12},{12,16},{16,20},{20,24},{24,28},{28,32},{32,36}... | collective-permute-start | bytes 1474568 | tf_op jit(solution)/shard_map/ppermute | solution.py:25
  3.8 19.8 %collective-permute-start = (bf16[1920,128]{1,0:T(8,128)(2,1)S(1)}, bf16[1920,128]{1,0:T(8,128)(2,1)S(1)}, u32[]{:S(2)}, u32[]{:S(2)}) collective-permute-start(bf16[1920,128]{1,0:T(8,128)(2,1)S(1)} %get-tuple-element.20), channel_id=1, source_target_pairs={{0,252},{4,0},{8,4},{12,8},{16,12},{20,16},{24,20},{28,24},{32,28}... | collective-permute-start | bytes 1474568 | tf_op jit(solution)/shard_map/ppermute | solution.py:25
  12.8 21.4 %collective-permute-start.8 = (bf16[1920,128]{1,0:T(8,128)(2,1)S(1)}, bf16[1920,128]{1,0:T(8,128)(2,1)S(1)}, u32[]{:S(2)}, u32[]{:S(2)}) collective-permute-start(bf16[1920,128]{1,0:T(8,128)(2,1)S(1)} %get-tuple-element.24), channel_id=1, source_target_pairs={{0,4},{4,8},{8,12},{12,16},{16,20},{20,24},{24,28},{28,32},{32,36}... | collective-permute-start | bytes 1474568 | tf_op jit(solution)/shard_map/ppermute | solution.py:25
  12.8 21.4 %collective-permute-start.6 = (bf16[1920,128]{1,0:T(8,128)(2,1)S(1)}, bf16[1920,128]{1,0:T(8,128)(2,1)S(1)}, u32[]{:S(2)}, u32[]{:S(2)}) collective-permute-start(bf16[1920,128]{1,0:T(8,128)(2,1)S(1)} %get-tuple-element.24), channel_id=1, source_target_pairs={{0,252},{4,0},{8,4},{12,8},{16,12},{20,16},{24,20},{28,24},{32,28}... | collective-permute-start | bytes 1474568 | tf_op jit(solution)/shard_map/ppermute | solution.py:25
  19.9 0.7 copy-start.3
  20.7 28.0 %copy-start.1 = (bf16[3840,128]{1,0:T(8,128)(2,1)S(1)}, bf16[3840,128]{1,0:T(8,128)(2,1)}, u32[]{:S(2)}) copy-start(bf16[3840,128]{1,0:T(8,128)(2,1)} %own.1) | copy-start | bytes 2949124
  23.6 20.1 %collective-permute-start.2 = (bf16[1920,128]{1,0:T(8,128)(2,1)S(1)}, bf16[1920,128]{1,0:T(8,128)(2,1)S(1)}, u32[]{:S(2)}, u32[]{:S(2)}) collective-permute-start(bf16[1920,128]{1,0:T(8,128)(2,1)S(1)} %collective-permute-done.p1.a1), channel_id=1, source_target_pairs={{0,252},{4,0},{8,4},{12,8},{16,12},{20,16},{24,20},{28,24},{32,28}... | collective-permute-start | bytes 1474568 | tf_op jit(solution)/shard_map/ppermute | solution.py:25
  30.6 16.1 %collective-permute-start.5 = (bf16[1920,128]{1,0:T(8,128)(2,1)S(1)}, bf16[1920,128]{1,0:T(8,128)(2,1)S(1)}, u32[]{:S(2)}, u32[]{:S(2)}) collective-permute-start(bf16[1920,128]{1,0:T(8,128)(2,1)S(1)} %collective-permute-done.1.p3.a2), channel_id=1, source_target_pairs={{0,4},{4,8},{8,12},{12,16},{16,20},{20,24},{24,28},{28,32},{32,36}... | collective-permute-start | bytes 1474568 | tf_op jit(solution)/shard_map/ppermute | solution.py:25
  34.1 22.5 %collective-permute-start.9 = (bf16[1920,128]{1,0:T(8,128)(2,1)S(1)}, bf16[1920,128]{1,0:T(8,128)(2,1)S(1)}, u32[]{:S(2)}, u32[]{:S(2)}) collective-permute-start(bf16[1920,128]{1,0:T(8,128)(2,1)S(1)} %collective-permute-done.8.b2), channel_id=1, source_target_pairs={{0,4},{4,8},{8,12},{12,16},{16,20},{20,24},{24,28},{28,32},{32,36}... | collective-permute-start | bytes 1474568 | tf_op jit(solution)/shard_map/ppermute | solution.py:25
  34.2 22.5 %collective-permute-start.7 = (bf16[1920,128]{1,0:T(8,128)(2,1)S(1)}, bf16[1920,128]{1,0:T(8,128)(2,1)S(1)}, u32[]{:S(2)}, u32[]{:S(2)}) collective-permute-start(bf16[1920,128]{1,0:T(8,128)(2,1)S(1)} %collective-permute-done.6.b1), channel_id=1, source_target_pairs={{0,252},{4,0},{8,4},{12,8},{16,12},{20,16},{24,20},{28,24},{32,28}... | collective-permute-start | bytes 1474568 | tf_op jit(solution)/shard_map/ppermute | solution.py:25
  43.7 5.0 %collective-permute-start.4 = (bf16[192,128]{1,0:T(8,128)(2,1)S(1)}, bf16[192,128]{1,0:T(8,128)(2,1)S(1)}, u32[]{:S(2)}, u32[]{:S(2)}) collective-permute-start(bf16[192,128]{1,0:T(8,128)(2,1)S(1)} %get-tuple-element.35), channel_id=1, source_target_pairs={{0,3},{1,0},{2,1},{3,2},{4,7},{5,4},{6,5},{7,6},{8,11},{9,8},{10,9... | collective-permute-start | bytes 147464 | tf_op jit(solution)/shard_map/ppermute | solution.py:25
  46.4 2.3 %collective-permute-start.3 = (bf16[192,128]{1,0:T(8,128)(2,1)S(1)}, bf16[192,128]{1,0:T(8,128)(2,1)S(1)}, u32[]{:S(2)}, u32[]{:S(2)}) collective-permute-start(bf16[192,128]{1,0:T(8,128)(2,1)S(1)} %get-tuple-element.36), channel_id=1, source_target_pairs={{0,1},{1,2},{2,3},{3,0},{4,5},{5,6},{6,7},{7,4},{8,9},{9,10},{10,1... | collective-permute-start | bytes 147464 | tf_op jit(solution)/shard_map/ppermute | solution.py:25
  51.6 18.2 %copy-start.2 = (f32[8192]{0:T(1024)S(1)}, f32[8192]{0:T(1024)}, u32[]{:S(2)}) copy-start(f32[8192]{0:T(1024)} %param.7) | copy-start | bytes 98308
  63.9 6.0 %collective-permute-start.10 = (bf16[96,640]{1,0:T(8,128)(2,1)S(1)}, bf16[96,640]{1,0:T(8,128)(2,1)S(1)}, u32[]{:S(2)}, u32[]{:S(2)}) collective-permute-start(bf16[96,640]{1,0:T(8,128)(2,1)S(1)} %get-tuple-element.28), channel_id=1, source_target_pairs={{0,1},{1,0},{2,3},{3,2},{4,5},{5,4},{6,7},{7,6},{8,9},{9,8},{10,11... | collective-permute-start | bytes 368648 | tf_op jit(solution)/shard_map/ppermute | solution.py:255
  67.9 4.6 %collective-permute-start.11 = (bf16[96,640]{1,0:T(8,128)(2,1)S(1)}, bf16[96,640]{1,0:T(8,128)(2,1)S(1)}, u32[]{:S(2)}, u32[]{:S(2)}) collective-permute-start(bf16[96,640]{1,0:T(8,128)(2,1)S(1)} %get-tuple-element.29), channel_id=1, source_target_pairs={{0,2},{1,3},{2,0},{3,1},{4,6},{5,7},{6,4},{7,5},{8,10},{9,11},{10,... | collective-permute-start | bytes 368648 | tf_op jit(solution)/shard_map/ppermute | solution.py:255
  68.2 7.4 %collective-permute-start.12 = (bf16[96,640]{1,0:T(8,128)(2,1)S(1)}, bf16[96,640]{1,0:T(8,128)(2,1)S(1)}, u32[]{:S(2)}, u32[]{:S(2)}) collective-permute-start(bf16[96,640]{1,0:T(8,128)(2,1)S(1)} %get-tuple-element.30), channel_id=1, source_target_pairs={{0,3},{1,2},{2,1},{3,0},{4,7},{5,6},{6,5},{7,4},{8,11},{9,10},{10,... | collective-permute-start | bytes 368648 | tf_op jit(solution)/shard_map/ppermute | solution.py:255
  76.4 2.2 %collective-permute-start.13 = (f32[2,128]{1,0:T(2,128)S(1)}, f32[2,128]{1,0:T(2,128)S(1)}, u32[]{:S(2)}, u32[]{:S(2)}) collective-permute-start(f32[2,128]{1,0:T(2,128)S(1)} %get-tuple-element.32), channel_id=1, source_target_pairs={{0,1},{1,0},{2,3},{3,2},{4,5},{5,4},{6,7},{7,6},{8,9},{9,8},{10,11... | collective-permute-start | bytes 3080 | tf_op jit(solution)/shard_map/ppermute | solution.py:255
  76.5 2.5 %collective-permute-start.14 = (f32[2,128]{1,0:T(2,128)S(1)}, f32[2,128]{1,0:T(2,128)S(1)}, u32[]{:S(2)}, u32[]{:S(2)}) collective-permute-start(f32[2,128]{1,0:T(2,128)S(1)} %get-tuple-element.33), channel_id=1, source_target_pairs={{0,2},{1,3},{2,0},{3,1},{4,6},{5,7},{6,4},{7,5},{8,10},{9,11},{10,... | collective-permute-start | bytes 3080 | tf_op jit(solution)/shard_map/ppermute | solution.py:255
  76.8 3.3 %collective-permute-start.15 = (f32[2,128]{1,0:T(2,128)S(1)}, f32[2,128]{1,0:T(2,128)S(1)}, u32[]{:S(2)}, u32[]{:S(2)}) collective-permute-start(f32[2,128]{1,0:T(2,128)S(1)} %get-tuple-element.34), channel_id=1, source_target_pairs={{0,3},{1,2},{2,1},{3,0},{4,7},{5,6},{6,5},{7,4},{8,11},{9,10},{10,... | collective-permute-start | bytes 3080 | tf_op jit(solution)/shard_map/ppermute | solution.py:255
  80.2 4.6 %collective-permute-start.16 = (f32[128]{0:T(128)S(1)}, f32[128]{0:T(128)S(1)}, u32[]{:S(2)}, u32[]{:S(2)}) collective-permute-start(f32[128]{0:T(128)S(1)} %slice_bitcast_fusion), channel_id=1, source_target_pairs={{0,4},{1,253},{2,10},{3,251},{4,8},{5,1},{6,14},{7,255},{8,12},{9,... | collective-permute-start | bytes 1544 | tf_op jit(solution)/shard_map/ppermute | solution.py:309
  84.7 8.3 %collective-permute-start.19 = (f32[128]{0:T(128)S(1)}, f32[128]{0:T(128)S(1)}, u32[]{:S(2)}, u32[]{:S(2)}) collective-permute-start(f32[128]{0:T(128)S(1)} %collective-permute-done.16), channel_id=1, source_target_pairs={{0,3},{1,2},{2,1},{3,0},{4,7},{5,6},{6,5},{7,4},{8,11},{9,10},{10,... | collective-permute-start | bytes 1544 | tf_op jit(solution)/shard_map/ppermute | solution.py:255
  91.8 2.4 %collective-permute-start.18 = (f32[128]{0:T(128)S(1)}, f32[128]{0:T(128)S(1)}, u32[]{:S(2)}, u32[]{:S(2)}) collective-permute-start(f32[128]{0:T(128)S(1)} %collective-permute-done.16), channel_id=1, source_target_pairs={{0,2},{1,3},{2,0},{3,1},{4,6},{5,7},{6,4},{7,5},{8,10},{9,11},{10,... | collective-permute-start | bytes 1544 | tf_op jit(solution)/shard_map/ppermute | solution.py:255
  91.8 2.4 %collective-permute-start.17 = (f32[128]{0:T(128)S(1)}, f32[128]{0:T(128)S(1)}, u32[]{:S(2)}, u32[]{:S(2)}) collective-permute-start(f32[128]{0:T(128)S(1)} %collective-permute-done.16), channel_id=1, source_target_pairs={{0,1},{1,0},{2,3},{3,2},{4,5},{5,4},{6,7},{7,6},{8,9},{9,8},{10,11... | collective-permute-start | bytes 1544 | tf_op jit(solution)/shard_map/ppermute | solution.py:255

commit v6 on v5

--- a/solution.py
+++ b/solution.py
@@ -75,23 +75,36 @@
     return up + ((2, 3) if meets(low - HALO, high - 2) else ())
 
 
-def fill_operator(table_ref, operator_ref):
-    for first_lane in range(0, ROWS, 128):
-        lanes = slice(first_lane, first_lane + 128)
-        wide = [jnp.broadcast_to(table_ref[0, at : at + 1, lanes], (TILE, 128)).astype(BF16) for at in range(TABLE)]
-        for first_row in range(0, WIN, TILE):
-            slots = tile_slots(first_row, first_lane)
-            if not slots:
-                continue
-            row = (lax.broadcasted_iota(jnp.int32, (TILE, 128), 0).astype(F32) + float(first_row)).astype(BF16)
-            masks = {k: row == wide[36 + k] for k in slots}
-            for a in range(3):
-                for q in range(3):
-                    value = jnp.zeros((TILE, 128), BF16)
-                    for k in reversed(slots):
-                        value = jnp.where(masks[k], wide[(k * 3 + a) * 3 + q], value)
-                    start = q * WIN + first_row
-                    operator_ref[start : start + TILE, a * ROWS + first_lane : a * ROWS + first_lane + 128] = value
+def fill_kernel(table_ref, out_ref):
+    for block in range(table_ref.shape[0]):
+        for first_lane in range(0, ROWS, 128):
+            lanes = slice(first_lane, first_lane + 128)
+            wide = [
+                jnp.broadcast_to(table_ref[block, at : at + 1, lanes], (TILE, 128)).astype(BF16) for at in range(TABLE)
+            ]
+            for first_row in range(0, WIN, TILE):
+                slots = tile_slots(first_row, first_lane)
+                row = (lax.broadcasted_iota(jnp.int32, (TILE, 128), 0).astype(F32) + float(first_row)).astype(BF16)
+                masks = {k: row == wide[36 + k] for k in slots}
+                for a in range(3):
+                    for q in range(3):
+                        value = jnp.zeros((TILE, 128), BF16)
+                        for k in reversed(slots):
+                            value = jnp.where(masks[k], wide[(k * 3 + a) * 3 + q], value)
+                        start, lane = q * WIN + first_row, a * ROWS + first_lane
+                        out_ref[block, start : start + TILE, lane : lane + 128] = value
+
+
+def filled_operator(table):
+    vmem = pl.BlockSpec(memory_space=pltpu.VMEM)
+    return pl.pallas_call(
+        fill_kernel,
+        in_specs=[vmem],
+        out_specs=vmem,
+        out_shape=jax.ShapeDtypeStruct((table.shape[0], 3 * WIN, 3 * ROWS), BF16),
+        compiler_params=pltpu.CompilerParams(vmem_limit_bytes=8 * 2**20),
+        cost_estimate=pl.CostEstimate(flops=4 * 10**9, bytes_accessed=10**6, transcendentals=0),
+    )(table)
 
 
 def copy_kernel(moves, *refs):
@@ -109,8 +122,7 @@
     )(*inputs)
 
 
-def star_step(planes_ref, start, table_ref, operator_ref, partners, total_ref):
-    fill_operator(table_ref, operator_ref)
+def star_step(planes_ref, start, operator_ref, partners, total_ref):
     window = [planes_ref[pl.ds(start + q, WIN, stride=3), :].astype(BF16) for q in range(3)]
     window = jnp.concatenate(window, axis=0).T
     applied = jnp.dot(window, operator_ref[...], preferred_element_type=F32).astype(BF16)
@@ -118,103 +130,73 @@
     total_ref[...] += jnp.dot(applied, jnp.concatenate(partners, axis=1), preferred_element_type=F32)
 
 
-def first_kernel(t_ref, far_ref, below_ref, above_ref, p0, p1, p2, p3, p4, out_ref, planes, dense):
-    g = pl.program_id(0)
+def first_kernel(t_ref, far_ref, below_ref, above_ref, p1, own, p2, p3, out_ref, planes):
     tail, edge = TAIL * ROWS, 3 * HALO
-
-    @pl.when(g == 0)
-    def _():
-        out_ref[...] = jnp.zeros_like(out_ref)
-        dense[...] = jnp.zeros_like(dense)
-        planes[0:tail, :] = far_ref[0:tail, :].astype(F32)
-        planes[tail : tail + edge, :] = above_ref[...].astype(F32)
-        planes[tail + edge : tail + 2 * edge, :] = below_ref[...].astype(F32)
-        planes[tail + 2 * edge :, :] = far_ref[tail:, :].astype(F32)
-
-    start = jnp.where(g < TAIL - 1, (g + 1) * ROWS - edge, tail + edge)
-    star_step(planes, start, t_ref, dense, [r[...] for r in (p0, p1, p2, p3, p4)], out_ref)
+    out_ref[...] = jnp.zeros_like(out_ref)
+    planes[0:tail, :] = far_ref[0:tail, :].astype(F32)
+    planes[tail : tail + edge, :] = above_ref[...].astype(F32)
+    planes[tail + edge : tail + 2 * edge, :] = below_ref[...].astype(F32)
+    planes[tail + 2 * edge :, :] = far_ref[tail:, :].astype(F32)
+    blocks = own.shape[0] // ROWS
+    for at in range(ROWS, tail + ROWS, ROWS):
+        block = (blocks - TAIL + at // ROWS) % blocks
+        near = [r[at : at + ROWS, :] for r in (far_ref, p1, p2, p3)]
+        near.insert(2, own[block * ROWS : (block + 1) * ROWS, :])
+        star_step(planes, at - edge if block else tail + edge, t_ref.at[block], near, out_ref)
 
 
 def second_kernel(
-    place_ref, t_ref, before_ref, far_a, far_b, own, a0, a1, a2, a3, b0, b1, b2, b3, o0, o1, o2, o3, planes, total, dense
+    place_ref, t_ref, before_ref, far_a, far_b, own, a1, a2, a3, b1, b2, b3, o0, o1, o2, o3, planes, total
 ):
-    g = pl.program_id(0)
-    steps = pl.num_programs(0)
     tail, head = TAIL * ROWS, HEAD * ROWS
     rows_b = far_b.shape[0]
-
-    @pl.when(g == 0)
-    def _():
-        planes[0:head, :] = far_a[tail:, :].astype(F32)
-        planes[head : head + rows_b, :] = far_b[...].astype(F32)
-        planes[head + rows_b :, :] = far_a[0:tail, :].astype(F32)
-        total[...] = before_ref[...]
-        dense[...] = jnp.zeros_like(dense)
-
-    start = (g + 1) * ROWS - 3 * HALO
-    in_first = jnp.logical_or(g == 0, g == steps - 1)
-
-    @pl.when(in_first)
-    def _():
-        star_step(planes, start, t_ref, dense, [a0[...], a1[...], own[...], a2[...], a3[...]], total)
-
-    @pl.when(jnp.logical_not(in_first))
-    def _():
-        star_step(planes, start, t_ref, dense, [b0[...], b1[...], own[...], b2[...], b3[...]], total)
-
-    @pl.when(g == steps - 1)
-    def _():
-        for k, out in enumerate((o0, o1, o2, o3)):
-            share = jnp.bitwise_xor(place_ref[0], k)
-            for a in range(3):
-                rows = pl.ds(pl.multiple_of(a * 128 + share * 32, 32), 32)
-                out[a * 32 : (a + 1) * 32, :] = total[rows, :].astype(BF16)
+    planes[0:head, :] = far_a[tail:, :].astype(F32)
+    planes[head : head + rows_b, :] = far_b[...].astype(F32)
+    planes[head + rows_b :, :] = far_a[0:tail, :].astype(F32)
+    total[...] = before_ref[...]
+    blocks = own.shape[0] // ROWS
+    for block in range(1, blocks - TAIL + 1):
+        if block < HEAD or block >= blocks - TAIL:
+            at = tail + block * ROWS if block < HEAD else (block - blocks + TAIL) * ROWS
+            near = [r[at : at + ROWS, :] for r in (far_a, a1, a2, a3)]
+        else:
+            at = (block - HEAD) * ROWS
+            near = [r[at : at + ROWS, :] for r in (far_b, b1, b2, b3)]
+        near.insert(2, own[block * ROWS : (block + 1) * ROWS, :])
+        star_step(planes, block * ROWS - 3 * HALO, t_ref.at[block], near, total)
+    for k, out in enumerate((o0, o1, o2, o3)):
+        share = jnp.bitwise_xor(place_ref[0], k)
+        for a in range(3):
+            rows = pl.ds(pl.multiple_of(a * 128 + share * 32, 32), 32)
+            out[a * 32 : (a + 1) * 32, :] = total[rows, :].astype(BF16)
 
 
 def star_products(place, operator, own, below, above, firsts, seconds):
     blocks = operator.shape[0]
     width = own.shape[1]
-    op_block = (1, TABLE, ROWS)
-    dense = pltpu.VMEM((3 * WIN, 3 * ROWS), BF16)
     shape = (3 * width, SLOTS * width)
-    whole = lambda x: pl.BlockSpec(x.shape, lambda g: (0,) * x.ndim)
+    vmem = pl.BlockSpec(memory_space=pltpu.VMEM)
     cost = lambda n: pl.CostEstimate(flops=n * 10**9, bytes_accessed=n * 3 * 10**6, transcendentals=0)
-    at = lambda g: lax.rem(g + blocks - TAIL + 1, blocks)
-    in_a = pl.BlockSpec((ROWS, width), lambda g: (g + 1, 0))
     before = pl.pallas_call(
         first_kernel,
-        grid=(TAIL,),
-        in_specs=[pl.BlockSpec(op_block, lambda g: (at(g), 0, 0)), whole(firsts[0]), whole(below), whole(above)]
-        + [in_a, in_a, pl.BlockSpec((ROWS, width), lambda g: (at(g), 0)), in_a, in_a],
-        out_specs=pl.BlockSpec(shape, lambda g: (0, 0)),
+        in_specs=[vmem] * 8,
+        out_specs=vmem,
         out_shape=jax.ShapeDtypeStruct(shape, F32),
-        scratch_shapes=[pltpu.VMEM((firsts[0].shape[0] + 6 * HALO, width), F32), dense],
-        compiler_params=pltpu.CompilerParams(vmem_limit_bytes=24 * 2**20),
+        scratch_shapes=[pltpu.VMEM((firsts[0].shape[0] + 6 * HALO, width), F32)],
+        compiler_params=pltpu.CompilerParams(vmem_limit_bytes=10 * 2**20),
         cost_estimate=cost(TAIL),
-    )(operator, firsts[0], below, above, firsts[0], firsts[1], own, firsts[2], firsts[3])
+    )(operator, firsts[0], below, above, firsts[1], own, *firsts[2:])
     steps = blocks - TAIL
-    in_a = pl.BlockSpec((ROWS, width), lambda g: (jnp.where(g == steps - 1, 0, TAIL + HEAD - 1), 0))
-    in_b = pl.BlockSpec((ROWS, width), lambda g: (jnp.clip(g - 1, 0, steps - 3), 0))
     out_shape = (shape[0] // 4, shape[1])
     return pl.pallas_call(
         second_kernel,
-        grid=(steps,),
-        in_specs=[
-            pl.BlockSpec(memory_space=pltpu.SMEM),
-            pl.BlockSpec(op_block, lambda g: (g + 1, 0, 0)),
-            pl.BlockSpec(shape, lambda g: (0, 0)),
-            whole(firsts[0]),
-            whole(seconds[0]),
-            pl.BlockSpec((ROWS, width), lambda g: (g + 1, 0)),
-        ]
-        + [in_a] * 4
-        + [in_b] * 4,
-        out_specs=[pl.BlockSpec(out_shape, lambda g: (0, 0))] * 4,
+        in_specs=[pl.BlockSpec(memory_space=pltpu.SMEM)] + [vmem] * 11,
+        out_specs=[vmem] * 4,
         out_shape=[jax.ShapeDtypeStruct(out_shape, BF16)] * 4,
-        scratch_shapes=[pltpu.VMEM((blocks * ROWS, width), F32), pltpu.VMEM(shape, F32), dense],
-        compiler_params=pltpu.CompilerParams(vmem_limit_bytes=32 * 2**20),
+        scratch_shapes=[pltpu.VMEM((blocks * ROWS, width), F32), pltpu.VMEM(shape, F32)],
+        compiler_params=pltpu.CompilerParams(vmem_limit_bytes=12 * 2**20),
         cost_estimate=cost(steps),
-    )(place, operator, before, firsts[0], seconds[0], own, *firsts, *seconds)
+    )(place, operator, before, firsts[0], seconds[0], own, *firsts[1:], *seconds[1:])
 
 
 RETURNS = (1, -1, 2, -2)
@@ -283,6 +265,8 @@
     below = shifted(up2a[tail - edge : tail], "atom", 1)
     above = shifted(up2a[tail : tail + edge], "atom", -1)
 
+    operator, up2a = lax.optimization_barrier((operator, up2a))
+    operator = filled_operator(operator)
     shares = star_products(
         place, operator, vectors, below, above, [up2a, up1a, dn1a, dn2a], [up2b, up1b, dn1b, dn2b]
     )

time: 94.8 us -> 93.4 us (0.985)
  waiting for transfers between devices: 24.7 us -> 21.7 us
  local copies, waits for them, and re-layouts: 1.87 us -> 3.19 us
    ppermute x10, waiting for transfers between devices: 14.7 us -> 11.6 us  [shifted(): lax.ppermute(x, axis, [(i, (i + distance) % count) for i in range(count)])]
    unnamed x11 -> x9, local copies, waits for them, and re-layouts: 1.86 us -> 3.18 us
    pallas_call x1, Pallas kernels: 0.06 us -> 1.04 us  [copied_rows(): pl.pallas_call(functools.partial(copy_kernel, moves), out_shape=[jax.Shap...]
    pallas_call x2 -> x3, Pallas kernels: 10.2 us -> 9.59 us  [the longest x1 4.78 us: star_products(): pl.pallas_call(second_kernel, in_specs=[pl.BlockSpec(memory_space=pltpu.S...]
  transfers between devices with their start and end apart: 20 -> 20, of which waited for: 12 -> 11; matrix products, arithmetic and copies ran while one was open for 0% -> 2% of each run, Pallas kernels for 4% -> 6%
where the time goes in v6:
time: 93.4 us; the launch traced here: 93.2 us
  starting transfers between devices  55 us (59%)
  waiting for transfers between devices  21.7 us (23%)
  Pallas kernels  12.5 us (13%)
  local copies, waits for them, and re-layouts  3.19 us (3%)
    ppermute x10, starting transfers between devices, shifted(): lax.ppermute(x, axis, [(i, (i + distance) % count) for i in range(count)])  35.7 us
    ppermute x9, starting transfers between devices, swapped(): return lax.ppermute(x, 'atom', [(i, i ^ k) for i in range(4)])  15.4 us
    ppermute x10, waiting for transfers between devices, shifted(): lax.ppermute(x, axis, [(i, (i + distance) % count) for i in range(count)])  11.6 us
    ppermute x9, waiting for transfers between devices, swapped(): return lax.ppermute(x, 'atom', [(i, i ^ k) for i in range(4)])  9.41 us
    pallas_call x1, Pallas kernels, star_products(): pl.pallas_call(second_kernel, in_specs=[pl.BlockSpec(memory_space=pltpu.S...  4.78 us
    ppermute x1, starting transfers between devices, local(): result = lax.ppermute(carried[0], ('mode', 'atom'), route)  3.85 us
    unnamed x9, local copies, waits for them, and re-layouts  3.18 us
    pallas_call x1, Pallas kernels, filled_operator(): pl.pallas_call(fill_kernel, in_specs=[vmem], out_specs=vmem, out_shape=ja...  2.92 us
  transfers between devices with their start and end apart: 20, of which 11 were waited for; matrix products, arithmetic and copies ran while one was open for 2% of the time, Pallas kernels for 6%

profile of v6, /device:TPU:1, one launch (start us, length us, event | category | flops | bytes accessed | tf_op | source)
XLA Modules:
  0.0 93.2 jit_solution(6842938815803474646)
XLA Ops:
  0.0 0.0 copy-start
  0.0 1.2 %copy-done = bf16[3840,128]{1,0:T(8,128)(2,1)S(1)} copy-done((bf16[3840,128]{1,0:T(8,128)(2,1)S(1)}, bf16[3840,128]{1,0:T(8,128)(2,1)}, u32[]{:S(2)}) %copy-start) | copy-done | bytes 983064
  1.2 0.0 copy-start.1
  1.2 1.0 %shard_map.46 = (bf16[1920,128]{1,0:T(8,128)(2,1)}, bf16[1920,128]{1,0:T(8,128)(2,1)}) custom-call(bf16[3840,128]{1,0:T(8,128)(2,1)S(1)} %copy-done), custom_call_target="tpu_custom_call" | custom-call | tf_op jit(solution)/shard_map/pallas_call | solution.py:118
  2.2 2.5 %collective-permute-start.1 = (bf16[1920,128]{1,0:T(8,128)(2,1)}, bf16[1920,128]{1,0:T(8,128)(2,1)S(1)}, u32[]{:S(2)}, u32[]{:S(2)}) collective-permute-start(bf16[1920,128]{1,0:T(8,128)(2,1)} %get-tuple-element.22), channel_id=1, source_target_pairs={{0,4},{4,8},{8,12},{12,16},{16,20},{20,24},{24,28},{28,32},{32,36}... | collective-permute-start | bytes 1474568 | tf_op jit(solution)/shard_map/ppermute | solution.py:25
  4.7 8.9 %collective-permute-start = (bf16[1920,128]{1,0:T(8,128)(2,1)}, bf16[1920,128]{1,0:T(8,128)(2,1)S(1)}, u32[]{:S(2)}, u32[]{:S(2)}) collective-permute-start(bf16[1920,128]{1,0:T(8,128)(2,1)} %get-tuple-element.22), channel_id=1, source_target_pairs={{0,252},{4,0},{8,4},{12,8},{16,12},{20,16},{24,20},{28,24},{32,28}... | collective-permute-start | bytes 1474568 | tf_op jit(solution)/shard_map/ppermute | solution.py:25
  13.6 0.0 collective-permute-start.8
  13.6 7.2 %collective-permute-start.6 = (bf16[1920,128]{1,0:T(8,128)(2,1)}, bf16[1920,128]{1,0:T(8,128)(2,1)S(1)}, u32[]{:S(2)}, u32[]{:S(2)}) collective-permute-start(bf16[1920,128]{1,0:T(8,128)(2,1)} %get-tuple-element.28), channel_id=1, source_target_pairs={{0,252},{4,0},{8,4},{12,8},{16,12},{20,16},{24,20},{28,24},{32,28}... | collective-permute-start | bytes 1474568 | tf_op jit(solution)/shard_map/ppermute | solution.py:25
  20.8 1.2 %copy.5.couplings_ref = f32[4,3,3,3,1280]{4,3,2,1,0:T(4,128)S(1)} copy(f32[4,3,3,3,1280]{4,0,3,2,1:T(4,128)} %param.5) | data formatting | bytes 1105920 | tf_op args[1]
  22.0 0.1 pad_add_fusion.place_ref
  22.1 0.0 copy-start.3
  22.1 0.7 copy-done.3
  22.8 1.1 %shard_map.47.table_ref = f32[10,40,384]{2,1,0:T(8,128)S(1)} custom-call(s32[2]{0:T(128)S(1)} %pad_add_fusion.place_ref, f32[4,3,3,3,1280]{4,3,2,1,0:T(4,128)S(1)} %copy.5.couplings_ref, s32[4,1280]{1,0:T(4,128)S(1)} %copy-done.3), custom_call_target="tpu_custom_call" | custom-call | flops 2000000000 | bytes 3000000 | tf_op jit(solution)/shard_map/pallas_call | solution.py:58
  23.9 0.8 collective-permute-done.1.p2.a2
  24.7 0.0 collective-permute-done.p1.a1
  24.7 6.9 %collective-permute-start.2 = (bf16[1920,128]{1,0:T(8,128)(2,1)S(1)}, bf16[1920,128]{1,0:T(8,128)(2,1)S(1)}, u32[]{:S(2)}, u32[]{:S(2)}) collective-permute-start(bf16[1920,128]{1,0:T(8,128)(2,1)S(1)} %collective-permute-done.p1.a1), channel_id=1, source_target_pairs={{0,252},{4,0},{8,4},{12,8},{16,12},{20,16},{24,20},{28,24},{32,28}... | collective-permute-start | bytes 1474568 | tf_op jit(solution)/shard_map/ppermute | solution.py:25
  31.6 0.0 collective-permute-start.5
  31.6 3.7 %collective-permute-done.8.b2 = bf16[1920,128]{1,0:T(8,128)(2,1)S(1)} collective-permute-done((bf16[1920,128]{1,0:T(8,128)(2,1)}, bf16[1920,128]{1,0:T(8,128)(2,1)S(1)}, u32[]{:S(2)}, u32[]{:S(2)}) %collective-permute-start.8) | collective-permute-done | bytes 491552 | tf_op jit(solution)/shard_map/ppermute | solution.py:25
  35.2 0.0 collective-permute-start.9
  35.3 0.0 collective-permute-done.6.b1
  35.3 7.2 %collective-permute-start.7 = (bf16[1920,128]{1,0:T(8,128)(2,1)S(1)}, bf16[1920,128]{1,0:T(8,128)(2,1)S(1)}, u32[]{:S(2)}, u32[]{:S(2)}) collective-permute-start(bf16[1920,128]{1,0:T(8,128)(2,1)S(1)} %collective-permute-done.6.b1), channel_id=1, source_target_pairs={{0,252},{4,0},{8,4},{12,8},{16,12},{20,16},{24,20},{28,24},{32,28}... | collective-permute-start | bytes 1474568 | tf_op jit(solution)/shard_map/ppermute | solution.py:25
  42.4 2.3 %collective-permute-done.2.far_ref.far_a = bf16[1920,128]{1,0:T(8,128)(2,1)S(1)} collective-permute-done((bf16[1920,128]{1,0:T(8,128)(2,1)S(1)}, bf16[1920,128]{1,0:T(8,128)(2,1)S(1)}, u32[]{:S(2)}, u32[]{:S(2)}) %collective-permute-start.2) | collective-permute-done | bytes 491552 | tf_op jit(solution)/shard_map/ppermute | solution.py:25
  44.7 2.7 %collective-permute-start.4 = (bf16[192,128]{1,0:T(8,128)(2,1)S(1)}, bf16[192,128]{1,0:T(8,128)(2,1)S(1)}, u32[]{:S(2)}, u32[]{:S(2)}) collective-permute-start(bf16[192,128]{1,0:T(8,128)(2,1)S(1)} %get-tuple-element.39), channel_id=1, source_target_pairs={{0,3},{1,0},{2,1},{3,2},{4,7},{5,4},{6,5},{7,6},{8,11},{9,8},{10,9... | collective-permute-start | bytes 147464 | tf_op jit(solution)/shard_map/ppermute | solution.py:25
  47.4 0.5 collective-permute-start.3
  47.9 2.9 %shard_map.48.t_ref = bf16[10,768,1152]{2,1,0:T(8,128)(2,1)S(1)} custom-call(f32[10,40,384]{2,1,0:T(8,128)S(1)} %shard_map.47.table_ref), custom_call_target="tpu_custom_call" | custom-call | flops 4000000000 | bytes 1000000 | tf_op jit(solution)/shard_map/pallas_call | solution.py:100
  50.8 0.0 collective-permute-done.5.p3.a3
  50.8 0.0 collective-permute-done.4.above_ref
  50.8 0.0 collective-permute-done.3.below_ref
  50.8 0.0 copy-done.1
  50.9 1.9 %shard_map.49.before_ref = f32[384,640]{1,0:T(8,128)S(1)} custom-call(bf16[10,768,1152]{2,1,0:T(8,128)(2,1)S(1)} %shard_map.48.t_ref, bf16[1920,128]{1,0:T(8,128)(2,1)S(1)} %collective-permute-done.2.far_ref.far_a, bf16[192,128]{1,0:T(8,128)(2,1)S(1)} %collective-permute-done.3.below_ref, bf16[192,128]{1,0:T(8,128)(2,1)S(1)} %collective-permute-done.4.above_ref, ...), custom_call_target="tpu_custom_call" | custom-call | flops 3000000000 | bytes 9000000 | tf_op jit(solution)/shard_map/pallas_call | solution.py:180
  52.8 0.0 copy-start.2
  52.8 4.9 %collective-permute-done.9.b3 = bf16[1920,128]{1,0:T(8,128)(2,1)S(1)} collective-permute-done((bf16[1920,128]{1,0:T(8,128)(2,1)S(1)}, bf16[1920,128]{1,0:T(8,128)(2,1)S(1)}, u32[]{:S(2)}, u32[]{:S(2)}) %collective-permute-start.9) | collective-permute-done | bytes 491552 | tf_op jit(solution)/shard_map/ppermute | solution.py:25
  57.6 0.0 collective-permute-done.7.far_b
  57.6 4.8 %shard_map.50 = (bf16[96,640]{1,0:T(8,128)(2,1)S(1)}, bf16[96,640]{1,0:T(8,128)(2,1)S(1)}, bf16[96,640]{1,0:T(8,128)(2,1)S(1)}, bf16[96,640]{1,0:T(8,128)(2,1)S(1)}) custom-call(s32[2]{0:T(128)S(1)} %pad_add_fusion.place_ref, bf16[10,768,1152]{2,1,0:T(8,128)(2,1)S(1)} %shard_map.48.t_ref, f32[384,640]{1,0:T(8,128)S(1)} %shard_map.49.before_ref, ...), custom_call_target="tpu_custom_call" | custom-call | flops 7000000000 | bytes 21000000 | tf_op jit(solution)/shard_map/pallas_call | solution.py:191
  62.4 4.0 %collective-permute-start.10 = (bf16[96,640]{1,0:T(8,128)(2,1)S(1)}, bf16[96,640]{1,0:T(8,128)(2,1)S(1)}, u32[]{:S(2)}, u32[]{:S(2)}) collective-permute-start(bf16[96,640]{1,0:T(8,128)(2,1)S(1)} %get-tuple-element.32), channel_id=1, source_target_pairs={{0,1},{1,0},{2,3},{3,2},{4,5},{5,4},{6,7},{7,6},{8,9},{9,8},{10,11... | collective-permute-start | bytes 368648 | tf_op jit(solution)/shard_map/ppermute | solution.py:237
  66.5 0.3 collective-permute-start.11
  66.8 1.4 %collective-permute-start.12 = (bf16[96,640]{1,0:T(8,128)(2,1)S(1)}, bf16[96,640]{1,0:T(8,128)(2,1)S(1)}, u32[]{:S(2)}, u32[]{:S(2)}) collective-permute-start(bf16[96,640]{1,0:T(8,128)(2,1)S(1)} %get-tuple-element.34), channel_id=1, source_target_pairs={{0,3},{1,2},{2,1},{3,0},{4,7},{5,6},{6,5},{7,4},{8,11},{9,10},{10,... | collective-permute-start | bytes 368648 | tf_op jit(solution)/shard_map/ppermute | solution.py:237
  68.2 0.0 copy-done.2
  68.2 0.1 fusion
  68.3 0.0 collective-permute-done.10.s1
  68.3 3.1 %collective-permute-done.11.s2 = bf16[96,640]{1,0:T(8,128)(2,1)S(1)} collective-permute-done((bf16[96,640]{1,0:T(8,128)(2,1)S(1)}, bf16[96,640]{1,0:T(8,128)(2,1)S(1)}, u32[]{:S(2)}, u32[]{:S(2)}) %collective-permute-start.11) | collective-permute-done | bytes 122912 | tf_op jit(solution)/shard_map/ppermute | solution.py:237
  71.3 2.8 %collective-permute-done.12.s3 = bf16[96,640]{1,0:T(8,128)(2,1)S(1)} collective-permute-done((bf16[96,640]{1,0:T(8,128)(2,1)S(1)}, bf16[96,640]{1,0:T(8,128)(2,1)S(1)}, u32[]{:S(2)}, u32[]{:S(2)}) %collective-permute-start.12) | collective-permute-done | bytes 122912 | tf_op jit(solution)/shard_map/ppermute | solution.py:237
  74.2 0.8 shard_map.51
  74.9 0.3 collective-permute-start.13
  75.2 0.3 collective-permute-start.14
  75.5 1.6 %collective-permute-start.15 = (f32[2,128]{1,0:T(2,128)S(1)}, f32[2,128]{1,0:T(2,128)S(1)}, u32[]{:S(2)}, u32[]{:S(2)}) collective-permute-start(f32[2,128]{1,0:T(2,128)S(1)} %get-tuple-element.38), channel_id=1, source_target_pairs={{0,3},{1,2},{2,1},{3,0},{4,7},{5,6},{6,5},{7,4},{8,11},{9,10},{10,... | collective-permute-start | bytes 3080 | tf_op jit(solution)/shard_map/ppermute | solution.py:237
  77.1 0.0 collective-permute-done.13
  77.1 0.5 collective-permute-done.14
  77.6 1.1 %collective-permute-done.15 = f32[2,128]{1,0:T(2,128)S(1)} collective-permute-done((f32[2,128]{1,0:T(2,128)S(1)}, f32[2,128]{1,0:T(2,128)S(1)}, u32[]{:S(2)}, u32[]{:S(2)}) %collective-permute-start.15) | collective-permute-done | bytes 1056 | tf_op jit(solution)/shard_map/ppermute | solution.py:237
  78.7 3.9 %collective-permute-start.16 = (f32[128]{0:T(128)S(1)}, f32[128]{0:T(128)S(1)}, u32[]{:S(2)}, u32[]{:S(2)}) collective-permute-start(f32[128]{0:T(128)S(1)} %slice_bitcast_fusion), channel_id=1, source_target_pairs={{0,4},{1,253},{2,10},{3,251},{4,8},{5,1},{6,14},{7,255},{8,12},{9,... | collective-permute-start | bytes 1544 | tf_op jit(solution)/shard_map/ppermute | solution.py:293
  82.6 0.7 collective-permute-done.16
  83.3 7.0 %collective-permute-start.19 = (f32[128]{0:T(128)S(1)}, f32[128]{0:T(128)S(1)}, u32[]{:S(2)}, u32[]{:S(2)}) collective-permute-start(f32[128]{0:T(128)S(1)} %collective-permute-done.16), channel_id=1, source_target_pairs={{0,3},{1,2},{2,1},{3,0},{4,7},{5,6},{6,5},{7,4},{8,11},{9,10},{10,... | collective-permute-start | bytes 1544 | tf_op jit(solution)/shard_map/ppermute | solution.py:237
  90.3 0.0 collective-permute-start.18
  90.3 0.4 collective-permute-start.17
  90.7 0.8 collective-permute-done.19
  91.5 1.2 %collective-permute-done.18 = f32[128]{0:T(128)S(1)} collective-permute-done((f32[128]{0:T(128)S(1)}, f32[128]{0:T(128)S(1)}, u32[]{:S(2)}, u32[]{:S(2)}) %collective-permute-start.18) | collective-permute-done | bytes 544 | tf_op jit(solution)/shard_map/ppermute | solution.py:237
  92.7 0.0 collective-permute-done.17
  92.7 0.5 fusion.1
  (3 shorter events, 0.0 us)
Async XLA Ops:
  0.0 1.2 %copy-start = (bf16[3840,128]{1,0:T(8,128)(2,1)S(1)}, bf16[3840,128]{1,0:T(8,128)(2,1)}, u32[]{:S(2)}) copy-start(bf16[3840,128]{1,0:T(8,128)(2,1)} %own.3) | copy-start | bytes 2949124
  1.2 49.6 %copy-start.1 = (bf16[3840,128]{1,0:T(8,128)(2,1)S(1)}, bf16[3840,128]{1,0:T(8,128)(2,1)}, u32[]{:S(2)}) copy-start(bf16[3840,128]{1,0:T(8,128)(2,1)} %own.3) | copy-start | bytes 2949124
  2.2 22.5 %collective-permute-start.1 = (bf16[1920,128]{1,0:T(8,128)(2,1)}, bf16[1920,128]{1,0:T(8,128)(2,1)S(1)}, u32[]{:S(2)}, u32[]{:S(2)}) collective-permute-start(bf16[1920,128]{1,0:T(8,128)(2,1)} %get-tuple-element.22), channel_id=1, source_target_pairs={{0,4},{4,8},{8,12},{12,16},{16,20},{20,24},{24,28},{28,32},{32,36}... | collective-permute-start | bytes 1474568 | tf_op jit(solution)/shard_map/ppermute | solution.py:25
  4.7 20.0 %collective-permute-start = (bf16[1920,128]{1,0:T(8,128)(2,1)}, bf16[1920,128]{1,0:T(8,128)(2,1)S(1)}, u32[]{:S(2)}, u32[]{:S(2)}) collective-permute-start(bf16[1920,128]{1,0:T(8,128)(2,1)} %get-tuple-element.22), channel_id=1, source_target_pairs={{0,252},{4,0},{8,4},{12,8},{16,12},{20,16},{24,20},{28,24},{32,28}... | collective-permute-start | bytes 1474568 | tf_op jit(solution)/shard_map/ppermute | solution.py:25
  13.6 21.7 %collective-permute-start.8 = (bf16[1920,128]{1,0:T(8,128)(2,1)}, bf16[1920,128]{1,0:T(8,128)(2,1)S(1)}, u32[]{:S(2)}, u32[]{:S(2)}) collective-permute-start(bf16[1920,128]{1,0:T(8,128)(2,1)} %get-tuple-element.28), channel_id=1, source_target_pairs={{0,4},{4,8},{8,12},{12,16},{16,20},{20,24},{24,28},{28,32},{32,36}... | collective-permute-start | bytes 1474568 | tf_op jit(solution)/shard_map/ppermute | solution.py:25
  13.6 21.7 %collective-permute-start.6 = (bf16[1920,128]{1,0:T(8,128)(2,1)}, bf16[1920,128]{1,0:T(8,128)(2,1)S(1)}, u32[]{:S(2)}, u32[]{:S(2)}) collective-permute-start(bf16[1920,128]{1,0:T(8,128)(2,1)} %get-tuple-element.28), channel_id=1, source_target_pairs={{0,252},{4,0},{8,4},{12,8},{16,12},{20,16},{24,20},{28,24},{32,28}... | collective-permute-start | bytes 1474568 | tf_op jit(solution)/shard_map/ppermute | solution.py:25
  22.1 0.7 copy-start.3
  24.7 20.0 %collective-permute-start.2 = (bf16[1920,128]{1,0:T(8,128)(2,1)S(1)}, bf16[1920,128]{1,0:T(8,128)(2,1)S(1)}, u32[]{:S(2)}, u32[]{:S(2)}) collective-permute-start(bf16[1920,128]{1,0:T(8,128)(2,1)S(1)} %collective-permute-done.p1.a1), channel_id=1, source_target_pairs={{0,252},{4,0},{8,4},{12,8},{16,12},{20,16},{24,20},{28,24},{32,28}... | collective-permute-start | bytes 1474568 | tf_op jit(solution)/shard_map/ppermute | solution.py:25
  31.6 19.2 %collective-permute-start.5 = (bf16[1920,128]{1,0:T(8,128)(2,1)S(1)}, bf16[1920,128]{1,0:T(8,128)(2,1)S(1)}, u32[]{:S(2)}, u32[]{:S(2)}) collective-permute-start(bf16[1920,128]{1,0:T(8,128)(2,1)S(1)} %collective-permute-done.1.p2.a2), channel_id=1, source_target_pairs={{0,4},{4,8},{8,12},{12,16},{16,20},{20,24},{24,28},{28,32},{32,36}... | collective-permute-start | bytes 1474568 | tf_op jit(solution)/shard_map/ppermute | solution.py:25
  35.2 22.4 %collective-permute-start.9 = (bf16[1920,128]{1,0:T(8,128)(2,1)S(1)}, bf16[1920,128]{1,0:T(8,128)(2,1)S(1)}, u32[]{:S(2)}, u32[]{:S(2)}) collective-permute-start(bf16[1920,128]{1,0:T(8,128)(2,1)S(1)} %collective-permute-done.8.b2), channel_id=1, source_target_pairs={{0,4},{4,8},{8,12},{12,16},{16,20},{20,24},{24,28},{28,32},{32,36}... | collective-permute-start | bytes 1474568 | tf_op jit(solution)/shard_map/ppermute | solution.py:25
  35.3 22.4 %collective-permute-start.7 = (bf16[1920,128]{1,0:T(8,128)(2,1)S(1)}, bf16[1920,128]{1,0:T(8,128)(2,1)S(1)}, u32[]{:S(2)}, u32[]{:S(2)}) collective-permute-start(bf16[1920,128]{1,0:T(8,128)(2,1)S(1)} %collective-permute-done.6.b1), channel_id=1, source_target_pairs={{0,252},{4,0},{8,4},{12,8},{16,12},{20,16},{24,20},{28,24},{32,28}... | collective-permute-start | bytes 1474568 | tf_op jit(solution)/shard_map/ppermute | solution.py:25
  44.7 6.1 %collective-permute-start.4 = (bf16[192,128]{1,0:T(8,128)(2,1)S(1)}, bf16[192,128]{1,0:T(8,128)(2,1)S(1)}, u32[]{:S(2)}, u32[]{:S(2)}) collective-permute-start(bf16[192,128]{1,0:T(8,128)(2,1)S(1)} %get-tuple-element.39), channel_id=1, source_target_pairs={{0,3},{1,0},{2,1},{3,2},{4,7},{5,4},{6,5},{7,6},{8,11},{9,8},{10,9... | collective-permute-start | bytes 147464 | tf_op jit(solution)/shard_map/ppermute | solution.py:25
  47.4 3.4 %collective-permute-start.3 = (bf16[192,128]{1,0:T(8,128)(2,1)S(1)}, bf16[192,128]{1,0:T(8,128)(2,1)S(1)}, u32[]{:S(2)}, u32[]{:S(2)}) collective-permute-start(bf16[192,128]{1,0:T(8,128)(2,1)S(1)} %get-tuple-element.40), channel_id=1, source_target_pairs={{0,1},{1,2},{2,3},{3,0},{4,5},{5,6},{6,7},{7,4},{8,9},{9,10},{10,1... | collective-permute-start | bytes 147464 | tf_op jit(solution)/shard_map/ppermute | solution.py:25
  52.8 15.4 %copy-start.2 = (f32[8192]{0:T(1024)S(1)}, f32[8192]{0:T(1024)}, u32[]{:S(2)}) copy-start(f32[8192]{0:T(1024)} %param.7) | copy-start | bytes 98308
  62.4 5.9 %collective-permute-start.10 = (bf16[96,640]{1,0:T(8,128)(2,1)S(1)}, bf16[96,640]{1,0:T(8,128)(2,1)S(1)}, u32[]{:S(2)}, u32[]{:S(2)}) collective-permute-start(bf16[96,640]{1,0:T(8,128)(2,1)S(1)} %get-tuple-element.32), channel_id=1, source_target_pairs={{0,1},{1,0},{2,3},{3,2},{4,5},{5,4},{6,7},{7,6},{8,9},{9,8},{10,11... | collective-permute-start | bytes 368648 | tf_op jit(solution)/shard_map/ppermute | solution.py:237
  66.5 4.9 %collective-permute-start.11 = (bf16[96,640]{1,0:T(8,128)(2,1)S(1)}, bf16[96,640]{1,0:T(8,128)(2,1)S(1)}, u32[]{:S(2)}, u32[]{:S(2)}) collective-permute-start(bf16[96,640]{1,0:T(8,128)(2,1)S(1)} %get-tuple-element.33), channel_id=1, source_target_pairs={{0,2},{1,3},{2,0},{3,1},{4,6},{5,7},{6,4},{7,5},{8,10},{9,11},{10,... | collective-permute-start | bytes 368648 | tf_op jit(solution)/shard_map/ppermute | solution.py:237
  66.8 7.4 %collective-permute-start.12 = (bf16[96,640]{1,0:T(8,128)(2,1)S(1)}, bf16[96,640]{1,0:T(8,128)(2,1)S(1)}, u32[]{:S(2)}, u32[]{:S(2)}) collective-permute-start(bf16[96,640]{1,0:T(8,128)(2,1)S(1)} %get-tuple-element.34), channel_id=1, source_target_pairs={{0,3},{1,2},{2,1},{3,0},{4,7},{5,6},{6,5},{7,4},{8,11},{9,10},{10,... | collective-permute-start | bytes 368648 | tf_op jit(solution)/shard_map/ppermute | solution.py:237
  74.9 2.2 %collective-permute-start.13 = (f32[2,128]{1,0:T(2,128)S(1)}, f32[2,128]{1,0:T(2,128)S(1)}, u32[]{:S(2)}, u32[]{:S(2)}) collective-permute-start(f32[2,128]{1,0:T(2,128)S(1)} %get-tuple-element.36), channel_id=1, source_target_pairs={{0,1},{1,0},{2,3},{3,2},{4,5},{5,4},{6,7},{7,6},{8,9},{9,8},{10,11... | collective-permute-start | bytes 3080 | tf_op jit(solution)/shard_map/ppermute | solution.py:237
  75.2 2.4 %collective-permute-start.14 = (f32[2,128]{1,0:T(2,128)S(1)}, f32[2,128]{1,0:T(2,128)S(1)}, u32[]{:S(2)}, u32[]{:S(2)}) collective-permute-start(f32[2,128]{1,0:T(2,128)S(1)} %get-tuple-element.37), channel_id=1, source_target_pairs={{0,2},{1,3},{2,0},{3,1},{4,6},{5,7},{6,4},{7,5},{8,10},{9,11},{10,... | collective-permute-start | bytes 3080 | tf_op jit(solution)/shard_map/ppermute | solution.py:237
  75.5 3.2 %collective-permute-start.15 = (f32[2,128]{1,0:T(2,128)S(1)}, f32[2,128]{1,0:T(2,128)S(1)}, u32[]{:S(2)}, u32[]{:S(2)}) collective-permute-start(f32[2,128]{1,0:T(2,128)S(1)} %get-tuple-element.38), channel_id=1, source_target_pairs={{0,3},{1,2},{2,1},{3,0},{4,7},{5,6},{6,5},{7,4},{8,11},{9,10},{10,... | collective-permute-start | bytes 3080 | tf_op jit(solution)/shard_map/ppermute | solution.py:237
  78.7 4.6 %collective-permute-start.16 = (f32[128]{0:T(128)S(1)}, f32[128]{0:T(128)S(1)}, u32[]{:S(2)}, u32[]{:S(2)}) collective-permute-start(f32[128]{0:T(128)S(1)} %slice_bitcast_fusion), channel_id=1, source_target_pairs={{0,4},{1,253},{2,10},{3,251},{4,8},{5,1},{6,14},{7,255},{8,12},{9,... | collective-permute-start | bytes 1544 | tf_op jit(solution)/shard_map/ppermute | solution.py:293
  83.3 8.2 %collective-permute-start.19 = (f32[128]{0:T(128)S(1)}, f32[128]{0:T(128)S(1)}, u32[]{:S(2)}, u32[]{:S(2)}) collective-permute-start(f32[128]{0:T(128)S(1)} %collective-permute-done.16), channel_id=1, source_target_pairs={{0,3},{1,2},{2,1},{3,0},{4,7},{5,6},{6,5},{7,4},{8,11},{9,10},{10,... | collective-permute-start | bytes 1544 | tf_op jit(solution)/shard_map/ppermute | solution.py:237
  90.3 2.4 %collective-permute-start.18 = (f32[128]{0:T(128)S(1)}, f32[128]{0:T(128)S(1)}, u32[]{:S(2)}, u32[]{:S(2)}) collective-permute-start(f32[128]{0:T(128)S(1)} %collective-permute-done.16), channel_id=1, source_target_pairs={{0,2},{1,3},{2,0},{3,1},{4,6},{5,7},{6,4},{7,5},{8,10},{9,11},{10,... | collective-permute-start | bytes 1544 | tf_op jit(solution)/shard_map/ppermute | solution.py:237
  90.3 2.4 %collective-permute-start.17 = (f32[128]{0:T(128)S(1)}, f32[128]{0:T(128)S(1)}, u32[]{:S(2)}, u32[]{:S(2)}) collective-permute-start(f32[128]{0:T(128)S(1)} %collective-permute-done.16), channel_id=1, source_target_pairs={{0,1},{1,0},{2,3},{3,2},{4,5},{5,4},{6,7},{7,6},{8,9},{9,8},{10,11... | collective-permute-start | bytes 1544 | tf_op jit(solution)/shard_map/ppermute | solution.py:237

commit v7 on v6

--- a/solution.py
+++ b/solution.py
@@ -122,12 +122,17 @@
     )(*inputs)
 
 
-def star_step(planes_ref, start, operator_ref, partners, total_ref):
+def applied_block(planes_ref, start, operator_ref):
     window = [planes_ref[pl.ds(start + q, WIN, stride=3), :].astype(BF16) for q in range(3)]
     window = jnp.concatenate(window, axis=0).T
     applied = jnp.dot(window, operator_ref[...], preferred_element_type=F32).astype(BF16)
-    applied = jnp.concatenate([applied[:, a * ROWS : (a + 1) * ROWS] for a in range(3)], axis=0)
-    total_ref[...] += jnp.dot(applied, jnp.concatenate(partners, axis=1), preferred_element_type=F32)
+    return jnp.concatenate([applied[:, a * ROWS : (a + 1) * ROWS] for a in range(3)], axis=0)
+
+
+def add_products(steps, total_ref):
+    left = jnp.concatenate([applied for applied, _ in steps], axis=1)
+    right = jnp.concatenate([jnp.concatenate(near, axis=1) for _, near in steps], axis=0)
+    total_ref[...] += jnp.dot(left, right, preferred_element_type=F32)
 
 
 def first_kernel(t_ref, far_ref, below_ref, above_ref, p1, own, p2, p3, out_ref, planes):
@@ -138,11 +143,13 @@
     planes[tail + edge : tail + 2 * edge, :] = below_ref[...].astype(F32)
     planes[tail + 2 * edge :, :] = far_ref[tail:, :].astype(F32)
     blocks = own.shape[0] // ROWS
+    steps = []
     for at in range(ROWS, tail + ROWS, ROWS):
         block = (blocks - TAIL + at // ROWS) % blocks
         near = [r[at : at + ROWS, :] for r in (far_ref, p1, p2, p3)]
         near.insert(2, own[block * ROWS : (block + 1) * ROWS, :])
-        star_step(planes, at - edge if block else tail + edge, t_ref.at[block], near, out_ref)
+        steps.append((applied_block(planes, at - edge if block else tail + edge, t_ref.at[block]), near))
+    add_products(steps, out_ref)
 
 
 def second_kernel(
@@ -155,6 +162,7 @@
     planes[head + rows_b :, :] = far_a[0:tail, :].astype(F32)
     total[...] = before_ref[...]
     blocks = own.shape[0] // ROWS
+    steps = []
     for block in range(1, blocks - TAIL + 1):
         if block < HEAD or block >= blocks - TAIL:
             at = tail + block * ROWS if block < HEAD else (block - blocks + TAIL) * ROWS
@@ -163,7 +171,10 @@
             at = (block - HEAD) * ROWS
             near = [r[at : at + ROWS, :] for r in (far_b, b1, b2, b3)]
         near.insert(2, own[block * ROWS : (block + 1) * ROWS, :])
-        star_step(planes, block * ROWS - 3 * HALO, t_ref.at[block], near, total)
+        steps.append((applied_block(planes, block * ROWS - 3 * HALO, t_ref.at[block]), near))
+        if len(steps) == 2 or block == blocks - TAIL:
+            add_products(steps, total)
+            steps = []
     for k, out in enumerate((o0, o1, o2, o3)):
         share = jnp.bitwise_xor(place_ref[0], k)
         for a in range(3):

time: 93.4 us -> 93.1 us (level)
  no operation moved by 1% of the time
where the time goes in v7:
time: 93.1 us; the launch traced here: 92.9 us
  starting transfers between devices  55 us (59%)
  waiting for transfers between devices  21.9 us (24%)
  Pallas kernels  12 us (13%)
  local copies, waits for them, and re-layouts  3.19 us (3%)
    ppermute x10, starting transfers between devices, shifted(): lax.ppermute(x, axis, [(i, (i + distance) % count) for i in range(count)])  35.7 us
    ppermute x9, starting transfers between devices, swapped(): return lax.ppermute(x, 'atom', [(i, i ^ k) for i in range(4)])  15.4 us
    ppermute x10, waiting for transfers between devices, shifted(): lax.ppermute(x, axis, [(i, (i + distance) % count) for i in range(count)])  11.7 us
    ppermute x9, waiting for transfers between devices, swapped(): return lax.ppermute(x, 'atom', [(i, i ^ k) for i in range(4)])  9.41 us
    pallas_call x1, Pallas kernels, star_products(): pl.pallas_call(second_kernel, in_specs=[pl.BlockSpec(memory_space=pltpu.S...  4.43 us
    ppermute x1, starting transfers between devices, local(): result = lax.ppermute(carried[0], ('mode', 'atom'), route)  3.85 us
    unnamed x9, local copies, waits for them, and re-layouts  3.18 us
    pallas_call x1, Pallas kernels, filled_operator(): pl.pallas_call(fill_kernel, in_specs=[vmem], out_specs=vmem, out_shape=ja...  2.92 us
  transfers between devices with their start and end apart: 20, of which 11 were waited for; matrix products, arithmetic and copies ran while one was open for 2% of the time, Pallas kernels for 6%

profile of v7, /device:TPU:1, one launch (start us, length us, event | category | flops | bytes accessed | tf_op | source)
XLA Modules:
  0.0 92.9 jit_solution(14989982462357174012)
XLA Ops:
  0.0 0.0 copy-start
  0.0 1.2 %copy-done = bf16[3840,128]{1,0:T(8,128)(2,1)S(1)} copy-done((bf16[3840,128]{1,0:T(8,128)(2,1)S(1)}, bf16[3840,128]{1,0:T(8,128)(2,1)}, u32[]{:S(2)}) %copy-start) | copy-done | bytes 983064
  1.2 0.0 copy-start.1
  1.2 1.0 %shard_map.46 = (bf16[1920,128]{1,0:T(8,128)(2,1)}, bf16[1920,128]{1,0:T(8,128)(2,1)}) custom-call(bf16[3840,128]{1,0:T(8,128)(2,1)S(1)} %copy-done), custom_call_target="tpu_custom_call" | custom-call | tf_op jit(solution)/shard_map/pallas_call | solution.py:118
  2.2 2.5 %collective-permute-start.1 = (bf16[1920,128]{1,0:T(8,128)(2,1)}, bf16[1920,128]{1,0:T(8,128)(2,1)S(1)}, u32[]{:S(2)}, u32[]{:S(2)}) collective-permute-start(bf16[1920,128]{1,0:T(8,128)(2,1)} %get-tuple-element.22), channel_id=1, source_target_pairs={{0,4},{4,8},{8,12},{12,16},{16,20},{20,24},{24,28},{28,32},{32,36}... | collective-permute-start | bytes 1474568 | tf_op jit(solution)/shard_map/ppermute | solution.py:25
  4.7 8.9 %collective-permute-start = (bf16[1920,128]{1,0:T(8,128)(2,1)}, bf16[1920,128]{1,0:T(8,128)(2,1)S(1)}, u32[]{:S(2)}, u32[]{:S(2)}) collective-permute-start(bf16[1920,128]{1,0:T(8,128)(2,1)} %get-tuple-element.22), channel_id=1, source_target_pairs={{0,252},{4,0},{8,4},{12,8},{16,12},{20,16},{24,20},{28,24},{32,28}... | collective-permute-start | bytes 1474568 | tf_op jit(solution)/shard_map/ppermute | solution.py:25
  13.6 0.0 collective-permute-start.8
  13.6 7.2 %collective-permute-start.6 = (bf16[1920,128]{1,0:T(8,128)(2,1)}, bf16[1920,128]{1,0:T(8,128)(2,1)S(1)}, u32[]{:S(2)}, u32[]{:S(2)}) collective-permute-start(bf16[1920,128]{1,0:T(8,128)(2,1)} %get-tuple-element.28), channel_id=1, source_target_pairs={{0,252},{4,0},{8,4},{12,8},{16,12},{20,16},{24,20},{28,24},{32,28}... | collective-permute-start | bytes 1474568 | tf_op jit(solution)/shard_map/ppermute | solution.py:25
  20.8 1.2 %copy.5.couplings_ref = f32[4,3,3,3,1280]{4,3,2,1,0:T(4,128)S(1)} copy(f32[4,3,3,3,1280]{4,0,3,2,1:T(4,128)} %param.5) | data formatting | bytes 1105920 | tf_op args[1]
  22.0 0.1 pad_add_fusion.place_ref
  22.1 0.0 copy-start.3
  22.1 0.7 copy-done.3
  22.8 1.1 %shard_map.47.table_ref = f32[10,40,384]{2,1,0:T(8,128)S(1)} custom-call(s32[2]{0:T(128)S(1)} %pad_add_fusion.place_ref, f32[4,3,3,3,1280]{4,3,2,1,0:T(4,128)S(1)} %copy.5.couplings_ref, s32[4,1280]{1,0:T(4,128)S(1)} %copy-done.3), custom_call_target="tpu_custom_call" | custom-call | flops 2000000000 | bytes 3000000 | tf_op jit(solution)/shard_map/pallas_call | solution.py:58
  23.9 0.8 collective-permute-done.1.p2.a2
  24.7 0.0 collective-permute-done.p1.a1
  24.7 6.9 %collective-permute-start.2 = (bf16[1920,128]{1,0:T(8,128)(2,1)S(1)}, bf16[1920,128]{1,0:T(8,128)(2,1)S(1)}, u32[]{:S(2)}, u32[]{:S(2)}) collective-permute-start(bf16[1920,128]{1,0:T(8,128)(2,1)S(1)} %collective-permute-done.p1.a1), channel_id=1, source_target_pairs={{0,252},{4,0},{8,4},{12,8},{16,12},{20,16},{24,20},{28,24},{32,28}... | collective-permute-start | bytes 1474568 | tf_op jit(solution)/shard_map/ppermute | solution.py:25
  31.6 0.0 collective-permute-start.5
  31.6 3.7 %collective-permute-done.8.b2 = bf16[1920,128]{1,0:T(8,128)(2,1)S(1)} collective-permute-done((bf16[1920,128]{1,0:T(8,128)(2,1)}, bf16[1920,128]{1,0:T(8,128)(2,1)S(1)}, u32[]{:S(2)}, u32[]{:S(2)}) %collective-permute-start.8) | collective-permute-done | bytes 491552 | tf_op jit(solution)/shard_map/ppermute | solution.py:25
  35.2 0.0 collective-permute-start.9
  35.3 0.0 collective-permute-done.6.b1
  35.3 7.2 %collective-permute-start.7 = (bf16[1920,128]{1,0:T(8,128)(2,1)S(1)}, bf16[1920,128]{1,0:T(8,128)(2,1)S(1)}, u32[]{:S(2)}, u32[]{:S(2)}) collective-permute-start(bf16[1920,128]{1,0:T(8,128)(2,1)S(1)} %collective-permute-done.6.b1), channel_id=1, source_target_pairs={{0,252},{4,0},{8,4},{12,8},{16,12},{20,16},{24,20},{28,24},{32,28}... | collective-permute-start | bytes 1474568 | tf_op jit(solution)/shard_map/ppermute | solution.py:25
  42.4 2.3 %collective-permute-done.2.far_ref.far_a = bf16[1920,128]{1,0:T(8,128)(2,1)S(1)} collective-permute-done((bf16[1920,128]{1,0:T(8,128)(2,1)S(1)}, bf16[1920,128]{1,0:T(8,128)(2,1)S(1)}, u32[]{:S(2)}, u32[]{:S(2)}) %collective-permute-start.2) | collective-permute-done | bytes 491552 | tf_op jit(solution)/shard_map/ppermute | solution.py:25
  44.7 2.7 %collective-permute-start.4 = (bf16[192,128]{1,0:T(8,128)(2,1)S(1)}, bf16[192,128]{1,0:T(8,128)(2,1)S(1)}, u32[]{:S(2)}, u32[]{:S(2)}) collective-permute-start(bf16[192,128]{1,0:T(8,128)(2,1)S(1)} %get-tuple-element.39), channel_id=1, source_target_pairs={{0,3},{1,0},{2,1},{3,2},{4,7},{5,4},{6,5},{7,6},{8,11},{9,8},{10,9... | collective-permute-start | bytes 147464 | tf_op jit(solution)/shard_map/ppermute | solution.py:25
  47.4 0.5 collective-permute-start.3
  47.9 2.9 %shard_map.48.t_ref = bf16[10,768,1152]{2,1,0:T(8,128)(2,1)S(1)} custom-call(f32[10,40,384]{2,1,0:T(8,128)S(1)} %shard_map.47.table_ref), custom_call_target="tpu_custom_call" | custom-call | flops 4000000000 | bytes 1000000 | tf_op jit(solution)/shard_map/pallas_call | solution.py:100
  50.8 0.0 collective-permute-done.5.p3.a3
  50.8 0.0 collective-permute-done.4.above_ref
  50.8 0.0 collective-permute-done.3.below_ref
  50.8 0.0 copy-done.1
  50.9 1.8 %shard_map.49.before_ref = f32[384,640]{1,0:T(8,128)S(1)} custom-call(bf16[10,768,1152]{2,1,0:T(8,128)(2,1)S(1)} %shard_map.48.t_ref, bf16[1920,128]{1,0:T(8,128)(2,1)S(1)} %collective-permute-done.2.far_ref.far_a, bf16[192,128]{1,0:T(8,128)(2,1)S(1)} %collective-permute-done.3.below_ref, bf16[192,128]{1,0:T(8,128)(2,1)S(1)} %collective-permute-done.4.above_ref, ...), custom_call_target="tpu_custom_call" | custom-call | flops 3000000000 | bytes 9000000 | tf_op jit(solution)/shard_map/pallas_call | solution.py:191
  52.6 0.0 copy-start.2
  52.6 5.0 %collective-permute-done.9.b3 = bf16[1920,128]{1,0:T(8,128)(2,1)S(1)} collective-permute-done((bf16[1920,128]{1,0:T(8,128)(2,1)S(1)}, bf16[1920,128]{1,0:T(8,128)(2,1)S(1)}, u32[]{:S(2)}, u32[]{:S(2)}) %collective-permute-start.9) | collective-permute-done | bytes 491552 | tf_op jit(solution)/shard_map/ppermute | solution.py:25
  57.6 0.0 collective-permute-done.7.far_b
  57.6 4.4 %shard_map.50 = (bf16[96,640]{1,0:T(8,128)(2,1)S(1)}, bf16[96,640]{1,0:T(8,128)(2,1)S(1)}, bf16[96,640]{1,0:T(8,128)(2,1)S(1)}, bf16[96,640]{1,0:T(8,128)(2,1)S(1)}) custom-call(s32[2]{0:T(128)S(1)} %pad_add_fusion.place_ref, bf16[10,768,1152]{2,1,0:T(8,128)(2,1)S(1)} %shard_map.48.t_ref, f32[384,640]{1,0:T(8,128)S(1)} %shard_map.49.before_ref, ...), custom_call_target="tpu_custom_call" | custom-call | flops 7000000000 | bytes 21000000 | tf_op jit(solution)/shard_map/pallas_call | solution.py:202
  62.1 4.0 %collective-permute-start.10 = (bf16[96,640]{1,0:T(8,128)(2,1)S(1)}, bf16[96,640]{1,0:T(8,128)(2,1)S(1)}, u32[]{:S(2)}, u32[]{:S(2)}) collective-permute-start(bf16[96,640]{1,0:T(8,128)(2,1)S(1)} %get-tuple-element.32), channel_id=1, source_target_pairs={{0,1},{1,0},{2,3},{3,2},{4,5},{5,4},{6,7},{7,6},{8,9},{9,8},{10,11... | collective-permute-start | bytes 368648 | tf_op jit(solution)/shard_map/ppermute | solution.py:248
  66.1 0.3 collective-permute-start.11
  66.5 1.4 %collective-permute-start.12 = (bf16[96,640]{1,0:T(8,128)(2,1)S(1)}, bf16[96,640]{1,0:T(8,128)(2,1)S(1)}, u32[]{:S(2)}, u32[]{:S(2)}) collective-permute-start(bf16[96,640]{1,0:T(8,128)(2,1)S(1)} %get-tuple-element.34), channel_id=1, source_target_pairs={{0,3},{1,2},{2,1},{3,0},{4,7},{5,6},{6,5},{7,4},{8,11},{9,10},{10,... | collective-permute-start | bytes 368648 | tf_op jit(solution)/shard_map/ppermute | solution.py:248
  67.8 0.0 copy-done.2
  67.8 0.1 fusion
  67.9 0.0 collective-permute-done.10.s1
  67.9 3.1 %collective-permute-done.11.s2 = bf16[96,640]{1,0:T(8,128)(2,1)S(1)} collective-permute-done((bf16[96,640]{1,0:T(8,128)(2,1)S(1)}, bf16[96,640]{1,0:T(8,128)(2,1)S(1)}, u32[]{:S(2)}, u32[]{:S(2)}) %collective-permute-start.11) | collective-permute-done | bytes 122912 | tf_op jit(solution)/shard_map/ppermute | solution.py:248
  71.0 2.8 %collective-permute-done.12.s3 = bf16[96,640]{1,0:T(8,128)(2,1)S(1)} collective-permute-done((bf16[96,640]{1,0:T(8,128)(2,1)S(1)}, bf16[96,640]{1,0:T(8,128)(2,1)S(1)}, u32[]{:S(2)}, u32[]{:S(2)}) %collective-permute-start.12) | collective-permute-done | bytes 122912 | tf_op jit(solution)/shard_map/ppermute | solution.py:248
  73.8 0.8 shard_map.51
  74.6 0.3 collective-permute-start.13
  74.9 0.3 collective-permute-start.14
  75.2 1.6 %collective-permute-start.15 = (f32[2,128]{1,0:T(2,128)S(1)}, f32[2,128]{1,0:T(2,128)S(1)}, u32[]{:S(2)}, u32[]{:S(2)}) collective-permute-start(f32[2,128]{1,0:T(2,128)S(1)} %get-tuple-element.38), channel_id=1, source_target_pairs={{0,3},{1,2},{2,1},{3,0},{4,7},{5,6},{6,5},{7,4},{8,11},{9,10},{10,... | collective-permute-start | bytes 3080 | tf_op jit(solution)/shard_map/ppermute | solution.py:248
  76.8 0.0 collective-permute-done.13
  76.8 0.5 collective-permute-done.14
  77.3 1.1 %collective-permute-done.15 = f32[2,128]{1,0:T(2,128)S(1)} collective-permute-done((f32[2,128]{1,0:T(2,128)S(1)}, f32[2,128]{1,0:T(2,128)S(1)}, u32[]{:S(2)}, u32[]{:S(2)}) %collective-permute-start.15) | collective-permute-done | bytes 1056 | tf_op jit(solution)/shard_map/ppermute | solution.py:248
  78.4 3.9 %collective-permute-start.16 = (f32[128]{0:T(128)S(1)}, f32[128]{0:T(128)S(1)}, u32[]{:S(2)}, u32[]{:S(2)}) collective-permute-start(f32[128]{0:T(128)S(1)} %slice_bitcast_fusion), channel_id=1, source_target_pairs={{0,4},{1,253},{2,10},{3,251},{4,8},{5,1},{6,14},{7,255},{8,12},{9,... | collective-permute-start | bytes 1544 | tf_op jit(solution)/shard_map/ppermute | solution.py:304
  82.2 0.7 collective-permute-done.16
  82.9 7.0 %collective-permute-start.19 = (f32[128]{0:T(128)S(1)}, f32[128]{0:T(128)S(1)}, u32[]{:S(2)}, u32[]{:S(2)}) collective-permute-start(f32[128]{0:T(128)S(1)} %collective-permute-done.16), channel_id=1, source_target_pairs={{0,3},{1,2},{2,1},{3,0},{4,7},{5,6},{6,5},{7,4},{8,11},{9,10},{10,... | collective-permute-start | bytes 1544 | tf_op jit(solution)/shard_map/ppermute | solution.py:248
  90.0 0.0 collective-permute-start.18
  90.0 0.4 collective-permute-start.17
  90.4 0.8 collective-permute-done.19
  91.2 1.2 %collective-permute-done.18 = f32[128]{0:T(128)S(1)} collective-permute-done((f32[128]{0:T(128)S(1)}, f32[128]{0:T(128)S(1)}, u32[]{:S(2)}, u32[]{:S(2)}) %collective-permute-start.18) | collective-permute-done | bytes 544 | tf_op jit(solution)/shard_map/ppermute | solution.py:248
  92.3 0.0 collective-permute-done.17
  92.3 0.5 fusion.1
  (3 shorter events, 0.0 us)
Async XLA Ops:
  0.0 1.2 %copy-start = (bf16[3840,128]{1,0:T(8,128)(2,1)S(1)}, bf16[3840,128]{1,0:T(8,128)(2,1)}, u32[]{:S(2)}) copy-start(bf16[3840,128]{1,0:T(8,128)(2,1)} %own.3) | copy-start | bytes 2949124
  1.2 49.6 %copy-start.1 = (bf16[3840,128]{1,0:T(8,128)(2,1)S(1)}, bf16[3840,128]{1,0:T(8,128)(2,1)}, u32[]{:S(2)}) copy-start(bf16[3840,128]{1,0:T(8,128)(2,1)} %own.3) | copy-start | bytes 2949124
  2.2 22.5 %collective-permute-start.1 = (bf16[1920,128]{1,0:T(8,128)(2,1)}, bf16[1920,128]{1,0:T(8,128)(2,1)S(1)}, u32[]{:S(2)}, u32[]{:S(2)}) collective-permute-start(bf16[1920,128]{1,0:T(8,128)(2,1)} %get-tuple-element.22), channel_id=1, source_target_pairs={{0,4},{4,8},{8,12},{12,16},{16,20},{20,24},{24,28},{28,32},{32,36}... | collective-permute-start | bytes 1474568 | tf_op jit(solution)/shard_map/ppermute | solution.py:25
  4.7 20.0 %collective-permute-start = (bf16[1920,128]{1,0:T(8,128)(2,1)}, bf16[1920,128]{1,0:T(8,128)(2,1)S(1)}, u32[]{:S(2)}, u32[]{:S(2)}) collective-permute-start(bf16[1920,128]{1,0:T(8,128)(2,1)} %get-tuple-element.22), channel_id=1, source_target_pairs={{0,252},{4,0},{8,4},{12,8},{16,12},{20,16},{24,20},{28,24},{32,28}... | collective-permute-start | bytes 1474568 | tf_op jit(solution)/shard_map/ppermute | solution.py:25
  13.6 21.7 %collective-permute-start.8 = (bf16[1920,128]{1,0:T(8,128)(2,1)}, bf16[1920,128]{1,0:T(8,128)(2,1)S(1)}, u32[]{:S(2)}, u32[]{:S(2)}) collective-permute-start(bf16[1920,128]{1,0:T(8,128)(2,1)} %get-tuple-element.28), channel_id=1, source_target_pairs={{0,4},{4,8},{8,12},{12,16},{16,20},{20,24},{24,28},{28,32},{32,36}... | collective-permute-start | bytes 1474568 | tf_op jit(solution)/shard_map/ppermute | solution.py:25
  13.6 21.7 %collective-permute-start.6 = (bf16[1920,128]{1,0:T(8,128)(2,1)}, bf16[1920,128]{1,0:T(8,128)(2,1)S(1)}, u32[]{:S(2)}, u32[]{:S(2)}) collective-permute-start(bf16[1920,128]{1,0:T(8,128)(2,1)} %get-tuple-element.28), channel_id=1, source_target_pairs={{0,252},{4,0},{8,4},{12,8},{16,12},{20,16},{24,20},{28,24},{32,28}... | collective-permute-start | bytes 1474568 | tf_op jit(solution)/shard_map/ppermute | solution.py:25
  22.1 0.7 copy-start.3
  24.7 20.0 %collective-permute-start.2 = (bf16[1920,128]{1,0:T(8,128)(2,1)S(1)}, bf16[1920,128]{1,0:T(8,128)(2,1)S(1)}, u32[]{:S(2)}, u32[]{:S(2)}) collective-permute-start(bf16[1920,128]{1,0:T(8,128)(2,1)S(1)} %collective-permute-done.p1.a1), channel_id=1, source_target_pairs={{0,252},{4,0},{8,4},{12,8},{16,12},{20,16},{24,20},{28,24},{32,28}... | collective-permute-start | bytes 1474568 | tf_op jit(solution)/shard_map/ppermute | solution.py:25
  31.6 19.2 %collective-permute-start.5 = (bf16[1920,128]{1,0:T(8,128)(2,1)S(1)}, bf16[1920,128]{1,0:T(8,128)(2,1)S(1)}, u32[]{:S(2)}, u32[]{:S(2)}) collective-permute-start(bf16[1920,128]{1,0:T(8,128)(2,1)S(1)} %collective-permute-done.1.p2.a2), channel_id=1, source_target_pairs={{0,4},{4,8},{8,12},{12,16},{16,20},{20,24},{24,28},{28,32},{32,36}... | collective-permute-start | bytes 1474568 | tf_op jit(solution)/shard_map/ppermute | solution.py:25
  35.2 22.4 %collective-permute-start.9 = (bf16[1920,128]{1,0:T(8,128)(2,1)S(1)}, bf16[1920,128]{1,0:T(8,128)(2,1)S(1)}, u32[]{:S(2)}, u32[]{:S(2)}) collective-permute-start(bf16[1920,128]{1,0:T(8,128)(2,1)S(1)} %collective-permute-done.8.b2), channel_id=1, source_target_pairs={{0,4},{4,8},{8,12},{12,16},{16,20},{20,24},{24,28},{28,32},{32,36}... | collective-permute-start | bytes 1474568 | tf_op jit(solution)/shard_map/ppermute | solution.py:25
  35.3 22.4 %collective-permute-start.7 = (bf16[1920,128]{1,0:T(8,128)(2,1)S(1)}, bf16[1920,128]{1,0:T(8,128)(2,1)S(1)}, u32[]{:S(2)}, u32[]{:S(2)}) collective-permute-start(bf16[1920,128]{1,0:T(8,128)(2,1)S(1)} %collective-permute-done.6.b1), channel_id=1, source_target_pairs={{0,252},{4,0},{8,4},{12,8},{16,12},{20,16},{24,20},{28,24},{32,28}... | collective-permute-start | bytes 1474568 | tf_op jit(solution)/shard_map/ppermute | solution.py:25
  44.7 6.1 %collective-permute-start.4 = (bf16[192,128]{1,0:T(8,128)(2,1)S(1)}, bf16[192,128]{1,0:T(8,128)(2,1)S(1)}, u32[]{:S(2)}, u32[]{:S(2)}) collective-permute-start(bf16[192,128]{1,0:T(8,128)(2,1)S(1)} %get-tuple-element.39), channel_id=1, source_target_pairs={{0,3},{1,0},{2,1},{3,2},{4,7},{5,4},{6,5},{7,6},{8,11},{9,8},{10,9... | collective-permute-start | bytes 147464 | tf_op jit(solution)/shard_map/ppermute | solution.py:25
  47.4 3.4 %collective-permute-start.3 = (bf16[192,128]{1,0:T(8,128)(2,1)S(1)}, bf16[192,128]{1,0:T(8,128)(2,1)S(1)}, u32[]{:S(2)}, u32[]{:S(2)}) collective-permute-start(bf16[192,128]{1,0:T(8,128)(2,1)S(1)} %get-tuple-element.40), channel_id=1, source_target_pairs={{0,1},{1,2},{2,3},{3,0},{4,5},{5,6},{6,7},{7,4},{8,9},{9,10},{10,1... | collective-permute-start | bytes 147464 | tf_op jit(solution)/shard_map/ppermute | solution.py:25
  52.6 15.2 %copy-start.2 = (f32[8192]{0:T(1024)S(1)}, f32[8192]{0:T(1024)}, u32[]{:S(2)}) copy-start(f32[8192]{0:T(1024)} %param.7) | copy-start | bytes 98308
  62.1 5.9 %collective-permute-start.10 = (bf16[96,640]{1,0:T(8,128)(2,1)S(1)}, bf16[96,640]{1,0:T(8,128)(2,1)S(1)}, u32[]{:S(2)}, u32[]{:S(2)}) collective-permute-start(bf16[96,640]{1,0:T(8,128)(2,1)S(1)} %get-tuple-element.32), channel_id=1, source_target_pairs={{0,1},{1,0},{2,3},{3,2},{4,5},{5,4},{6,7},{7,6},{8,9},{9,8},{10,11... | collective-permute-start | bytes 368648 | tf_op jit(solution)/shard_map/ppermute | solution.py:248
  66.1 4.9 %collective-permute-start.11 = (bf16[96,640]{1,0:T(8,128)(2,1)S(1)}, bf16[96,640]{1,0:T(8,128)(2,1)S(1)}, u32[]{:S(2)}, u32[]{:S(2)}) collective-permute-start(bf16[96,640]{1,0:T(8,128)(2,1)S(1)} %get-tuple-element.33), channel_id=1, source_target_pairs={{0,2},{1,3},{2,0},{3,1},{4,6},{5,7},{6,4},{7,5},{8,10},{9,11},{10,... | collective-permute-start | bytes 368648 | tf_op jit(solution)/shard_map/ppermute | solution.py:248
  66.5 7.4 %collective-permute-start.12 = (bf16[96,640]{1,0:T(8,128)(2,1)S(1)}, bf16[96,640]{1,0:T(8,128)(2,1)S(1)}, u32[]{:S(2)}, u32[]{:S(2)}) collective-permute-start(bf16[96,640]{1,0:T(8,128)(2,1)S(1)} %get-tuple-element.34), channel_id=1, source_target_pairs={{0,3},{1,2},{2,1},{3,0},{4,7},{5,6},{6,5},{7,4},{8,11},{9,10},{10,... | collective-permute-start | bytes 368648 | tf_op jit(solution)/shard_map/ppermute | solution.py:248
  74.6 2.2 %collective-permute-start.13 = (f32[2,128]{1,0:T(2,128)S(1)}, f32[2,128]{1,0:T(2,128)S(1)}, u32[]{:S(2)}, u32[]{:S(2)}) collective-permute-start(f32[2,128]{1,0:T(2,128)S(1)} %get-tuple-element.36), channel_id=1, source_target_pairs={{0,1},{1,0},{2,3},{3,2},{4,5},{5,4},{6,7},{7,6},{8,9},{9,8},{10,11... | collective-permute-start | bytes 3080 | tf_op jit(solution)/shard_map/ppermute | solution.py:248
  74.9 2.4 %collective-permute-start.14 = (f32[2,128]{1,0:T(2,128)S(1)}, f32[2,128]{1,0:T(2,128)S(1)}, u32[]{:S(2)}, u32[]{:S(2)}) collective-permute-start(f32[2,128]{1,0:T(2,128)S(1)} %get-tuple-element.37), channel_id=1, source_target_pairs={{0,2},{1,3},{2,0},{3,1},{4,6},{5,7},{6,4},{7,5},{8,10},{9,11},{10,... | collective-permute-start | bytes 3080 | tf_op jit(solution)/shard_map/ppermute | solution.py:248
  75.2 3.2 %collective-permute-start.15 = (f32[2,128]{1,0:T(2,128)S(1)}, f32[2,128]{1,0:T(2,128)S(1)}, u32[]{:S(2)}, u32[]{:S(2)}) collective-permute-start(f32[2,128]{1,0:T(2,128)S(1)} %get-tuple-element.38), channel_id=1, source_target_pairs={{0,3},{1,2},{2,1},{3,0},{4,7},{5,6},{6,5},{7,4},{8,11},{9,10},{10,... | collective-permute-start | bytes 3080 | tf_op jit(solution)/shard_map/ppermute | solution.py:248
  78.4 4.6 %collective-permute-start.16 = (f32[128]{0:T(128)S(1)}, f32[128]{0:T(128)S(1)}, u32[]{:S(2)}, u32[]{:S(2)}) collective-permute-start(f32[128]{0:T(128)S(1)} %slice_bitcast_fusion), channel_id=1, source_target_pairs={{0,4},{1,253},{2,10},{3,251},{4,8},{5,1},{6,14},{7,255},{8,12},{9,... | collective-permute-start | bytes 1544 | tf_op jit(solution)/shard_map/ppermute | solution.py:304
  82.9 8.2 %collective-permute-start.19 = (f32[128]{0:T(128)S(1)}, f32[128]{0:T(128)S(1)}, u32[]{:S(2)}, u32[]{:S(2)}) collective-permute-start(f32[128]{0:T(128)S(1)} %collective-permute-done.16), channel_id=1, source_target_pairs={{0,3},{1,2},{2,1},{3,0},{4,7},{5,6},{6,5},{7,4},{8,11},{9,10},{10,... | collective-permute-start | bytes 1544 | tf_op jit(solution)/shard_map/ppermute | solution.py:248
  90.0 2.4 %collective-permute-start.18 = (f32[128]{0:T(128)S(1)}, f32[128]{0:T(128)S(1)}, u32[]{:S(2)}, u32[]{:S(2)}) collective-permute-start(f32[128]{0:T(128)S(1)} %collective-permute-done.16), channel_id=1, source_target_pairs={{0,2},{1,3},{2,0},{3,1},{4,6},{5,7},{6,4},{7,5},{8,10},{9,11},{10,... | collective-permute-start | bytes 1544 | tf_op jit(solution)/shard_map/ppermute | solution.py:248
  90.0 2.4 %collective-permute-start.17 = (f32[128]{0:T(128)S(1)}, f32[128]{0:T(128)S(1)}, u32[]{:S(2)}, u32[]{:S(2)}) collective-permute-start(f32[128]{0:T(128)S(1)} %collective-permute-done.16), channel_id=1, source_target_pairs={{0,1},{1,0},{2,3},{3,2},{4,5},{5,4},{6,7},{7,6},{8,9},{9,8},{10,11... | collective-permute-start | bytes 1544 | tf_op jit(solution)/shard_map/ppermute | solution.py:248
